TPU v7x, 128 devices: a whole 4x4x4 slice. The times are simulated.
128 devices in a mesh: dom: 32 (over y, x, core), grp: 4 (over z).
Axes of the slice: x: 4, y: 4, z: 4, core: 2. Of those that a mesh axis runs over, the one named last changes fastest.
Arguments:
- encoded: float32 [65536, 1024], P(('dom', 'grp')), may hold values from -6 to 6
- owner_of: int32 [65536], P(('dom', 'grp')), may hold values from 0 to 65535, as said below
- nbr_blocks: int32 [512, 16], P(('dom', 'grp')), may hold values from 0 to 15, as said below
- nbr_count: int32 [512], P(('dom', 'grp')), may hold values from 1 to 16, as said below
- edge_weights: bfloat16 [512, 16, 128, 128], P(('dom', 'grp')), may hold values from 0.01 to 16
Outputs:
- propagated: bfloat16 [65536, 1024], P(('dom', 'grp'))
Inputs may be any that keep to these rules, and one draw needn't show every extreme that they name: owner_of is a permutation; the batch rows of each device go to the nodes of every device in equal numbers (512 / the device count to each), where device d owns nodes d * 512 to (d + 1) * 512 - 1. `nbr_blocks`: A partition group is the 2048 nodes of the devices that share a dom index; block g of a group is its nodes g * 128 to (g + 1) * 128 - 1. The first nbr_count[b] entries of row block b are distinct; later entries are padding and are ignored. `nbr_count`: some row block has exactly 16 live blocks.
All inputs are finite; a program needn't handle non-finite values.
Results may differ from a plain program's by a relative error of at most 0.005.
Values may be sent and summed in bfloat16 or wider, within the bound.
No kernel may reach another device: no remote copies, remote signals or barrier semaphores. Data moves between devices by JAX's collectives and lax.ppermute only.
A program may use at most 64 MiB of HBM per device.

v0:
```python
import jax
import jax.numpy as jnp
from jax import lax
from jax.sharding import PartitionSpec as P

STEPS = 2


mix_weight = 0.3


def propagate(base_rows, weight_table, list_table, count_table, panel_blocks, gather_panel):
    block_count, slot_count, block_size, _ = weight_table.shape
    live_table = jnp.arange(slot_count, dtype=jnp.int32)[None, :] < count_table[:, None]
    picks = (
        list_table[:, :, None] == jnp.arange(panel_blocks, dtype=jnp.int32)[None, None, :]
    ) & live_table[:, :, None]
    select = picks.astype(jnp.bfloat16)
    dense = jnp.einsum(
        "bkg,bkpq->bpgq", select, weight_table, preferred_element_type=jnp.float32
    ).astype(jnp.bfloat16)
    dense = dense.reshape(block_count * block_size, panel_blocks * block_size)
    degree = jnp.sum(dense, axis=1, dtype=jnp.float32)
    row_scale = lax.rsqrt(degree)[:, None]
    hidden = base_rows.astype(jnp.bfloat16)
    for step_index in range(STEPS):
        panel_rows = gather_panel(hidden)
        running = jnp.dot(dense, panel_rows, preferred_element_type=jnp.float32)
        hidden = (mix_weight * base_rows + (1.0 - mix_weight) * running * row_scale).astype(
            jnp.bfloat16
        )
    return hidden


def shards(encoded, owner_of, nbr_blocks, nbr_count, edge_weights):
    row_count, feat_width = encoded.shape
    block_count, slot_count, block_size, _ = edge_weights.shape
    target_dev = owner_of // row_count
    send_order = jnp.argsort(target_dev, stable=True)
    row_ids = jnp.arange(row_count, dtype=jnp.int32)
    send_pick = (send_order[:, None] == row_ids[None, :]).astype(jnp.float32)
    outgoing = jnp.dot(
        send_pick, encoded, precision=lax.Precision.HIGHEST, preferred_element_type=jnp.float32
    )
    places = jnp.take(owner_of, send_order, axis=0)
    arrived, where_to = (
        lax.all_to_all(
            outgoing.astype(jnp.bfloat16), ("dom", "grp"), split_axis=0, concat_axis=0, tiled=True
        ).astype(outgoing.dtype),
        lax.all_to_all(places, ("dom", "grp"), split_axis=0, concat_axis=0, tiled=True),
    )
    place_pick = (row_ids[:, None] == (where_to % row_count)[None, :]).astype(jnp.float32)
    base_rows = jnp.dot(
        place_pick, arrived, precision=lax.Precision.HIGHEST, preferred_element_type=jnp.float32
    )

    def group_panel(hidden):
        return lax.all_gather(hidden, "grp", axis=0, tiled=True)

    panel_blocks = block_count * lax.axis_size("grp")
    return propagate(base_rows, edge_weights, nbr_blocks, nbr_count, panel_blocks, group_panel)


def solution(mesh):
    return jax.shard_map(
        shards,
        mesh=mesh,
        in_specs=(
            P(("dom", "grp"), None),
            P(("dom", "grp")),
            P(("dom", "grp"), None),
            P(("dom", "grp")),
            P(("dom", "grp"), None, None, None),
        ),
        out_specs=P(("dom", "grp"), None),
        check_vma=False,
    )
```

profile of v0, /device:TPU:0, one launch (start us, length us, event | category | flops | bytes accessed | tf_op | source)
XLA Modules:
  0.0 178.7 jit_solution(9671089370718514029)
XLA Ops:
  6.5 0.0 copy-start
  6.5 0.8 add_select_fusion.1
  7.4 3.8 %sort.17 = (s32[512]{0:T(512)}, s32[512]{0:T(512)S(1)}) sort(s32[512]{0:T(512)S(1)} %add_select_fusion.1, s32[512]{0:T(512)S(1)} %iota.22), dimensions={0}, to_apply=%region_0.1 | sort | flops 4608 | bytes 8192 | tf_op jit(solution)/shard_map/jit(argsort)/sort | solution.py:39
  11.2 3.6 %gather_fusion = s32[512]{0:T(512)S(1)} fusion(s32[512]{0:T(512)} %param.6, s32[1024]{0:T(1024)S(1)} %pad_clamp_fusion), kind=kCustom, calls=%fused_computation | custom fusion | bytes 6144 | tf_op jit(solution)/shard_map/jit(_take)/gather | solution.py:45
  14.8 0.7 select_n.37
  15.5 11.1 %all-to-all-start = ((s32[128,4,1]{1,2,0:T(1,128)}), s32[128,4,1]{1,2,0:T(1,128)S(1)}, u32[]{:S(2)}, u32[]{:S(2)}) async-start(s32[128,4,1]{1,2,0:T(1,128)} %bitcast), calls=%async_computation | async-start | bytes 131072 | tf_op jit(solution)/shard_map/all_to_all | solution.py:50
  26.7 3.6 %convolution_convert_fusion = bf16[512,1024]{1,0:T(8,128)(2,1)S(1)} fusion(f32[512,1024]{1,0:T(8,128)} %param.5, s32[512]{0:T(512)S(1)} %get-tuple-element.6), kind=kOutput, calls=%fused_computation.13 | convolution fusion | flops 3222011904 | bytes 3147776 | tf_op jit(solution)/shard_map/dot_general | solution.py:42
  30.3 1.2 all_to_all.16
  31.5 4.3 %all-to-all-done = s32[128,4,1]{1,2,0:T(1,128)S(1)} async-done(((s32[128,4,1]{1,2,0:T(1,128)}), s32[128,4,1]{1,2,0:T(1,128)S(1)}, u32[]{:S(2)}, u32[]{:S(2)}) %all-to-all-start) | async-done | bytes 2080 | tf_op jit(solution)/shard_map/all_to_all | solution.py:50
  35.8 5.5 %all-to-all-start.1 = ((bf16[128,4,1024]{2,1,0:T(4,128)(2,1)}), bf16[128,4,1024]{2,1,0:T(4,128)(2,1)S(1)}, u32[]{:S(2)}, u32[]{:S(2)}) async-start(bf16[128,4,1024]{2,1,0:T(4,128)(2,1)} %all_to_all.16), calls=%async_computation.1 | async-start | bytes 2097152 | tf_op jit(solution)/shard_map/all_to_all | solution.py:47
  41.2 0.0 all-gather.3.cloned.1.call-start
  41.3 0.5 broadcast.84
  41.8 0.8 reduce.4
  42.6 0.1 all_to_all.15
  42.7 17.2 %all-to-all-done.1 = bf16[128,4,1024]{2,1,0:T(4,128)(2,1)S(1)} async-done(((bf16[128,4,1024]{2,1,0:T(4,128)(2,1)}), bf16[128,4,1024]{2,1,0:T(4,128)(2,1)S(1)}, u32[]{:S(2)}, u32[]{:S(2)}) %all-to-all-start.1) | async-done | bytes 1048608 | tf_op jit(solution)/shard_map/all_to_all | solution.py:47
  60.0 1.1 all_to_all.18
  61.1 0.0 copy-start.2
  61.1 0.0 copy-start.1
  61.1 3.7 %fusion.26 = (bf16[512,1024]{1,0:T(8,128)(2,1)}, f32[512,1024]{1,0:T(8,128)}) fusion(bf16[512,1024]{1,0:T(8,128)(2,1)} %all_to_all.18, s32[512]{0:T(512)S(1)} %add_select_fusion), kind=kOutput, calls=%fused_computation.40 | convolution fusion | flops 537657344 | bytes 4196352 | tf_op jit(solution)/shard_map/dot_general | solution.py:53
  64.8 0.0 all-gather.3.cloned.1.call-update
  64.8 0.2 all-gather.5.cloned.1.call-start
  65.0 0.0 copy-done.2
  65.0 0.1 iota_compare_fusion.5
  65.1 0.0 copy-done
  65.1 0.0 copy-done.1
  65.1 3.6 %convert_reduce_fusion = (f32[4,128]{1,0:T(4,128)S(1)}, bf16[4,16,128,128]{3,1,2,0:T(8,128)(2,1)}) fusion(bf16[4,16,128,128]{3,2,1,0:T(8,128)(2,1)S(1)} %copy-done, s32[4,16]{1,0:T(4,128)S(1)} %copy-done.1, pred[4,16]{1,0:T(4,128)(4,1)S(1)} %iota_compare_fusion.5), kind=kOutput, calls=%fused_computation.1 | convolution fusion | flops 36701696 | bytes 4196672 | tf_op jit(solution)/shard_map/bkg,bkpq->bpgq/dot_general | solution.py:19
  68.7 40.7 %all-gather.3.cloned.1.call-done = bf16[2048,1024]{1,0:T(8,128)(2,1)} async-done(((bf16[512,1024]{1,0:T(8,128)(2,1)}), bf16[2048,1024]{1,0:T(8,128)(2,1)}) %all-gather.3.cloned.1.call-update) | async-done | bytes 4194320 | tf_op jit(solution)/shard_map/all_gather | solution.py:58
  109.5 6.8 %add_convert_fusion.1 = bf16[512,1024]{1,0:T(8,128)(2,1)} fusion(f32[512,1024]{1,0:T(8,128)} %get-tuple-element.8, bf16[2048,1024]{1,0:T(8,128)(2,1)} %all-gather.3.cloned.1.call-done, bf16[64,8,16,128]{3,2,1,0:T(8,128)(2,1)} %bitcast.28, f32[512]{0:T(512)S(1)} %multiply_bitcast_fusion), kind=kOutput, calls=%fused_computation.9 | convolution fusion | flops 2149580800 | bytes 9439232 | tf_op jit(solution)/shard_map/dot_general | solution.py:28
  116.3 0.0 all-gather.5.cloned.1.call-update
  116.3 48.8 %all-gather.5.cloned.1.call-done = bf16[2048,1024]{1,0:T(8,128)(2,1)} async-done(((bf16[512,1024]{1,0:T(8,128)(2,1)}), bf16[2048,1024]{1,0:T(8,128)(2,1)}) %all-gather.5.cloned.1.call-update) | async-done | bytes 4194320 | tf_op jit(solution)/shard_map/all_gather | solution.py:58
  165.1 6.8 %add_convert_fusion = bf16[512,1024]{1,0:T(8,128)(2,1)} fusion(f32[512,1024]{1,0:T(8,128)} %get-tuple-element.8, bf16[2048,1024]{1,0:T(8,128)(2,1)} %all-gather.5.cloned.1.call-done, bf16[64,8,16,128]{3,2,1,0:T(8,128)(2,1)} %bitcast.29, f32[512]{0:T(512)S(1)} %multiply_bitcast_fusion), kind=kOutput, calls=%fused_computation.8 | convolution fusion | flops 2149580800 | bytes 9439232 | tf_op jit(solution)/shard_map/dot_general | solution.py:28
  (6 shorter events, 0.0 us)
Async XLA Ops:
  6.5 58.6 %copy-start = (bf16[4,16,128,128]{3,2,1,0:T(8,128)(2,1)S(1)}, bf16[4,16,128,128]{3,2,1,0:T(8,128)(2,1)}, u32[]{:S(2)}) copy-start(bf16[4,16,128,128]{3,2,1,0:T(8,128)(2,1)} %param.9) | copy-start | bytes 6291460
  15.5 20.3 %all-to-all-start = ((s32[128,4,1]{1,2,0:T(1,128)}), s32[128,4,1]{1,2,0:T(1,128)S(1)}, u32[]{:S(2)}, u32[]{:S(2)}) async-start(s32[128,4,1]{1,2,0:T(1,128)} %bitcast), calls=%async_computation | async-start | bytes 131072 | tf_op jit(solution)/shard_map/all_to_all | solution.py:50
  35.8 24.2 %all-to-all-start.1 = ((bf16[128,4,1024]{2,1,0:T(4,128)(2,1)}), bf16[128,4,1024]{2,1,0:T(4,128)(2,1)S(1)}, u32[]{:S(2)}, u32[]{:S(2)}) async-start(bf16[128,4,1024]{2,1,0:T(4,128)(2,1)} %all_to_all.16), calls=%async_computation.1 | async-start | bytes 2097152 | tf_op jit(solution)/shard_map/all_to_all | solution.py:47
  41.2 68.2 %all-gather.3.cloned.1.call-start = ((), (), s32[]{:S(2)}) async-start(), calls=%async_computation.2 | async-start | bytes 5242880 | tf_op jit(solution)/shard_map/all_gather | solution.py:58
  61.1 4.0 %copy-start.2 = (s32[4]{0:T(128)S(1)}, s32[4]{0:T(128)}, u32[]{:S(2)}) copy-start(s32[4]{0:T(128)} %param.8) | copy-start | bytes 52
  61.1 4.0 %copy-start.1 = (s32[4,16]{1,0:T(4,128)S(1)}, s32[4,16]{1,0:T(4,128)}, u32[]{:S(2)}) copy-start(s32[4,16]{1,0:T(4,128)} %param.7) | copy-start | bytes 772
  64.8 100.3 %all-gather.5.cloned.1.call-start = ((), (), s32[]{:S(2)}) async-start(), calls=%async_computation.3 | async-start | bytes 5242880 | tf_op jit(solution)/shard_map/all_gather | solution.py:58
Sparse Core Ops, SparseCore 0:
  64.9 44.5 all-gather.2
  116.4 48.6 all-gather.4
where the time goes:
time: 180 us; the launch traced here: 179 us
  waiting for transfers between devices  111 us (62%)
  matrix products  24.5 us (14%)
  starting transfers between devices  16.9 us (9%)
  between operations  13.5 us (8%)
  local copies, waits for them, and re-layouts  7.3 us (4%)
  other arithmetic  5.51 us (3%)
    all_gather x2, waiting for transfers between devices, group_panel(): return lax.all_gather(hidden, 'grp', axis=0, tiled=True)  89.6 us
    all_to_all x1, waiting for transfers between devices, shards(): lax.all_to_all(outgoing.astype(jnp.bfloat16), ('dom', 'grp'), split_axis=...  17.2 us
    dot_general x2, matrix products, propagate(): running = jnp.dot(dense, panel_rows, preferred_element_type=jnp.float32)  13.6 us
    all_to_all x1, starting transfers between devices, shards(): lax.all_to_all(places, ('dom', 'grp'), split_axis=0, concat_axis=0, tiled...  11.1 us
    all_to_all x1, starting transfers between devices, shards(): lax.all_to_all(outgoing.astype(jnp.bfloat16), ('dom', 'grp'), split_axis=...  5.46 us
    all_to_all x1, waiting for transfers between devices, shards(): lax.all_to_all(places, ('dom', 'grp'), split_axis=0, concat_axis=0, tiled...  4.31 us
    sort x1, other arithmetic, shards(): send_order = jnp.argsort(target_dev, stable=True)  3.77 us
    dot_general x1, matrix products, shards(): jnp.dot(place_pick, arrived, precision=lax.Precision.HIGHEST, preferred_e...  3.69 us
  transfers between devices with their start and end apart: 4, of which 4 were waited for; matrix products, arithmetic and copies ran while one was open for 5% of the time, Pallas kernels for 0%

commit v1 on v0

v1 whole, which is shorter than its diff:
```python
import functools

import jax
import jax.numpy as jnp
from jax import lax
from jax.experimental import pallas as pl
from jax.experimental.pallas import tpu as pltpu
from jax.sharding import PartitionSpec as P

AXES = ("dom", "grp")
MIX = 0.3
CHUNKS = 2
VMEM = pl.BlockSpec(memory_space=pltpu.VMEM)
SMEM = pl.BlockSpec(memory_space=pltpu.SMEM)


def kernel_call(body, out_shape, in_specs, flops, moved, scratch=(), limit=40):
    outs = out_shape if isinstance(out_shape, (tuple, list)) else (out_shape,)
    specs = tuple(VMEM for _ in outs)
    return pl.pallas_call(
        body,
        out_shape=out_shape,
        in_specs=in_specs,
        out_specs=specs if isinstance(out_shape, (tuple, list)) else specs[0],
        scratch_shapes=scratch,
        compiler_params=pltpu.CompilerParams(vmem_limit_bytes=limit * 1024 * 1024),
        cost_estimate=pl.CostEstimate(flops=flops, bytes_accessed=moved, transcendentals=0),
    )


def sort_kernel(doms, flip_ref, owner_ref, enc_ref, other_ref, mine_ref):
    rows, width = enc_ref.shape
    half = width // 2
    per = rows // doms
    owner = owner_ref[...]
    group_nodes = rows * 4
    tdom = owner // group_nodes
    place = (owner - tdom * group_nodes).astype(jnp.float32)
    hot = (lax.broadcasted_iota(jnp.int32, (doms, rows), 0) == tdom).astype(jnp.float32)
    before = (
        lax.broadcasted_iota(jnp.int32, (rows, rows), 0)
        < lax.broadcasted_iota(jnp.int32, (rows, rows), 1)
    ).astype(jnp.bfloat16)
    seen = jnp.dot(hot.astype(jnp.bfloat16), before, preferred_element_type=jnp.float32)
    rank = jnp.sum(hot * seen, axis=0, keepdims=True)
    slot = tdom * per + rank.astype(jnp.int32)
    pick = lax.broadcasted_iota(jnp.int32, (rows, rows), 0) == slot
    place_of = jnp.sum(jnp.where(pick, place, 0.0), axis=1, keepdims=True)
    pick = pick.astype(jnp.bfloat16)
    slot_row = lax.broadcasted_iota(jnp.int32, (rows, 1), 0)
    parity = (slot_row // per) % 2
    upper = jnp.where(parity == 0, flip_ref[0], flip_ref[1]) == 1
    moved = jnp.dot(pick, enc_ref[...].astype(jnp.bfloat16), preferred_element_type=jnp.float32)
    low, high = moved[:, :half], moved[:, half:]
    other_ref[:, :half] = jnp.where(upper, low, high).astype(jnp.bfloat16)
    mine_ref[...] = jnp.where(upper, high, low).astype(jnp.bfloat16)
    place_of = place_of.astype(jnp.int32)
    lane = lax.broadcasted_iota(jnp.int32, (rows, 128), 1)
    coded = jnp.where(lane == 0, place_of // 64, jnp.where(lane == 1, place_of % 64, 0))
    other_ref[:, half:] = coded.astype(jnp.float32).astype(jnp.bfloat16)


def place_kernel(arrived_ref, places_ref, rows_ref):
    rows, width = rows_ref.shape
    lane = lax.broadcasted_iota(jnp.int32, (8, 128), 1)
    weight = jnp.where(lane == 0, 64.0, jnp.where(lane == 1, 1.0, 0.0)).astype(jnp.bfloat16)
    places_ref[...] = lax.dot_general(
        weight, arrived_ref[:, width:], (((1,), (1,)), ((), ())), preferred_element_type=jnp.float32
    )
    rows_ref[...] = arrived_ref[:, :width]


def dense_kernel(count_ref, column_ref, weight_ref, dense_ref, scale_ref):
    blocks, _, size, _ = weight_ref.shape
    for b in range(blocks):
        span = pl.ds(b * size, size)
        dense_ref[span, :] = jnp.zeros((size, dense_ref.shape[1]), dense_ref.dtype)

        def put(k, total):
            block = weight_ref[b, k]
            start = pl.multiple_of(column_ref[b, k] * size, size)
            dense_ref[span, pl.ds(start, size)] = block
            return total + block.astype(jnp.float32)

        total = lax.fori_loop(0, count_ref[b], put, jnp.zeros((size, size), jnp.float32))
        degree = jnp.sum(total, axis=1, keepdims=True)
        scale_ref[span, :] = jnp.broadcast_to((1.0 - MIX) * lax.rsqrt(degree), (size, 128))


def scatter_kernel(fz_ref, own_at, row_at, both_at, last_at, own_ref, row_ref, both_ref, part_ref, last_pick_ref):
    nodes = part_ref.shape[0]
    rx, fx = fz_ref[0], fz_ref[1]
    z = fz_ref[2]
    size = own_ref.shape[0]

    def local(at):
        p = at[0:1, :].astype(jnp.int32)
        step = (p // size) ^ z
        where = jnp.where(step == 0, 0, jnp.where(step == rx, 1, jnp.where(step == fx, 2, 3)))
        return where * size + p % size

    spots = [local(a) for a in (own_at, row_at, both_at, last_at)]
    tile = 256

    def one(t, _):
        base = pl.multiple_of(t * tile, tile)
        node = lax.broadcasted_iota(jnp.int32, (tile, size), 0) + base
        picks = [(node == s).astype(jnp.bfloat16) for s in spots]
        total = jnp.dot(picks[0], own_ref[...], preferred_element_type=jnp.float32)
        total += jnp.dot(picks[1], row_ref[...], preferred_element_type=jnp.float32)
        total += jnp.dot(picks[2], both_ref[...], preferred_element_type=jnp.float32)
        part_ref[pl.ds(base, tile), :] = total.astype(jnp.bfloat16)
        last_pick_ref[pl.ds(base, tile), :] = picks[3]
        return 0

    lax.fori_loop(0, nodes // tile, one, 0)


def first_kernel(col, dense_a, dense_b, scale_a, scale_b, part_ref, last_pick_ref, last_ref, base_ref, hidden_ref, panel):
    width = hidden_ref.shape[1]
    cols = pl.ds(col * width, width)
    nodes = part_ref.shape[0]
    tile = 256
    last = last_ref[:, cols]

    def one(t, _):
        at = pl.ds(pl.multiple_of(t * tile, tile), tile)
        fresh = jnp.dot(last_pick_ref[at, :], last, preferred_element_type=jnp.float32)
        panel[at, :] = (part_ref[at, cols].astype(jnp.float32) + fresh).astype(jnp.bfloat16)
        return 0

    lax.fori_loop(0, nodes // tile, one, 0)
    size = dense_a.shape[0]
    for n, (dense, scale) in enumerate(((dense_a, scale_a), (dense_b, scale_b))):

        def two(t, _):
            at = pl.ds(pl.multiple_of(t * tile, tile), tile)
            to = pl.ds(pl.multiple_of(t * tile + n * size, tile), tile)
            total = jnp.dot(dense[at, :], panel[...], preferred_element_type=jnp.float32)
            base = panel[to, :]
            base_ref[to, :] = base
            hidden_ref[to, :] = (MIX * base.astype(jnp.float32) + total * scale[at, 0:1]).astype(jnp.bfloat16)
            return 0

        lax.fori_loop(0, size // tile, two, 0)


def half_kernel(dense_a, dense_b, hidden_ref, total_ref):
    size = dense_a.shape[0]
    depth = hidden_ref.shape[0]
    tile = 256
    for n, dense in enumerate((dense_a, dense_b)):

        def one(t, _):
            at = pl.ds(pl.multiple_of(t * tile, tile), tile)
            to = pl.ds(pl.multiple_of(t * tile + n * size, tile), tile)
            total_ref[to, :] = jnp.dot(dense[at, :depth], hidden_ref[...], preferred_element_type=jnp.float32)
            return 0

        lax.fori_loop(0, size // tile, one, 0)


def last_kernel(dense_a, dense_b, scale_a, scale_b, total_ref, hidden_ref, base_ref, keep_ref, send_ref):
    size = dense_a.shape[0]
    depth = hidden_ref.shape[0]
    tile = 256
    for n, (dense, scale, out) in enumerate(((dense_a, scale_a, keep_ref), (dense_b, scale_b, send_ref))):

        def one(t, _):
            at = pl.ds(pl.multiple_of(t * tile, tile), tile)
            to = pl.ds(pl.multiple_of(t * tile + n * size, tile), tile)
            total = total_ref[to, :] + jnp.dot(
                dense[at, depth:], hidden_ref[...], preferred_element_type=jnp.float32
            )
            out[at, :] = (MIX * base_ref[to, :].astype(jnp.float32) + total * scale[at, 0:1]).astype(jnp.bfloat16)
            return 0

        lax.fori_loop(0, size // tile, one, 0)


def row_step(core):
    return 1 if core == 0 else 3


def upper_half(core, z):
    return int(z in (1, 2)) if core == 0 else z // 2


def shards(doms, depth, encoded, owner_of, nbr_blocks, nbr_count, edge_weights):
    f32, bf16, i32 = jnp.float32, jnp.bfloat16, jnp.int32
    rows, width = encoded.shape
    half = width // 2
    blocks, slots, size, _ = edge_weights.shape
    nodes = rows * depth
    part = half // CHUNKS
    z = lax.axis_index("grp").astype(i32)
    core = (lax.axis_index("dom") % 2).astype(i32)
    rx = jnp.where(core == 0, 1, 3).astype(i32)
    fx = jnp.where(core == 0, 3, 1).astype(i32)
    halves = jnp.array([[upper_half(c, q) for c in range(2)] for q in range(depth)], i32)
    flips = halves[z]
    upper = flips[core]
    row_pairs = [(d * depth + q, d * depth + (q ^ row_step(d % 2))) for d in range(doms) for q in range(depth)]
    col_pairs = [(d * depth + q, d * depth + (q ^ row_step(1 - d % 2))) for d in range(doms) for q in range(depth)]
    both_pairs = [(d * depth + q, d * depth + (q ^ 2)) for d in range(doms) for q in range(depth)]

    def to_row(a):
        return lax.ppermute(a, AXES, row_pairs)

    def to_col(a):
        return lax.ppermute(a, AXES, col_pairs)

    lists = jnp.concatenate([nbr_blocks, jnp.broadcast_to(nbr_count[:, None], (blocks, slots))], 0)
    far_weights = to_row(edge_weights)
    far_lists = to_row(lists)

    def columns(table):
        step = (table // blocks) ^ z
        where = jnp.where(step == 0, 0, jnp.where(step == rx, 1, jnp.where(step == fx, 2, 3)))
        return (where * blocks + table % blocks).astype(i32)

    def dense_of(lists, weights):
        return kernel_call(
            dense_kernel,
            (jax.ShapeDtypeStruct((blocks * size, nodes), bf16), jax.ShapeDtypeStruct((blocks * size, 128), f32)),
            [SMEM, SMEM, VMEM],
            0,
            8 << 20,
        )(lists[blocks:, 0], columns(lists[:blocks]), weights)

    other, mine = kernel_call(
        functools.partial(sort_kernel, doms),
        (jax.ShapeDtypeStruct((rows, half + 128), bf16), jax.ShapeDtypeStruct((rows, half), bf16)),
        [SMEM, VMEM, VMEM],
        2 * rows * rows * width,
        4 << 20,
    )(flips, owner_of.reshape(1, rows), encoded)

    got_other = lax.all_to_all(other, "dom", 0, 0, tiled=True)
    got_mine = lax.all_to_all(mine, "dom", 0, 0, tiled=True)
    own_at, got_other = kernel_call(
        place_kernel,
        (jax.ShapeDtypeStruct((8, rows), f32), jax.ShapeDtypeStruct((rows, half), bf16)),
        [VMEM],
        1 << 20,
        1 << 20,
    )(got_other)
    row_at, last_at, both_at = (
        to_row(own_at),
        to_col(own_at),
        lax.ppermute(own_at, AXES, both_pairs),
    )
    row_rows = to_row(got_other)
    both_rows = to_col(row_rows)
    last_rows = to_col(got_mine)

    dense_a, scale_a = dense_of(lists, edge_weights)
    dense_b, scale_b = dense_of(far_lists, far_weights)

    placed, last_pick = kernel_call(
        scatter_kernel,
        (jax.ShapeDtypeStruct((nodes, half), bf16), jax.ShapeDtypeStruct((nodes, rows), bf16)),
        [SMEM] + [VMEM] * 7,
        2 * nodes * 3 * rows * half,
        8 << 20,
    )(jnp.stack([rx, fx, z]), own_at, row_at, both_at, last_at, got_mine, row_rows, both_rows)

    mine_n = 2 * rows
    kept, sent = [], []
    for c in range(CHUNKS):
        base, hidden = kernel_call(
            functools.partial(first_kernel, c),
            (jax.ShapeDtypeStruct((mine_n, part), bf16), jax.ShapeDtypeStruct((mine_n, part), bf16)),
            [VMEM] * 7,
            2 * nodes * rows * part + 2 * mine_n * nodes * part,
            8 << 20,
            scratch=[pltpu.VMEM((nodes, part), bf16)],
        )(dense_a, dense_b, scale_a, scale_b, placed, last_pick, last_rows)
        far_hidden = to_col(hidden)
        total = kernel_call(
            half_kernel,
            jax.ShapeDtypeStruct((mine_n, part), f32),
            [VMEM] * 3,
            2 * mine_n * mine_n * part,
            4 << 20,
        )(dense_a, dense_b, hidden)
        keep, send = kernel_call(
            last_kernel,
            (jax.ShapeDtypeStruct((rows, part), bf16), jax.ShapeDtypeStruct((rows, part), bf16)),
            [VMEM] * 7,
            2 * mine_n * mine_n * part,
            4 << 20,
        )(dense_a, dense_b, scale_a, scale_b, total, far_hidden, base)
        kept.append(keep)
        sent.append(to_row(send))
    kept = jnp.concatenate(kept, 1)
    sent = jnp.concatenate(sent, 1)
    low = jnp.where(upper == 0, kept, sent)
    high = jnp.where(upper == 0, sent, kept)
    return jnp.concatenate([low, high], 1)


def solution(mesh):
    return jax.shard_map(
        functools.partial(shards, mesh.shape["dom"], mesh.shape["grp"]),
        mesh=mesh,
        in_specs=(P(AXES, None), P(AXES), P(AXES, None), P(AXES), P(AXES, None, None, None)),
        out_specs=P(AXES, None),
        check_vma=False,
    )
```

time: 180 us -> 109 us (0.61)
  waiting for transfers between devices: 111 us -> 38.2 us
  Pallas kernels: 0 us -> 31.9 us
  matrix products: 24.5 us -> 0 us
  between operations: 13.5 us -> 0.88 us
  starting transfers between devices: 16.9 us -> 29.4 us
  other arithmetic: 5.51 us -> 1.35 us
    all_gather x2 -> x0, waiting for transfers between devices: 89.6 us -> none  [group_panel(): return lax.all_gather(hidden, 'grp', axis=0, tiled=True)]
    pallas_call x0 -> x11, Pallas kernels: none -> 31.9 us  [the longest x2 8.97 us: shards(): kernel_call(functools.partial(first_kernel, c), (jax.ShapeDtypeStruct((mi...]
    ppermute x0 -> x12, waiting for transfers between devices: none -> 27 us  [the longest x6 19.6 us: to_row(): return lax.ppermute(a, AXES, row_pairs)]
    dot_general x5 -> x0, matrix products: 24.5 us -> none  [the longest x2 13.6 us: propagate(): running = jnp.dot(dense, panel_rows, preferred_element_type=jnp.float32)]
    ppermute x0 -> x12, starting transfers between devices: none -> 16.7 us  [the longest x5 10.6 us: to_col(): return lax.ppermute(a, AXES, col_pairs)]
    all_to_all x2, waiting for transfers between devices: 21.5 us -> 11.2 us  [the longest x1 11.2 us: shards(): got_other = lax.all_to_all(other, 'dom', 0, 0, tiled=True)]
    unnamed x6 -> x18, local copies, waits for them, and re-layouts: 0.01 us -> 3.91 us
    all_to_all x2, starting transfers between devices: 16.6 us -> 12.7 us  [the longest x1 7.4 us: shards(): got_other = lax.all_to_all(other, 'dom', 0, 0, tiled=True)]
  transfers between devices with their start and end apart: 4 -> 14, of which waited for: 4 -> 6; matrix products, arithmetic and copies ran while one was open for 5% -> 2% of each run, Pallas kernels for 0% -> 23%
where the time goes in v1:
time: 109 us; the launch traced here: 108 us
  waiting for transfers between devices  38.2 us (35%)
  Pallas kernels  31.9 us (29%)
  starting transfers between devices  29.4 us (27%)
  local copies, waits for them, and re-layouts  6.15 us (6%)
  other arithmetic  1.35 us (1%)
    ppermute x6, waiting for transfers between devices, to_row(): return lax.ppermute(a, AXES, row_pairs)  19.6 us
    all_to_all x1, waiting for transfers between devices, shards(): got_other = lax.all_to_all(other, 'dom', 0, 0, tiled=True)  11.2 us
    ppermute x5, starting transfers between devices, to_col(): return lax.ppermute(a, AXES, col_pairs)  10.6 us
    pallas_call x2, Pallas kernels, shards(): kernel_call(functools.partial(first_kernel, c), (jax.ShapeDtypeStruct((mi...  8.97 us
    ppermute x5, waiting for transfers between devices, to_col(): return lax.ppermute(a, AXES, col_pairs)  7.43 us
    all_to_all x1, starting transfers between devices, shards(): got_other = lax.all_to_all(other, 'dom', 0, 0, tiled=True)  7.4 us
    ppermute x6, starting transfers between devices, to_row(): return lax.ppermute(a, AXES, row_pairs)  6.06 us
    pallas_call x1, Pallas kernels, shards(): kernel_call(scatter_kernel, (jax.ShapeDtypeStruct((nodes, half), bf16), j...  5.84 us
  transfers between devices with their start and end apart: 14, of which 6 were waited for; matrix products, arithmetic and copies ran while one was open for 2% of the time, Pallas kernels for 23%

profile of v1, /device:TPU:0, one launch (start us, length us, event | category | flops | bytes accessed | tf_op | source)
XLA Modules:
  0.0 108.0 jit_solution(17319420943871513574)
XLA Ops:
  0.0 0.7 dynamic-slice_bitcast_fusion.flip_ref
  0.7 0.0 copy-start.2
  0.7 1.6 %copy-done.2 = f32[512,1024]{1,0:T(8,128)S(1)} copy-done((f32[512,1024]{1,0:T(8,128)S(1)}, f32[512,1024]{1,0:T(8,128)}, u32[]{:S(2)}) %copy-start.2) | copy-done | bytes 2097176
  2.3 0.0 copy-start.5
  2.3 0.7 copy-done.5
  3.0 0.0 copy-start.6
  3.0 0.0 copy-start.7
  3.0 2.7 %shard_map.66 = (bf16[512,640]{1,0:T(8,128)(2,1)}, bf16[512,512]{1,0:T(8,128)(2,1)}) custom-call(s32[2]{0:T(128)S(1)} %dynamic-slice_bitcast_fusion.flip_ref, s32[1,512]{1,0:T(1,128)S(1)} %bitcast.14, f32[512,1024]{1,0:T(8,128)S(1)} %copy-done.2), custom_call_target="tpu_custom_call" | custom-call | flops 536870912 | bytes 4194304 | tf_op jit(solution)/shard_map/pallas_call | solution.py:231
  5.7 7.4 %all-to-all-start = ((bf16[32,16,640]{2,1,0:T(8,128)(2,1)}), bf16[32,16,640]{2,1,0:T(8,128)(2,1)S(1)}, u32[]{:S(2)}, u32[]{:S(2)}) async-start(bf16[32,16,640]{2,1,0:T(8,128)(2,1)} %bitcast.6), calls=%async_computation | async-start | bytes 1310720 | tf_op jit(solution)/shard_map/all_to_all | solution.py:239
  13.1 2.0 %collective-permute-start.1 = (bf16[4,16,128,128]{3,2,1,0:T(8,128)(2,1)}, bf16[4,16,128,128]{3,2,1,0:T(8,128)(2,1)}, u32[]{:S(2)}, u32[]{:S(2)}) collective-permute-start(bf16[4,16,128,128]{3,2,1,0:T(8,128)(2,1)} %weight_ref.1), channel_id=1, source_target_pairs={{0,1},{1,0},{2,3},{3,2},{4,7},{5,6},{6,5},{7,4},{8,9},{9,8},{10,11... | collective-permute-start | bytes 6291464 | tf_op jit(solution)/shard_map/ppermute | solution.py:208
  15.1 11.2 %all-to-all-done = bf16[32,16,640]{2,1,0:T(8,128)(2,1)S(1)} async-done(((bf16[32,16,640]{2,1,0:T(8,128)(2,1)}), bf16[32,16,640]{2,1,0:T(8,128)(2,1)S(1)}, u32[]{:S(2)}, u32[]{:S(2)}) %all-to-all-start) | async-done | bytes 655392 | tf_op jit(solution)/shard_map/all_to_all | solution.py:239
  26.3 0.2 shard_map.67
  26.5 1.9 %collective-permute-start.5 = (bf16[512,512]{1,0:T(8,128)(2,1)S(1)}, bf16[512,512]{1,0:T(8,128)(2,1)}, u32[]{:S(2)}, u32[]{:S(2)}) collective-permute-start(bf16[512,512]{1,0:T(8,128)(2,1)S(1)} %get-tuple-element.30), channel_id=1, source_target_pairs={{0,1},{1,0},{2,3},{3,2},{4,7},{5,6},{6,5},{7,4},{8,9},{9,8},{10,11... | collective-permute-start | bytes 1572872 | tf_op jit(solution)/shard_map/ppermute | solution.py:208
  28.4 5.3 %all-to-all-start.1 = ((bf16[32,16,512]{2,1,0:T(8,128)(2,1)}), bf16[32,16,512]{2,1,0:T(8,128)(2,1)S(1)}, u32[]{:S(2)}, u32[]{:S(2)}) async-start(bf16[32,16,512]{2,1,0:T(8,128)(2,1)} %bitcast.8), calls=%async_computation.1 | async-start | bytes 1048576 | tf_op jit(solution)/shard_map/all_to_all | solution.py:240
  33.7 0.0 copy-done.6
  33.7 0.1 pad.6.clone
  33.8 0.0 copy-done.7
  33.8 0.1 pad_add_fusion
  33.9 0.0 collective-permute-start
  33.9 11.3 %collective-permute-done.5.row_ref = bf16[512,512]{1,0:T(8,128)(2,1)} collective-permute-done((bf16[512,512]{1,0:T(8,128)(2,1)S(1)}, bf16[512,512]{1,0:T(8,128)(2,1)}, u32[]{:S(2)}, u32[]{:S(2)}) %collective-permute-start.5) | collective-permute-done | bytes 524320 | tf_op jit(solution)/shard_map/ppermute | solution.py:208
  45.2 4.0 %collective-permute-start.6 = (bf16[512,512]{1,0:T(8,128)(2,1)}, bf16[512,512]{1,0:T(8,128)(2,1)}, u32[]{:S(2)}, u32[]{:S(2)}) collective-permute-start(bf16[512,512]{1,0:T(8,128)(2,1)} %collective-permute-done.5.row_ref), channel_id=1, source_target_pairs={{0,3},{1,2},{2,1},{3,0},{4,5},{5,4},{6,7},{7,6},{8,11},{9,10},{10,... | collective-permute-start | bytes 1572872 | tf_op jit(solution)/shard_map/ppermute | solution.py:211
  49.2 0.1 pad_add_fusion.1.fz_ref
  49.3 2.4 %shard_map.64 = (bf16[512,2048]{1,0:T(8,128)(2,1)S(1)}, f32[512,128]{1,0:T(8,128)S(1)}) custom-call(s32[4]{0:T(128)S(1)} %copy-done.6, s32[4,16]{1,0:T(4,128)S(1)} %fusion.1.column_ref, bf16[4,16,128,128]{3,2,1,0:T(8,128)(2,1)} %weight_ref.1), custom_call_target="tpu_custom_call" | custom-call | bytes 8388608 | tf_op jit(solution)/shard_map/pallas_call | solution.py:223
  51.7 0.0 all-to-all-done.1
  51.7 0.3 collective-permute-start.7
  52.0 3.1 %collective-permute-start.4 = (f32[8,512]{1,0:T(8,128)S(1)}, f32[8,512]{1,0:T(8,128)S(1)}, u32[]{:S(2)}, u32[]{:S(2)}) collective-permute-start(f32[8,512]{1,0:T(8,128)S(1)} %get-tuple-element.28.own_at), channel_id=1, source_target_pairs={{0,3},{1,2},{2,1},{3,0},{4,5},{5,4},{6,7},{7,6},{8,11},{9,10},{10,... | collective-permute-start | bytes 49160 | tf_op jit(solution)/shard_map/ppermute | solution.py:211
  55.0 0.0 collective-permute-done
  55.1 0.1 collective-permute-start.3
  55.2 7.4 %collective-permute-done.4.last_at = f32[8,512]{1,0:T(8,128)S(1)} collective-permute-done((f32[8,512]{1,0:T(8,128)S(1)}, f32[8,512]{1,0:T(8,128)S(1)}, u32[]{:S(2)}, u32[]{:S(2)}) %collective-permute-start.4) | collective-permute-done | bytes 16416 | tf_op jit(solution)/shard_map/ppermute | solution.py:211
  62.5 0.0 collective-permute-start.2
  62.5 0.1 slice_reduce_fusion.count_ref
  62.7 0.0 collective-permute-done.3.both_at
  62.7 3.6 %collective-permute-done.2.row_at = f32[8,512]{1,0:T(8,128)S(1)} collective-permute-done((f32[8,512]{1,0:T(8,128)S(1)}, f32[8,512]{1,0:T(8,128)S(1)}, u32[]{:S(2)}, u32[]{:S(2)}) %collective-permute-start.2) | collective-permute-done | bytes 16416 | tf_op jit(solution)/shard_map/ppermute | solution.py:208
  66.3 0.0 collective-permute-done.6.both_ref
  66.3 5.8 %shard_map.68 = (bf16[2048,512]{1,0:T(8,128)(2,1)S(1)}, bf16[2048,512]{1,0:T(8,128)(2,1)S(1)}) custom-call(s32[3]{0:T(128)S(1)} %pad_add_fusion.1.fz_ref, f32[8,512]{1,0:T(8,128)S(1)} %get-tuple-element.28.own_at, f32[8,512]{1,0:T(8,128)S(1)} %collective-permute-done.2.row_at, f32[8,512]{1,0:T(8,128)S(1)} %collective-permute-done.3.both_at, ...), custom_call_target="tpu_custom_call" | custom-call | flops 3221225472 | bytes 8388608 | tf_op jit(solution)/shard_map/pallas_call | solution.py:260
  72.1 0.0 collective-permute-done.1.weight_ref
  72.1 2.6 %shard_map.65 = (bf16[512,2048]{1,0:T(8,128)(2,1)S(1)}, f32[512,128]{1,0:T(8,128)S(1)}) custom-call(s32[4]{0:T(128)S(1)} %slice_reduce_fusion.count_ref, s32[4,16]{1,0:T(4,128)S(1)} %fusion.3.column_ref, bf16[4,16,128,128]{3,2,1,0:T(8,128)(2,1)} %collective-permute-done.1.weight_ref), custom_call_target="tpu_custom_call" | custom-call | bytes 8388608 | tf_op jit(solution)/shard_map/pallas_call | solution.py:223
  74.8 0.0 copy-start
  74.8 0.0 collective-permute-done.7.last_ref
  74.8 4.5 %shard_map.69 = (bf16[1024,256]{1,0:T(8,128)(2,1)S(1)}, bf16[1024,256]{1,0:T(8,128)(2,1)}) custom-call(bf16[512,2048]{1,0:T(8,128)(2,1)S(1)} %get-tuple-element.23.dense_a, bf16[512,2048]{1,0:T(8,128)(2,1)S(1)} %get-tuple-element.24.dense_b, f32[512,128]{1,0:T(8,128)S(1)} %get-tuple-element.25.scale_a, f32[512,128]{1,0:T(8,128)S(1)} %get-tuple-element.26.scale_b, ...), custom_call_target="tpu_custom_call" | custom-call | flops 1610612736 | bytes 8388608 | tf_op jit(solution)/shard_map/pallas_call | solution.py:271
  79.3 0.0 copy-start.3
  79.3 3.1 %collective-permute-start.8 = (bf16[1024,256]{1,0:T(8,128)(2,1)}, bf16[1024,256]{1,0:T(8,128)(2,1)}, u32[]{:S(2)}, u32[]{:S(2)}) collective-permute-start(bf16[1024,256]{1,0:T(8,128)(2,1)} %get-tuple-element.33.hidden_ref), channel_id=1, source_target_pairs={{0,3},{1,2},{2,1},{3,0},{4,5},{5,4},{6,7},{7,6},{8,11},{9,10},{10,... | collective-permute-start | bytes 1572872 | tf_op jit(solution)/shard_map/ppermute | solution.py:211
  82.4 0.0 copy-done
  82.4 4.5 %shard_map.72 = (bf16[1024,256]{1,0:T(8,128)(2,1)S(1)}, bf16[1024,256]{1,0:T(8,128)(2,1)}) custom-call(bf16[512,2048]{1,0:T(8,128)(2,1)S(1)} %get-tuple-element.23.dense_a, bf16[512,2048]{1,0:T(8,128)(2,1)S(1)} %get-tuple-element.24.dense_b, f32[512,128]{1,0:T(8,128)S(1)} %get-tuple-element.25.scale_a, f32[512,128]{1,0:T(8,128)S(1)} %get-tuple-element.26.scale_b, ...), custom_call_target="tpu_custom_call" | custom-call | flops 1610612736 | bytes 8388608 | tf_op jit(solution)/shard_map/pallas_call | solution.py:271
  86.9 0.0 copy-done.3
  86.9 0.1 collective-permute-start.9
  87.0 1.3 %dynamic_slice.6 = s32[1,1]{1,0:T(1,128)} dynamic-slice(s32[4,2]{1,0:T(4,128)} %constant.79.clone, s32[]{:T(128)S(6)} %select_n.75, s32[]{:T(128)S(6)} %select_n.78), dynamic_slice_sizes={1,1} | dynamic-slice | bytes 12 | tf_op jit(solution)/shard_map/dynamic_slice | solution.py:202
  89.0 0.0 copy-start.1
  89.0 1.6 %copy-done.1 = bf16[512,2048]{1,0:T(8,128)(2,1)S(1)} copy-done((bf16[512,2048]{1,0:T(8,128)(2,1)S(1)}, bf16[512,2048]{1,0:T(8,128)(2,1)}, u32[]{:S(2)}) %copy-start.1) | copy-done | bytes 2097176
  90.6 2.3 %shard_map.73.total_ref = f32[1024,256]{1,0:T(8,128)S(1)} custom-call(bf16[512,2048]{1,0:T(8,128)(2,1)S(1)} %get-tuple-element.23.dense_a, bf16[512,2048]{1,0:T(8,128)(2,1)S(1)} %copy-done.1, bf16[1024,256]{1,0:T(8,128)(2,1)} %get-tuple-element.36.hidden_ref), custom_call_target="tpu_custom_call" | custom-call | flops 536870912 | bytes 4194304 | tf_op jit(solution)/shard_map/pallas_call | solution.py:280
  92.9 0.0 copy-start.4
  92.9 2.3 %shard_map.70.total_ref = f32[1024,256]{1,0:T(8,128)S(1)} custom-call(bf16[512,2048]{1,0:T(8,128)(2,1)S(1)} %get-tuple-element.23.dense_a, bf16[512,2048]{1,0:T(8,128)(2,1)S(1)} %copy-done.1, bf16[1024,256]{1,0:T(8,128)(2,1)} %get-tuple-element.33.hidden_ref), custom_call_target="tpu_custom_call" | custom-call | flops 536870912 | bytes 4194304 | tf_op jit(solution)/shard_map/pallas_call | solution.py:280
  95.2 0.0 collective-permute-done.8.hidden_ref
  95.2 0.0 copy-done.4
  95.2 2.3 %shard_map.71 = (bf16[512,256]{1,0:T(8,128)(2,1)S(1)}, bf16[512,256]{1,0:T(8,128)(2,1)S(1)}) custom-call(bf16[512,2048]{1,0:T(8,128)(2,1)S(1)} %get-tuple-element.23.dense_a, bf16[512,2048]{1,0:T(8,128)(2,1)S(1)} %copy-done.1, f32[512,128]{1,0:T(8,128)S(1)} %get-tuple-element.25.scale_a, f32[512,128]{1,0:T(8,128)S(1)} %get-tuple-element.26.scale_b, ...), custom_call_target="tpu_custom_call" | custom-call | flops 536870912 | bytes 4194304 | tf_op jit(solution)/shard_map/pallas_call | solution.py:287
  97.5 0.1 collective-permute-start.10
  97.6 0.0 collective-permute-done.9.hidden_ref
  97.6 2.3 %shard_map.74 = (bf16[512,256]{1,0:T(8,128)(2,1)S(1)}, bf16[512,256]{1,0:T(8,128)(2,1)S(1)}) custom-call(bf16[512,2048]{1,0:T(8,128)(2,1)S(1)} %get-tuple-element.23.dense_a, bf16[512,2048]{1,0:T(8,128)(2,1)S(1)} %copy-done.1, f32[512,128]{1,0:T(8,128)S(1)} %get-tuple-element.25.scale_a, f32[512,128]{1,0:T(8,128)S(1)} %get-tuple-element.26.scale_b, ...), custom_call_target="tpu_custom_call" | custom-call | flops 536870912 | bytes 4194304 | tf_op jit(solution)/shard_map/pallas_call | solution.py:287
  99.9 2.1 %collective-permute-start.11 = (bf16[512,256]{1,0:T(8,128)(2,1)S(1)}, bf16[512,256]{1,0:T(8,128)(2,1)S(1)}, u32[]{:S(2)}, u32[]{:S(2)}) collective-permute-start(bf16[512,256]{1,0:T(8,128)(2,1)S(1)} %get-tuple-element.40), channel_id=1, source_target_pairs={{0,1},{1,0},{2,3},{3,2},{4,7},{5,6},{6,5},{7,4},{8,9},{9,8},{10,11... | collective-permute-start | bytes 786440 | tf_op jit(solution)/shard_map/ppermute | solution.py:208
  102.0 1.9 %collective-permute-done.10 = bf16[512,256]{1,0:T(8,128)(2,1)S(1)} collective-permute-done((bf16[512,256]{1,0:T(8,128)(2,1)S(1)}, bf16[512,256]{1,0:T(8,128)(2,1)S(1)}, u32[]{:S(2)}, u32[]{:S(2)}) %collective-permute-start.10) | collective-permute-done | bytes 262176 | tf_op jit(solution)/shard_map/ppermute | solution.py:208
  104.0 2.8 %collective-permute-done.11 = bf16[512,256]{1,0:T(8,128)(2,1)S(1)} collective-permute-done((bf16[512,256]{1,0:T(8,128)(2,1)S(1)}, bf16[512,256]{1,0:T(8,128)(2,1)S(1)}, u32[]{:S(2)}, u32[]{:S(2)}) %collective-permute-start.11) | collective-permute-done | bytes 262176 | tf_op jit(solution)/shard_map/ppermute | solution.py:208
  106.8 0.1 broadcast_select_fusion.1
  106.9 1.1 %pad_maximum_fusion = bf16[512,1024]{1,0:T(8,128)(2,1)} fusion(bf16[512,512]{1,0:T(8,128)(2,1)S(1)} %get-tuple-element.42, bf16[512,512]{1,0:T(8,128)(2,1)S(1)} %get-tuple-element.41), kind=kLoop, calls=%fused_computation | loop fusion | flops 2097152 | bytes 2097152 | tf_op jit(solution)/shard_map/concatenate | solution.py:300
  (6 shorter events, 0.1 us)
Async XLA Ops:
  0.7 1.6 %copy-start.2 = (f32[512,1024]{1,0:T(8,128)S(1)}, f32[512,1024]{1,0:T(8,128)}, u32[]{:S(2)}) copy-start(f32[512,1024]{1,0:T(8,128)} %enc_ref.1) | copy-start | bytes 6291460
  2.3 0.7 copy-start.5
  3.0 30.7 %copy-start.6 = (s32[4]{0:T(128)S(1)}, s32[4]{0:T(128)}, u32[]{:S(2)}) copy-start(s32[4]{0:T(128)} %count_ref) | copy-start | bytes 52
  3.0 30.8 %copy-start.7 = (s32[4,16]{1,0:T(4,128)S(1)}, s32[4,16]{1,0:T(4,128)}, u32[]{:S(2)}) copy-start(s32[4,16]{1,0:T(4,128)} %param.8) | copy-start | bytes 772
  5.7 20.6 %all-to-all-start = ((bf16[32,16,640]{2,1,0:T(8,128)(2,1)}), bf16[32,16,640]{2,1,0:T(8,128)(2,1)S(1)}, u32[]{:S(2)}, u32[]{:S(2)}) async-start(bf16[32,16,640]{2,1,0:T(8,128)(2,1)} %bitcast.6), calls=%async_computation | async-start | bytes 1310720 | tf_op jit(solution)/shard_map/all_to_all | solution.py:239
  13.1 59.0 %collective-permute-start.1 = (bf16[4,16,128,128]{3,2,1,0:T(8,128)(2,1)}, bf16[4,16,128,128]{3,2,1,0:T(8,128)(2,1)}, u32[]{:S(2)}, u32[]{:S(2)}) collective-permute-start(bf16[4,16,128,128]{3,2,1,0:T(8,128)(2,1)} %weight_ref.1), channel_id=1, source_target_pairs={{0,1},{1,0},{2,3},{3,2},{4,7},{5,6},{6,5},{7,4},{8,9},{9,8},{10,11... | collective-permute-start | bytes 6291464 | tf_op jit(solution)/shard_map/ppermute | solution.py:208
  26.5 18.7 %collective-permute-start.5 = (bf16[512,512]{1,0:T(8,128)(2,1)S(1)}, bf16[512,512]{1,0:T(8,128)(2,1)}, u32[]{:S(2)}, u32[]{:S(2)}) collective-permute-start(bf16[512,512]{1,0:T(8,128)(2,1)S(1)} %get-tuple-element.30), channel_id=1, source_target_pairs={{0,1},{1,0},{2,3},{3,2},{4,7},{5,6},{6,5},{7,4},{8,9},{9,8},{10,11... | collective-permute-start | bytes 1572872 | tf_op jit(solution)/shard_map/ppermute | solution.py:208
  28.4 23.3 %all-to-all-start.1 = ((bf16[32,16,512]{2,1,0:T(8,128)(2,1)}), bf16[32,16,512]{2,1,0:T(8,128)(2,1)S(1)}, u32[]{:S(2)}, u32[]{:S(2)}) async-start(bf16[32,16,512]{2,1,0:T(8,128)(2,1)} %bitcast.8), calls=%async_computation.1 | async-start | bytes 1048576 | tf_op jit(solution)/shard_map/all_to_all | solution.py:240
  33.9 21.2 %collective-permute-start = (s32[8,16]{1,0:T(8,128)S(1)}, s32[8,16]{1,0:T(8,128)S(1)}, u32[]{:S(2)}, u32[]{:S(2)}) collective-permute-start(s32[8,16]{1,0:T(8,128)S(1)} %pad_add_fusion), channel_id=1, source_target_pairs={{0,1},{1,0},{2,3},{3,2},{4,7},{5,6},{6,5},{7,4},{8,9},{9,8},{10,11... | collective-permute-start | bytes 1544 | tf_op jit(solution)/shard_map/ppermute | solution.py:208
  45.2 21.1 %collective-permute-start.6 = (bf16[512,512]{1,0:T(8,128)(2,1)}, bf16[512,512]{1,0:T(8,128)(2,1)}, u32[]{:S(2)}, u32[]{:S(2)}) collective-permute-start(bf16[512,512]{1,0:T(8,128)(2,1)} %collective-permute-done.5.row_ref), channel_id=1, source_target_pairs={{0,3},{1,2},{2,1},{3,0},{4,5},{5,4},{6,7},{7,6},{8,11},{9,10},{10,... | collective-permute-start | bytes 1572872 | tf_op jit(solution)/shard_map/ppermute | solution.py:211
  51.7 23.1 %collective-permute-start.7 = (bf16[512,512]{1,0:T(8,128)(2,1)S(1)}, bf16[512,512]{1,0:T(8,128)(2,1)S(1)}, u32[]{:S(2)}, u32[]{:S(2)}) collective-permute-start(bf16[512,512]{1,0:T(8,128)(2,1)S(1)} %bitcast.12), channel_id=1, source_target_pairs={{0,3},{1,2},{2,1},{3,0},{4,5},{5,4},{6,7},{7,6},{8,11},{9,10},{10,... | collective-permute-start | bytes 1572872 | tf_op jit(solution)/shard_map/ppermute | solution.py:211
  52.0 10.6 %collective-permute-start.4 = (f32[8,512]{1,0:T(8,128)S(1)}, f32[8,512]{1,0:T(8,128)S(1)}, u32[]{:S(2)}, u32[]{:S(2)}) collective-permute-start(f32[8,512]{1,0:T(8,128)S(1)} %get-tuple-element.28.own_at), channel_id=1, source_target_pairs={{0,3},{1,2},{2,1},{3,0},{4,5},{5,4},{6,7},{7,6},{8,11},{9,10},{10,... | collective-permute-start | bytes 49160 | tf_op jit(solution)/shard_map/ppermute | solution.py:211
  55.1 7.6 %collective-permute-start.3 = (f32[8,512]{1,0:T(8,128)S(1)}, f32[8,512]{1,0:T(8,128)S(1)}, u32[]{:S(2)}, u32[]{:S(2)}) collective-permute-start(f32[8,512]{1,0:T(8,128)S(1)} %get-tuple-element.28.own_at), channel_id=1, source_target_pairs={{0,2},{1,3},{2,0},{3,1},{4,6},{5,7},{6,4},{7,5},{8,10},{9,11},{10,... | collective-permute-start | bytes 49160 | tf_op jit(solution)/shard_map/ppermute | solution.py:251
  62.5 3.7 %collective-permute-start.2 = (f32[8,512]{1,0:T(8,128)S(1)}, f32[8,512]{1,0:T(8,128)S(1)}, u32[]{:S(2)}, u32[]{:S(2)}) collective-permute-start(f32[8,512]{1,0:T(8,128)S(1)} %get-tuple-element.28.own_at), channel_id=1, source_target_pairs={{0,1},{1,0},{2,3},{3,2},{4,7},{5,6},{6,5},{7,4},{8,9},{9,8},{10,11... | collective-permute-start | bytes 49160 | tf_op jit(solution)/shard_map/ppermute | solution.py:208
  74.8 7.6 %copy-start = (bf16[512,2048]{1,0:T(8,128)(2,1)}, bf16[512,2048]{1,0:T(8,128)(2,1)S(1)}, u32[]{:S(2)}) copy-start(bf16[512,2048]{1,0:T(8,128)(2,1)S(1)} %get-tuple-element.24.dense_b) | copy-start | bytes 6291460
  79.3 7.6 %copy-start.3 = (bf16[1024,256]{1,0:T(8,128)(2,1)}, bf16[1024,256]{1,0:T(8,128)(2,1)S(1)}, u32[]{:S(2)}) copy-start(bf16[1024,256]{1,0:T(8,128)(2,1)S(1)} %get-tuple-element.34.base_ref) | copy-start | bytes 1572868
  79.3 15.9 %collective-permute-start.8 = (bf16[1024,256]{1,0:T(8,128)(2,1)}, bf16[1024,256]{1,0:T(8,128)(2,1)}, u32[]{:S(2)}, u32[]{:S(2)}) collective-permute-start(bf16[1024,256]{1,0:T(8,128)(2,1)} %get-tuple-element.33.hidden_ref), channel_id=1, source_target_pairs={{0,3},{1,2},{2,1},{3,0},{4,5},{5,4},{6,7},{7,6},{8,11},{9,10},{10,... | collective-permute-start | bytes 1572872 | tf_op jit(solution)/shard_map/ppermute | solution.py:211
  86.9 10.7 %collective-permute-start.9 = (bf16[1024,256]{1,0:T(8,128)(2,1)}, bf16[1024,256]{1,0:T(8,128)(2,1)}, u32[]{:S(2)}, u32[]{:S(2)}) collective-permute-start(bf16[1024,256]{1,0:T(8,128)(2,1)} %get-tuple-element.36.hidden_ref), channel_id=1, source_target_pairs={{0,3},{1,2},{2,1},{3,0},{4,5},{5,4},{6,7},{7,6},{8,11},{9,10},{10,... | collective-permute-start | bytes 1572872 | tf_op jit(solution)/shard_map/ppermute | solution.py:211
  89.0 1.6 %copy-start.1 = (bf16[512,2048]{1,0:T(8,128)(2,1)S(1)}, bf16[512,2048]{1,0:T(8,128)(2,1)}, u32[]{:S(2)}) copy-start(bf16[512,2048]{1,0:T(8,128)(2,1)} %copy-done) | copy-start | bytes 6291460
  92.9 2.3 %copy-start.4 = (bf16[1024,256]{1,0:T(8,128)(2,1)S(1)}, bf16[1024,256]{1,0:T(8,128)(2,1)}, u32[]{:S(2)}) copy-start(bf16[1024,256]{1,0:T(8,128)(2,1)} %copy-done.3) | copy-start | bytes 1572868
  97.5 6.5 %collective-permute-start.10 = (bf16[512,256]{1,0:T(8,128)(2,1)S(1)}, bf16[512,256]{1,0:T(8,128)(2,1)S(1)}, u32[]{:S(2)}, u32[]{:S(2)}) collective-permute-start(bf16[512,256]{1,0:T(8,128)(2,1)S(1)} %get-tuple-element.39), channel_id=1, source_target_pairs={{0,1},{1,0},{2,3},{3,2},{4,7},{5,6},{6,5},{7,4},{8,9},{9,8},{10,11... | collective-permute-start | bytes 786440 | tf_op jit(solution)/shard_map/ppermute | solution.py:208
  99.9 6.8 %collective-permute-start.11 = (bf16[512,256]{1,0:T(8,128)(2,1)S(1)}, bf16[512,256]{1,0:T(8,128)(2,1)S(1)}, u32[]{:S(2)}, u32[]{:S(2)}) collective-permute-start(bf16[512,256]{1,0:T(8,128)(2,1)S(1)} %get-tuple-element.40), channel_id=1, source_target_pairs={{0,1},{1,0},{2,3},{3,2},{4,7},{5,6},{6,5},{7,4},{8,9},{9,8},{10,11... | collective-permute-start | bytes 786440 | tf_op jit(solution)/shard_map/ppermute | solution.py:208

commit v2 on v0

v2 whole, which is shorter than its diff:
```python
import functools

import jax
import jax.numpy as jnp
from jax import lax
from jax.experimental import pallas as pl
from jax.experimental.pallas import tpu as pltpu
from jax.sharding import PartitionSpec as P

AXES = ("dom", "grp")
MIX = 0.3
CHUNKS = 2
VMEM = pl.BlockSpec(memory_space=pltpu.VMEM)
SMEM = pl.BlockSpec(memory_space=pltpu.SMEM)
ANY = pl.BlockSpec(memory_space=pl.ANY)


def kernel_call(body, out_shape, in_specs, flops, moved, scratch=(), limit=10):
    outs = out_shape if isinstance(out_shape, (tuple, list)) else (out_shape,)
    specs = tuple(VMEM for _ in outs)
    return pl.pallas_call(
        body,
        out_shape=out_shape,
        in_specs=in_specs,
        out_specs=specs if isinstance(out_shape, (tuple, list)) else specs[0],
        scratch_shapes=scratch,
        compiler_params=pltpu.CompilerParams(vmem_limit_bytes=limit * 1024 * 1024),
        cost_estimate=pl.CostEstimate(flops=flops, bytes_accessed=moved, transcendentals=0),
    )


def half_of(core_is_odd, z):
    return jnp.where(core_is_odd, z // 2, ((z + 1) // 2) % 2)


def sort_kernel(doms, owner_hbm, enc_ref, other_0, other_1, pick_ref, place_ref, enc, owner_ref, sems):
    rows, width = enc_ref.shape
    half = width // 2
    z = lax.axis_index("grp")
    first = pltpu.make_async_copy(owner_hbm, owner_ref, sems.at[2])
    first.start()
    loads = []
    for core in range(2):
        start = pl.multiple_of((1 - half_of(core == 1, z)) * half, half)
        loads.append(pltpu.make_async_copy(enc_ref.at[:, pl.ds(start, half)], enc.at[core], sems.at[core]))
    for load in loads:
        load.start()
    per = rows // doms
    before = (
        lax.broadcasted_iota(jnp.int32, (rows, rows), 0)
        < lax.broadcasted_iota(jnp.int32, (rows, rows), 1)
    ).astype(jnp.bfloat16)
    first.wait()
    owner = owner_ref[...]
    group_nodes = rows * 4
    tdom = owner // group_nodes
    place = owner - tdom * group_nodes
    hot = (lax.broadcasted_iota(jnp.int32, (doms, rows), 0) == tdom).astype(jnp.float32)
    seen = jnp.dot(hot.astype(jnp.bfloat16), before, preferred_element_type=jnp.float32)
    rank = jnp.sum(hot * seen, axis=0, keepdims=True)
    block = (tdom % 2) * (doms // 2) + tdom // 2
    slot = block * per + rank.astype(jnp.int32)
    pick_ref[...] = (lax.broadcasted_iota(jnp.int32, (rows, rows), 0) == slot).astype(jnp.bfloat16)
    line = lax.broadcasted_iota(jnp.int32, (16, rows), 0)
    coded = jnp.where(line == 0, place // 64, jnp.where(line == 1, place % 64, 0))
    places = lax.dot_general(
        coded.astype(jnp.float32).astype(jnp.bfloat16),
        pick_ref[...],
        (((1,), (1,)), ((), ())),
        preferred_element_type=jnp.float32,
    ).astype(jnp.bfloat16)
    place_ref[...] = places
    part = rows // 2
    for core, out in enumerate((other_0, other_1)):
        out[part:, :part] = places[:, core * part : (core + 1) * part]
        out[part:, part:] = jnp.zeros((16, half - part), jnp.bfloat16)
        loads[core].wait()
        out[:part, :] = jnp.dot(
            pick_ref[pl.ds(core * part, part), :],
            enc[core].astype(jnp.bfloat16),
            preferred_element_type=jnp.float32,
        ).astype(jnp.bfloat16)


def mine_kernel(enc_ref, pick_ref, mine_ref, enc, sems):
    rows, width = enc_ref.shape
    half = width // 2
    z = lax.axis_index("grp")
    loads = []
    for core in range(2):
        start = pl.multiple_of(half_of(core == 1, z) * half, half)
        loads.append(pltpu.make_async_copy(enc_ref.at[:, pl.ds(start, half)], enc.at[core], sems.at[core]))
    for load in loads:
        load.start()
    for core in range(2):
        span = pl.ds(core * rows // 2, rows // 2)
        loads[core].wait()
        mine_ref[span, :] = jnp.dot(
            pick_ref[span, :], enc[core].astype(jnp.bfloat16), preferred_element_type=jnp.float32
        ).astype(jnp.bfloat16)


def pack_kernel(mine_ref, place_ref, row_0, row_1, out_ref):
    rows, half = mine_ref.shape
    part = half // CHUNKS
    line = lax.broadcasted_iota(jnp.int32, (16, 128), 0)
    lane = lax.broadcasted_iota(jnp.int32, (16, 128), 1)
    for core, row in enumerate((row_0, row_1)):
        span = pl.ds(core * rows // 2, rows // 2)
        for c in range(CHUNKS):
            cols = pl.ds(c * part, part)
            out_ref[span, 2 * c * part : (2 * c + 1) * part] = mine_ref[span, cols]
            out_ref[span, (2 * c + 1) * part : (2 * c + 2) * part] = row[: rows // 2, cols]
        total = jnp.zeros((rows // 2, 128), jnp.float32)
        for n, lines in enumerate((place_ref[:, span], row[rows // 2 :, : rows // 2])):
            spread = ((lane == line + 2 * n) & (line < 2)).astype(jnp.bfloat16)
            total += lax.dot_general(
                lines, spread, (((0,), (0,)), ((), ())), preferred_element_type=jnp.float32
            )
        out_ref[span, 2 * half :] = total.astype(jnp.bfloat16)


def place_kernel(arrived_ref, *outs):
    rows = arrived_ref.shape[0]
    part = outs[0].shape[1]
    line = lax.broadcasted_iota(jnp.int32, (16, 128), 0)
    lane = lax.broadcasted_iota(jnp.int32, (16, 128), 1)
    spread = ((lane == line) & (line < 4)).astype(jnp.bfloat16)
    outs[0][rows:, :] = lax.dot_general(
        spread, arrived_ref[:, len(outs) * part :], (((1,), (1,)), ((), ())), preferred_element_type=jnp.float32
    ).astype(jnp.bfloat16)
    for c, out in enumerate(outs):
        out[:rows, :] = arrived_ref[:, c * part : (c + 1) * part]


def dense_kernel(list_ref, count_ref, weight_ref, dense_ref, scale_ref, held, sems):
    blocks, _, size, _ = weight_ref.shape
    dom, z = lax.axis_index("dom"), lax.axis_index("grp")
    loads = [pltpu.make_async_copy(weight_ref.at[b], held.at[b], sems.at[b]) for b in range(blocks)]
    for load in loads:
        load.start()
    for b in range(blocks):
        dense_ref[pl.ds(b * size, size), :] = jnp.zeros((size, dense_ref.shape[1]), dense_ref.dtype)
    for b in range(blocks):
        span = pl.ds(b * size, size)
        loads[b].wait()

        def put(k, total):
            block = held[b, k]
            target = list_ref[b, k]
            column = steps_of(dom, z, target // blocks) * blocks + target % blocks
            start = pl.multiple_of(column * size, size)
            dense_ref[span, pl.ds(start, size)] = block
            return total + block.astype(jnp.float32)

        total = lax.fori_loop(0, count_ref[b], put, jnp.zeros((size, size), jnp.float32))
        degree = jnp.sum(total, axis=1, keepdims=True)
        scale_ref[span, :] = jnp.broadcast_to((1.0 - MIX) * lax.rsqrt(degree), (size, 128))


def steps_of(dom, z, q):
    odd = dom % 2 == 1
    rx, fx = jnp.where(odd, 3, 1), jnp.where(odd, 1, 3)
    step = q ^ z
    return jnp.where(step == 0, 0, jnp.where(step == rx, 1, jnp.where(step == fx, 2, 3)))


def pick_kernel(order, rows_ref, pick_ref):
    nodes, size = pick_ref.shape[1:]
    dom, z = lax.axis_index("dom"), lax.axis_index("grp")
    coded = rows_ref[pl.ds(size, 16), :].astype(jnp.float32).astype(jnp.int32)
    for k, n in enumerate(order):
        p = coded[2 * n : 2 * n + 1, :] * 64 + coded[2 * n + 1 : 2 * n + 2, :]
        spot = steps_of(dom, z, p // size) * size + p % size
        for n in range(nodes // size):
            node = lax.broadcasted_iota(jnp.int32, (size, size), 0) + n * size
            pick_ref[k, pl.ds(n * size, size), :] = (node == spot).astype(jnp.bfloat16)


def part_kernel(pick_ref, near_ref, part_ref):
    size, width = pick_ref.shape[2], part_ref.shape[1]
    for n in range(part_ref.shape[0] // size):
        at = pl.ds(n * size, size)
        total = jnp.dot(pick_ref[0, at, :], near_ref[:size, :width], preferred_element_type=jnp.float32)
        total += jnp.dot(pick_ref[1, at, :], near_ref[:size, width:], preferred_element_type=jnp.float32)
        part_ref[at, :] = total.astype(jnp.bfloat16)


def first_kernel(dense_a, dense_b, scale_a, scale_b, pick_ref, part_ref, far_ref, base_ref, hidden_ref, panel):
    size = dense_a.shape[0]
    width = part_ref.shape[1]
    for n in range(panel.shape[0] // size):
        at = pl.ds(n * size, size)
        total = jnp.dot(pick_ref[0, at, :], far_ref[:size, :width], preferred_element_type=jnp.float32)
        total += jnp.dot(pick_ref[1, at, :], far_ref[:size, width:], preferred_element_type=jnp.float32)
        panel[at, :] = part_ref[at, :] + total.astype(jnp.bfloat16)
    for n, (dense, scale) in enumerate(((dense_a, scale_a), (dense_b, scale_b))):
        at = pl.ds(n * size, size)
        total = jnp.dot(dense[...], panel[...], preferred_element_type=jnp.float32)
        base = panel[at, :]
        base_ref[at, :] = base
        hidden_ref[at, :] = (MIX * base.astype(jnp.float32) + total * scale[:, 0:1]).astype(jnp.bfloat16)


def half_kernel(dense_a, dense_b, hidden_ref, total_ref):
    size = dense_a.shape[0]
    depth = hidden_ref.shape[0]
    for n, dense in enumerate((dense_a, dense_b)):
        total_ref[pl.ds(n * size, size), :] = jnp.dot(
            dense[:, :depth], hidden_ref[...], preferred_element_type=jnp.float32
        )


def last_kernel(dense_a, dense_b, scale_a, scale_b, total_ref, hidden_ref, base_ref, keep_ref, send_ref):
    size = dense_a.shape[0]
    depth = hidden_ref.shape[0]
    for n, (dense, scale, out) in enumerate(((dense_a, scale_a, keep_ref), (dense_b, scale_b, send_ref))):
        at = pl.ds(n * size, size)
        total = total_ref[at, :] + jnp.dot(dense[:, depth:], hidden_ref[...], preferred_element_type=jnp.float32)
        out[...] = (MIX * base_ref[at, :].astype(jnp.float32) + total * scale[:, 0:1]).astype(jnp.bfloat16)


def join_kernel(keep_0, keep_1, got_0, got_1, out_ref, sems):
    part = keep_0.shape[1]
    dom, z = lax.axis_index("dom"), lax.axis_index("grp")
    upper = half_of(dom % 2 == 1, z)
    copies = []
    for n, piece in enumerate((keep_0, keep_1, got_0, got_1)):
        start = (upper if n < 2 else 1 - upper) * 2 * part + (n % 2) * part
        copies.append(
            pltpu.make_async_copy(piece, out_ref.at[:, pl.ds(pl.multiple_of(start, part), part)], sems.at[n])
        )
    for copy in copies:
        copy.start()
    for copy in copies:
        copy.wait()


def row_step(core):
    return 1 if core == 0 else 3


def shards(doms, depth, encoded, owner_of, nbr_blocks, nbr_count, edge_weights):
    f32, bf16, i32 = jnp.float32, jnp.bfloat16, jnp.int32
    rows, width = encoded.shape
    half = width // 2
    blocks, slots, size, _ = edge_weights.shape
    nodes = rows * depth
    part = half // CHUNKS
    devices = [(d, q) for d in range(doms) for q in range(depth)]
    row_pairs = [(d * depth + q, d * depth + (q ^ row_step(d % 2))) for d, q in devices]
    col_pairs = [(d * depth + q, d * depth + (q ^ row_step(1 - d % 2))) for d, q in devices]
    core_major = [[d for core in range(2) for d in range(core, doms, 2)]]

    def to_row(a):
        return lax.ppermute(a, AXES, row_pairs)

    def to_col(a):
        return lax.ppermute(a, AXES, col_pairs)

    def to_row_of(core, a):
        return lax.ppermute(a, AXES, [(d * depth + q, d * depth + (q ^ row_step(core))) for d, q in devices])

    far_blocks, far_count = to_row(nbr_blocks), to_row(nbr_count)

    def dense_of(lists, count, weights, limit):
        return kernel_call(
            dense_kernel,
            (jax.ShapeDtypeStruct((blocks * size, nodes), bf16), jax.ShapeDtypeStruct((blocks * size, 128), f32)),
            [SMEM, SMEM, ANY],
            0,
            8 << 20,
            scratch=[pltpu.VMEM(weights.shape, bf16), pltpu.SemaphoreType.DMA((blocks,))],
            limit=limit,
        )(lists, count, weights)

    held = pltpu.VMEM((2, rows, half), f32)
    other = jax.ShapeDtypeStruct((rows // 2 + 16, half), bf16)
    other_0, other_1, pick, place = kernel_call(
        functools.partial(sort_kernel, doms),
        (other, other, jax.ShapeDtypeStruct((rows, rows), bf16), jax.ShapeDtypeStruct((16, rows), bf16)),
        [ANY, ANY],
        2 * rows * rows * half,
        4 << 20,
        scratch=[held, pltpu.VMEM((1, rows), i32), pltpu.SemaphoreType.DMA((3,))],
        limit=58,
    )(owner_of.reshape(1, rows), encoded)
    row_0, row_1 = to_row_of(0, other_0), to_row_of(1, other_1)
    mine = kernel_call(
        mine_kernel,
        jax.ShapeDtypeStruct((rows, half), bf16),
        [ANY, VMEM],
        2 * rows * rows * half,
        4 << 20,
        scratch=[held, pltpu.SemaphoreType.DMA((2,))],
        limit=50,
    )(encoded, pick)
    sent_weights, row_0, row_1, far_blocks, far_count = lax.optimization_barrier(
        (edge_weights, row_0, row_1, far_blocks, far_count)
    )
    far_weights = to_row(sent_weights)
    packed = kernel_call(
        pack_kernel,
        jax.ShapeDtypeStruct((rows, width + 128), bf16),
        [VMEM] * 4,
        1 << 20,
        2 << 20,
    )(mine, place, row_0, row_1)

    packed = lax.all_to_all(packed, "dom", 0, 0, axis_index_groups=core_major, tiled=True)
    near_rows = kernel_call(
        place_kernel,
        tuple(jax.ShapeDtypeStruct((rows + (16 if c == 0 else 0), 2 * part), bf16) for c in range(CHUNKS)),
        [VMEM],
        1 << 20,
        1 << 20,
    )(packed)
    far_rows = [to_col(a) for a in near_rows]

    dense_a, scale_a = dense_of(nbr_blocks, nbr_count, edge_weights, 50)
    dense_b, scale_b = dense_of(far_blocks, far_count, far_weights, 10)

    def picks_of(order, first_rows):
        return kernel_call(
            functools.partial(pick_kernel, order),
            jax.ShapeDtypeStruct((2, nodes, rows), bf16),
            [VMEM],
            1 << 20,
            4 << 20,
        )(first_rows)

    near_picks, far_picks = picks_of((0, 1), near_rows[0]), picks_of((0, 1), far_rows[0])

    mine_n = 2 * rows
    kept, sent = [], []
    for c in range(CHUNKS):
        placed = kernel_call(
            part_kernel,
            jax.ShapeDtypeStruct((nodes, part), bf16),
            [VMEM] * 2,
            4 * nodes * rows * part,
            4 << 20,
        )(near_picks, near_rows[c])
        base, hidden = kernel_call(
            first_kernel,
            (jax.ShapeDtypeStruct((mine_n, part), bf16), jax.ShapeDtypeStruct((mine_n, part), bf16)),
            [VMEM] * 7,
            4 * nodes * rows * part + 2 * mine_n * nodes * part,
            4 << 20,
            scratch=[pltpu.VMEM((nodes, part), bf16)],
        )(dense_a, dense_b, scale_a, scale_b, far_picks, placed, far_rows[c])
        far_hidden = to_col(hidden)
        running = kernel_call(
            half_kernel,
            jax.ShapeDtypeStruct((mine_n, part), f32),
            [VMEM] * 3,
            2 * mine_n * mine_n * part,
            4 << 20,
        )(dense_a, dense_b, hidden)
        keep, send = kernel_call(
            last_kernel,
            (jax.ShapeDtypeStruct((rows, part), bf16), jax.ShapeDtypeStruct((rows, part), bf16)),
            [VMEM] * 7,
            2 * mine_n * mine_n * part,
            4 << 20,
        )(dense_a, dense_b, scale_a, scale_b, running, far_hidden, base)
        kept.append(keep)
        sent.append(to_row(send))
    return pl.pallas_call(
        join_kernel,
        out_shape=jax.ShapeDtypeStruct((rows, width), bf16),
        in_specs=[VMEM] * 4,
        out_specs=ANY,
        scratch_shapes=[pltpu.SemaphoreType.DMA((4,))],
        compiler_params=pltpu.CompilerParams(vmem_limit_bytes=8 << 20),
    )(*kept, *sent)


def solution(mesh):
    return jax.shard_map(
        functools.partial(shards, mesh.shape["dom"], mesh.shape["grp"]),
        mesh=mesh,
        in_specs=(P(AXES, None), P(AXES), P(AXES, None), P(AXES), P(AXES, None, None, None)),
        out_specs=P(AXES, None),
        check_vma=False,
    )
```

time: 180 us -> 88.9 us (0.49)
  waiting for transfers between devices: 111 us -> 25 us
  blocking collectives: 0 us -> 26.2 us
  matrix products: 24.5 us -> 0 us
  Pallas kernels: 0 us -> 21.6 us
  between operations: 13.5 us -> 0.31 us
  local copies, waits for them, and re-layouts: 7.3 us -> 1.06 us
  other arithmetic: 5.51 us -> 0 us
  starting transfers between devices: 16.9 us -> 14.2 us
    all_gather x2 -> x0, waiting for transfers between devices: 89.6 us -> none  [group_panel(): return lax.all_gather(hidden, 'grp', axis=0, tiled=True)]
    all_to_all x0 -> x1, blocking collectives: none -> 26.2 us  [shards(): lax.all_to_all(packed, 'dom', 0, 0, axis_index_groups=core_major, tiled=T...]
    ppermute x0 -> x11, waiting for transfers between devices: none -> 25 us  [the longest x4 13.6 us: to_col(): return lax.ppermute(a, AXES, col_pairs)]
    dot_general x5 -> x0, matrix products: 24.5 us -> none  [the longest x2 13.6 us: propagate(): running = jnp.dot(dense, panel_rows, preferred_element_type=jnp.float32)]
    pallas_call x0 -> x17, Pallas kernels: none -> 21.6 us  [the longest x2 4.68 us: shards(): kernel_call(first_kernel, (jax.ShapeDtypeStruct((mine_n, part), bf16), ja...]
    all_to_all x2 -> x0, waiting for transfers between devices: 21.5 us -> none  [the longest x1 17.2 us: shards(): lax.all_to_all(outgoing.astype(jnp.bfloat16), ('dom', 'grp'), split_axis=...]
    all_to_all x2 -> x0, starting transfers between devices: 16.6 us -> none  [the longest x1 11.1 us: shards(): lax.all_to_all(places, ('dom', 'grp'), split_axis=0, concat_axis=0, tiled...]
    ppermute x0 -> x11, starting transfers between devices: none -> 14.2 us  [the longest x4 6.82 us: to_col(): return lax.ppermute(a, AXES, col_pairs)]
  transfers between devices with their start and end apart: 4 -> 11, of which waited for: 4 -> 6; matrix products, arithmetic and copies ran while one was open for 5% -> 0% of each run, Pallas kernels for 0% -> 20%
where the time goes in v2:
time: 88.9 us; the launch traced here: 88.4 us
  blocking collectives  26.2 us (29%)
  waiting for transfers between devices  25 us (28%)
  Pallas kernels  21.6 us (24%)
  starting transfers between devices  14.2 us (16%)
  local copies, waits for them, and re-layouts  1.06 us (1%)
    all_to_all x1, blocking collectives, shards(): lax.all_to_all(packed, 'dom', 0, 0, axis_index_groups=core_major, tiled=T...  26.2 us
    ppermute x4, waiting for transfers between devices, to_col(): return lax.ppermute(a, AXES, col_pairs)  13.6 us
    ppermute x5, waiting for transfers between devices, to_row(): return lax.ppermute(a, AXES, row_pairs)  8.89 us
    ppermute x4, starting transfers between devices, to_col(): return lax.ppermute(a, AXES, col_pairs)  6.82 us
    pallas_call x2, Pallas kernels, shards(): kernel_call(first_kernel, (jax.ShapeDtypeStruct((mine_n, part), bf16), ja...  4.68 us
    ppermute x2, starting transfers between devices, to_row_of(): lax.ppermute(a, AXES, [(d * depth + q, d * depth + (q ^ row_step(core)))...  4.61 us
    pallas_call x2, Pallas kernels, dense_of(): kernel_call(dense_kernel, (jax.ShapeDtypeStruct((blocks * size, nodes), b...  4.49 us
    pallas_call x1, Pallas kernels, shards(): kernel_call(functools.partial(sort_kernel, doms), (other, other, jax.Shap...  2.94 us
  transfers between devices with their start and end apart: 11, of which 6 were waited for; matrix products, arithmetic and copies ran while one was open for 0% of the time, Pallas kernels for 20%

profile of v2, /device:TPU:0, one launch (start us, length us, event | category | flops | bytes accessed | tf_op | source)
XLA Modules:
  0.0 88.4 jit_solution(5625267640257370759)
XLA Ops:
  0.0 0.0 copy-start
  0.0 0.0 copy-start.3
  0.0 0.0 copy-start.4
  0.0 2.9 %shard_map.56 = (bf16[272,512]{1,0:T(8,128)(2,1)}, bf16[272,512]{1,0:T(8,128)(2,1)}, bf16[512,512]{1,0:T(8,128)(2,1)}, bf16[16,512]{1,0:T(8,128)(2,1)}) custom-call(s32[1,512]{1,0:T(1,128)} %bitcast.5, f32[512,1024]{1,0:T(8,128)} %enc_ref.3), custom_call_target="tpu_custom_call" | custom-call | flops 268435456 | bytes 4194304 | tf_op jit(solution)/shard_map/pallas_call | solution.py:279
  3.0 2.1 %collective-permute-start = (bf16[272,512]{1,0:T(8,128)(2,1)}, bf16[272,512]{1,0:T(8,128)(2,1)S(1)}, u32[]{:S(2)}, u32[]{:S(2)}) collective-permute-start(bf16[272,512]{1,0:T(8,128)(2,1)} %get-tuple-element.29), channel_id=1, source_target_pairs={{0,1},{1,0},{2,3},{3,2},{4,5},{5,4},{6,7},{7,6},{8,9},{9,8},{10,11... | collective-permute-start | bytes 835592 | tf_op jit(solution)/shard_map/ppermute | solution.py:262
  5.0 2.5 %collective-permute-start.1 = (bf16[272,512]{1,0:T(8,128)(2,1)}, bf16[272,512]{1,0:T(8,128)(2,1)S(1)}, u32[]{:S(2)}, u32[]{:S(2)}) collective-permute-start(bf16[272,512]{1,0:T(8,128)(2,1)} %get-tuple-element.30), channel_id=1, source_target_pairs={{0,3},{1,2},{2,1},{3,0},{4,7},{5,6},{6,5},{7,4},{8,11},{9,10},{10,... | collective-permute-start | bytes 835592 | tf_op jit(solution)/shard_map/ppermute | solution.py:262
  7.6 0.0 copy-done.3
  7.6 1.0 %collective-permute-start.2 = (s32[4,16]{1,0:T(4,128)S(1)}, s32[4,16]{1,0:T(4,128)S(1)}, u32[]{:S(2)}, u32[]{:S(2)}) collective-permute-start(s32[4,16]{1,0:T(4,128)S(1)} %copy-done.3), channel_id=1, source_target_pairs={{0,1},{1,0},{2,3},{3,2},{4,7},{5,6},{6,5},{7,4},{8,9},{9,8},{10,11... | collective-permute-start | bytes 776 | tf_op jit(solution)/shard_map/ppermute | solution.py:256
  8.6 0.0 copy-done.4
  8.6 1.0 %collective-permute-start.3 = (s32[4]{0:T(128)S(1)}, s32[4]{0:T(128)S(1)}, u32[]{:S(2)}, u32[]{:S(2)}) collective-permute-start(s32[4]{0:T(128)S(1)} %copy-done.4), channel_id=1, source_target_pairs={{0,1},{1,0},{2,3},{3,2},{4,7},{5,6},{6,5},{7,4},{8,9},{9,8},{10,11... | collective-permute-start | bytes 56 | tf_op jit(solution)/shard_map/ppermute | solution.py:256
  9.6 2.5 %collective-permute-done.3.count_ref = s32[4]{0:T(128)S(1)} collective-permute-done((s32[4]{0:T(128)S(1)}, s32[4]{0:T(128)S(1)}, u32[]{:S(2)}, u32[]{:S(2)}) %collective-permute-start.3) | collective-permute-done | bytes 48 | tf_op jit(solution)/shard_map/ppermute | solution.py:256
  12.1 0.0 collective-permute-done.2.list_ref
  12.1 0.0 collective-permute-done.row_0
  12.1 2.5 %collective-permute-done.1.row_1 = bf16[272,512]{1,0:T(8,128)(2,1)S(1)} collective-permute-done((bf16[272,512]{1,0:T(8,128)(2,1)}, bf16[272,512]{1,0:T(8,128)(2,1)S(1)}, u32[]{:S(2)}, u32[]{:S(2)}) %collective-permute-start.1) | collective-permute-done | bytes 278560 | tf_op jit(solution)/shard_map/ppermute | solution.py:262
  14.6 0.6 collective-permute-start.4
  15.2 0.0 copy-done
  15.2 0.0 copy-start.1
  15.2 1.0 %copy-done.1 = bf16[512,512]{1,0:T(8,128)(2,1)S(1)} copy-done((bf16[512,512]{1,0:T(8,128)(2,1)S(1)}, bf16[512,512]{1,0:T(8,128)(2,1)}, u32[]{:S(2)}) %copy-start.1) | copy-done | bytes 524312
  16.2 0.0 copy-start.2
  16.2 1.0 %shard_map.58.mine_ref = bf16[512,512]{1,0:T(8,128)(2,1)S(1)} custom-call(f32[512,1024]{1,0:T(8,128)S(1)} %copy-done, bf16[512,512]{1,0:T(8,128)(2,1)S(1)} %copy-done.1), custom_call_target="tpu_custom_call" | custom-call | flops 268435456 | bytes 4194304 | tf_op jit(solution)/shard_map/pallas_call | solution.py:289
  17.3 0.0 copy-done.2
  17.3 0.3 shard_map.59
  17.6 26.2 %all_to_all.11 = bf16[32,16,1152]{2,1,0:T(8,128)(2,1)S(1)} all-to-all(bf16[32,16,1152]{2,1,0:T(8,128)(2,1)S(1)} %bitcast.3), channel_id=1, replica_groups={{0,8,16,24,32,40,48,56,64,72,80,88,96,104,112,120,4,12,20,28,36,44,52,6..., dimensions={0} | all-to-all | bytes 2359296 | tf_op jit(solution)/shard_map/all_to_all | solution.py:310
  43.8 0.2 shard_map.60
  43.9 2.3 %collective-permute-start.5 = (bf16[528,512]{1,0:T(8,128)(2,1)S(1)}, bf16[528,512]{1,0:T(8,128)(2,1)S(1)}, u32[]{:S(2)}, u32[]{:S(2)}) collective-permute-start(bf16[528,512]{1,0:T(8,128)(2,1)S(1)} %get-tuple-element.41.rows_ref.near_ref), channel_id=1, source_target_pairs={{0,3},{1,2},{2,1},{3,0},{4,5},{5,4},{6,7},{7,6},{8,11},{9,10},{10,... | collective-permute-start | bytes 1622024 | tf_op jit(solution)/shard_map/ppermute | solution.py:259
  46.2 0.9 %collective-permute-start.7 = (bf16[512,512]{1,0:T(8,128)(2,1)S(1)}, bf16[512,512]{1,0:T(8,128)(2,1)S(1)}, u32[]{:S(2)}, u32[]{:S(2)}) collective-permute-start(bf16[512,512]{1,0:T(8,128)(2,1)S(1)} %get-tuple-element.45.near_ref), channel_id=1, source_target_pairs={{0,3},{1,2},{2,1},{3,0},{4,5},{5,4},{6,7},{7,6},{8,11},{9,10},{10,... | collective-permute-start | bytes 1572872 | tf_op jit(solution)/shard_map/ppermute | solution.py:259
  47.2 2.7 %shard_map.55 = (bf16[512,2048]{1,0:T(8,128)(2,1)S(1)}, f32[512,128]{1,0:T(8,128)S(1)}) custom-call(s32[4,16]{1,0:T(4,128)S(1)} %copy-done.3, s32[4]{0:T(128)S(1)} %copy-done.4, bf16[4,16,128,128]{3,2,1,0:T(8,128)(2,1)} %weight_ref.1), custom_call_target="tpu_custom_call" | custom-call | bytes 8388608 | tf_op jit(solution)/shard_map/pallas_call | solution.py:267
  49.8 0.8 shard_map.62.pick_ref
  50.6 1.2 %shard_map.63.part_ref = bf16[2048,256]{1,0:T(8,128)(2,1)S(1)} custom-call(bf16[2,2048,512]{2,1,0:T(8,128)(2,1)S(1)} %shard_map.62.pick_ref, bf16[528,512]{1,0:T(8,128)(2,1)S(1)} %get-tuple-element.41.rows_ref.near_ref), custom_call_target="tpu_custom_call" | custom-call | flops 1073741824 | bytes 4194304 | tf_op jit(solution)/shard_map/pallas_call | solution.py:337
  51.9 1.2 %shard_map.67.part_ref = bf16[2048,256]{1,0:T(8,128)(2,1)S(1)} custom-call(bf16[2,2048,512]{2,1,0:T(8,128)(2,1)S(1)} %shard_map.62.pick_ref, bf16[512,512]{1,0:T(8,128)(2,1)S(1)} %get-tuple-element.45.near_ref), custom_call_target="tpu_custom_call" | custom-call | flops 1073741824 | bytes 4194304 | tf_op jit(solution)/shard_map/pallas_call | solution.py:337
  53.2 1.3 %collective-permute-done.5.rows_ref.far_ref = bf16[528,512]{1,0:T(8,128)(2,1)S(1)} collective-permute-done((bf16[528,512]{1,0:T(8,128)(2,1)S(1)}, bf16[528,512]{1,0:T(8,128)(2,1)S(1)}, u32[]{:S(2)}, u32[]{:S(2)}) %collective-permute-start.5) | collective-permute-done | bytes 540704 | tf_op jit(solution)/shard_map/ppermute | solution.py:259
  54.5 0.8 shard_map.61.pick_ref
  55.3 0.0 collective-permute-done.4.weight_ref
  55.3 1.8 %shard_map.57 = (bf16[512,2048]{1,0:T(8,128)(2,1)S(1)}, f32[512,128]{1,0:T(8,128)S(1)}) custom-call(s32[4,16]{1,0:T(4,128)S(1)} %collective-permute-done.2.list_ref, s32[4]{0:T(128)S(1)} %collective-permute-done.3.count_ref, bf16[4,16,128,128]{3,2,1,0:T(8,128)(2,1)S(1)} %collective-permute-done.4.weight_ref), custom_call_target="tpu_custom_call" | custom-call | bytes 8388608 | tf_op jit(solution)/shard_map/pallas_call | solution.py:267
  57.2 2.3 %shard_map.64 = (bf16[1024,256]{1,0:T(8,128)(2,1)S(1)}, bf16[1024,256]{1,0:T(8,128)(2,1)S(1)}) custom-call(bf16[512,2048]{1,0:T(8,128)(2,1)S(1)} %get-tuple-element.28.dense_a, bf16[512,2048]{1,0:T(8,128)(2,1)S(1)} %get-tuple-element.34.dense_b, f32[512,128]{1,0:T(8,128)S(1)} %get-tuple-element.35.scale_a, f32[512,128]{1,0:T(8,128)S(1)} %get-tuple-element.36.scale_b, ...), custom_call_target="tpu_custom_call" | custom-call | flops 2147483648 | bytes 4194304 | tf_op jit(solution)/shard_map/pallas_call | solution.py:344
  59.5 2.4 %collective-permute-start.6 = (bf16[1024,256]{1,0:T(8,128)(2,1)S(1)}, bf16[1024,256]{1,0:T(8,128)(2,1)S(1)}, u32[]{:S(2)}, u32[]{:S(2)}) collective-permute-start(bf16[1024,256]{1,0:T(8,128)(2,1)S(1)} %get-tuple-element.42.hidden_ref), channel_id=1, source_target_pairs={{0,3},{1,2},{2,1},{3,0},{4,5},{5,4},{6,7},{7,6},{8,11},{9,10},{10,... | collective-permute-start | bytes 1572872 | tf_op jit(solution)/shard_map/ppermute | solution.py:259
  61.9 0.0 collective-permute-done.7.far_ref
  61.9 2.3 %shard_map.68 = (bf16[1024,256]{1,0:T(8,128)(2,1)S(1)}, bf16[1024,256]{1,0:T(8,128)(2,1)S(1)}) custom-call(bf16[512,2048]{1,0:T(8,128)(2,1)S(1)} %get-tuple-element.28.dense_a, bf16[512,2048]{1,0:T(8,128)(2,1)S(1)} %get-tuple-element.34.dense_b, f32[512,128]{1,0:T(8,128)S(1)} %get-tuple-element.35.scale_a, f32[512,128]{1,0:T(8,128)S(1)} %get-tuple-element.36.scale_b, ...), custom_call_target="tpu_custom_call" | custom-call | flops 2147483648 | bytes 4194304 | tf_op jit(solution)/shard_map/pallas_call | solution.py:344
  64.3 1.2 %collective-permute-start.8 = (bf16[1024,256]{1,0:T(8,128)(2,1)S(1)}, bf16[1024,256]{1,0:T(8,128)(2,1)S(1)}, u32[]{:S(2)}, u32[]{:S(2)}) collective-permute-start(bf16[1024,256]{1,0:T(8,128)(2,1)S(1)} %get-tuple-element.46.hidden_ref), channel_id=1, source_target_pairs={{0,3},{1,2},{2,1},{3,0},{4,5},{5,4},{6,7},{7,6},{8,11},{9,10},{10,... | collective-permute-start | bytes 1572872 | tf_op jit(solution)/shard_map/ppermute | solution.py:259
  65.4 0.7 shard_map.65.total_ref
  66.2 0.7 shard_map.69.total_ref
  66.9 3.1 %collective-permute-done.6.hidden_ref = bf16[1024,256]{1,0:T(8,128)(2,1)S(1)} collective-permute-done((bf16[1024,256]{1,0:T(8,128)(2,1)S(1)}, bf16[1024,256]{1,0:T(8,128)(2,1)S(1)}, u32[]{:S(2)}, u32[]{:S(2)}) %collective-permute-start.6) | collective-permute-done | bytes 524320 | tf_op jit(solution)/shard_map/ppermute | solution.py:259
  70.0 0.7 shard_map.66
  70.7 0.1 collective-permute-start.9
  70.8 9.2 %collective-permute-done.8.hidden_ref = bf16[1024,256]{1,0:T(8,128)(2,1)S(1)} collective-permute-done((bf16[1024,256]{1,0:T(8,128)(2,1)S(1)}, bf16[1024,256]{1,0:T(8,128)(2,1)S(1)}, u32[]{:S(2)}, u32[]{:S(2)}) %collective-permute-start.8) | collective-permute-done | bytes 524320 | tf_op jit(solution)/shard_map/ppermute | solution.py:259
  80.0 0.7 shard_map.70
  80.7 0.1 collective-permute-start.10
  80.8 0.0 collective-permute-done.9.got_0
  80.9 6.3 %collective-permute-done.10.got_1 = bf16[512,256]{1,0:T(8,128)(2,1)S(1)} collective-permute-done((bf16[512,256]{1,0:T(8,128)(2,1)S(1)}, bf16[512,256]{1,0:T(8,128)(2,1)S(1)}, u32[]{:S(2)}, u32[]{:S(2)}) %collective-permute-start.10) | collective-permute-done | bytes 262176 | tf_op jit(solution)/shard_map/ppermute | solution.py:256
  87.2 1.0 %shard_map.71 = bf16[512,1024]{1,0:T(8,128)(2,1)} custom-call(bf16[512,256]{1,0:T(8,128)(2,1)S(1)} %get-tuple-element.44.keep_0, bf16[512,256]{1,0:T(8,128)(2,1)S(1)} %get-tuple-element.48.keep_1, bf16[512,256]{1,0:T(8,128)(2,1)S(1)} %collective-permute-done.9.got_0, bf16[512,256]{1,0:T(8,128)(2,1)S(1)} %collective-permute-done.10.got_1), custom_call_target="tpu_custom_call" | custom-call | tf_op jit(solution)/shard_map/pallas_call | solution.py:369
Async XLA Ops:
  0.0 15.2 %copy-start = (f32[512,1024]{1,0:T(8,128)S(1)}, f32[512,1024]{1,0:T(8,128)}, u32[]{:S(2)}) copy-start(f32[512,1024]{1,0:T(8,128)} %enc_ref.3) | copy-start | bytes 6291460
  0.0 7.6 %copy-start.3 = (s32[4,16]{1,0:T(4,128)S(1)}, s32[4,16]{1,0:T(4,128)}, u32[]{:S(2)}) copy-start(s32[4,16]{1,0:T(4,128)} %list_ref.1) | copy-start | bytes 772
  0.0 8.6 %copy-start.4 = (s32[4]{0:T(128)S(1)}, s32[4]{0:T(128)}, u32[]{:S(2)}) copy-start(s32[4]{0:T(128)} %count_ref.1) | copy-start | bytes 52
  3.0 9.2 %collective-permute-start = (bf16[272,512]{1,0:T(8,128)(2,1)}, bf16[272,512]{1,0:T(8,128)(2,1)S(1)}, u32[]{:S(2)}, u32[]{:S(2)}) collective-permute-start(bf16[272,512]{1,0:T(8,128)(2,1)} %get-tuple-element.29), channel_id=1, source_target_pairs={{0,1},{1,0},{2,3},{3,2},{4,5},{5,4},{6,7},{7,6},{8,9},{9,8},{10,11... | collective-permute-start | bytes 835592 | tf_op jit(solution)/shard_map/ppermute | solution.py:262
  5.0 9.6 %collective-permute-start.1 = (bf16[272,512]{1,0:T(8,128)(2,1)}, bf16[272,512]{1,0:T(8,128)(2,1)S(1)}, u32[]{:S(2)}, u32[]{:S(2)}) collective-permute-start(bf16[272,512]{1,0:T(8,128)(2,1)} %get-tuple-element.30), channel_id=1, source_target_pairs={{0,3},{1,2},{2,1},{3,0},{4,7},{5,6},{6,5},{7,4},{8,11},{9,10},{10,... | collective-permute-start | bytes 835592 | tf_op jit(solution)/shard_map/ppermute | solution.py:262
  7.6 4.6 %collective-permute-start.2 = (s32[4,16]{1,0:T(4,128)S(1)}, s32[4,16]{1,0:T(4,128)S(1)}, u32[]{:S(2)}, u32[]{:S(2)}) collective-permute-start(s32[4,16]{1,0:T(4,128)S(1)} %copy-done.3), channel_id=1, source_target_pairs={{0,1},{1,0},{2,3},{3,2},{4,7},{5,6},{6,5},{7,4},{8,9},{9,8},{10,11... | collective-permute-start | bytes 776 | tf_op jit(solution)/shard_map/ppermute | solution.py:256
  8.6 3.5 %collective-permute-start.3 = (s32[4]{0:T(128)S(1)}, s32[4]{0:T(128)S(1)}, u32[]{:S(2)}, u32[]{:S(2)}) collective-permute-start(s32[4]{0:T(128)S(1)} %copy-done.4), channel_id=1, source_target_pairs={{0,1},{1,0},{2,3},{3,2},{4,7},{5,6},{6,5},{7,4},{8,9},{9,8},{10,11... | collective-permute-start | bytes 56 | tf_op jit(solution)/shard_map/ppermute | solution.py:256
  14.6 40.7 %collective-permute-start.4 = (bf16[4,16,128,128]{3,2,1,0:T(8,128)(2,1)}, bf16[4,16,128,128]{3,2,1,0:T(8,128)(2,1)S(1)}, u32[]{:S(2)}, u32[]{:S(2)}) collective-permute-start(bf16[4,16,128,128]{3,2,1,0:T(8,128)(2,1)} %weight_ref.1), channel_id=1, source_target_pairs={{0,1},{1,0},{2,3},{3,2},{4,7},{5,6},{6,5},{7,4},{8,9},{9,8},{10,11... | collective-permute-start | bytes 6291464 | tf_op jit(solution)/shard_map/ppermute | solution.py:256
  15.2 1.0 %copy-start.1 = (bf16[512,512]{1,0:T(8,128)(2,1)S(1)}, bf16[512,512]{1,0:T(8,128)(2,1)}, u32[]{:S(2)}) copy-start(bf16[512,512]{1,0:T(8,128)(2,1)} %get-tuple-element.37.pick_ref) | copy-start | bytes 1572868
  16.2 1.0 %copy-start.2 = (bf16[16,512]{1,0:T(8,128)(2,1)S(1)}, bf16[16,512]{1,0:T(8,128)(2,1)}, u32[]{:S(2)}) copy-start(bf16[16,512]{1,0:T(8,128)(2,1)} %get-tuple-element.38.place_ref) | copy-start | bytes 49156
  43.9 10.6 %collective-permute-start.5 = (bf16[528,512]{1,0:T(8,128)(2,1)S(1)}, bf16[528,512]{1,0:T(8,128)(2,1)S(1)}, u32[]{:S(2)}, u32[]{:S(2)}) collective-permute-start(bf16[528,512]{1,0:T(8,128)(2,1)S(1)} %get-tuple-element.41.rows_ref.near_ref), channel_id=1, source_target_pairs={{0,3},{1,2},{2,1},{3,0},{4,5},{5,4},{6,7},{7,6},{8,11},{9,10},{10,... | collective-permute-start | bytes 1622024 | tf_op jit(solution)/shard_map/ppermute | solution.py:259
  46.2 15.7 %collective-permute-start.7 = (bf16[512,512]{1,0:T(8,128)(2,1)S(1)}, bf16[512,512]{1,0:T(8,128)(2,1)S(1)}, u32[]{:S(2)}, u32[]{:S(2)}) collective-permute-start(bf16[512,512]{1,0:T(8,128)(2,1)S(1)} %get-tuple-element.45.near_ref), channel_id=1, source_target_pairs={{0,3},{1,2},{2,1},{3,0},{4,5},{5,4},{6,7},{7,6},{8,11},{9,10},{10,... | collective-permute-start | bytes 1572872 | tf_op jit(solution)/shard_map/ppermute | solution.py:259
  59.5 10.5 %collective-permute-start.6 = (bf16[1024,256]{1,0:T(8,128)(2,1)S(1)}, bf16[1024,256]{1,0:T(8,128)(2,1)S(1)}, u32[]{:S(2)}, u32[]{:S(2)}) collective-permute-start(bf16[1024,256]{1,0:T(8,128)(2,1)S(1)} %get-tuple-element.42.hidden_ref), channel_id=1, source_target_pairs={{0,3},{1,2},{2,1},{3,0},{4,5},{5,4},{6,7},{7,6},{8,11},{9,10},{10,... | collective-permute-start | bytes 1572872 | tf_op jit(solution)/shard_map/ppermute | solution.py:259
  64.3 15.7 %collective-permute-start.8 = (bf16[1024,256]{1,0:T(8,128)(2,1)S(1)}, bf16[1024,256]{1,0:T(8,128)(2,1)S(1)}, u32[]{:S(2)}, u32[]{:S(2)}) collective-permute-start(bf16[1024,256]{1,0:T(8,128)(2,1)S(1)} %get-tuple-element.46.hidden_ref), channel_id=1, source_target_pairs={{0,3},{1,2},{2,1},{3,0},{4,5},{5,4},{6,7},{7,6},{8,11},{9,10},{10,... | collective-permute-start | bytes 1572872 | tf_op jit(solution)/shard_map/ppermute | solution.py:259
  70.7 10.1 %collective-permute-start.9 = (bf16[512,256]{1,0:T(8,128)(2,1)S(1)}, bf16[512,256]{1,0:T(8,128)(2,1)S(1)}, u32[]{:S(2)}, u32[]{:S(2)}) collective-permute-start(bf16[512,256]{1,0:T(8,128)(2,1)S(1)} %get-tuple-element.49), channel_id=1, source_target_pairs={{0,1},{1,0},{2,3},{3,2},{4,7},{5,6},{6,5},{7,4},{8,9},{9,8},{10,11... | collective-permute-start | bytes 786440 | tf_op jit(solution)/shard_map/ppermute | solution.py:256
  80.7 6.5 %collective-permute-start.10 = (bf16[512,256]{1,0:T(8,128)(2,1)S(1)}, bf16[512,256]{1,0:T(8,128)(2,1)S(1)}, u32[]{:S(2)}, u32[]{:S(2)}) collective-permute-start(bf16[512,256]{1,0:T(8,128)(2,1)S(1)} %get-tuple-element.50), channel_id=1, source_target_pairs={{0,1},{1,0},{2,3},{3,2},{4,7},{5,6},{6,5},{7,4},{8,9},{9,8},{10,11... | collective-permute-start | bytes 786440 | tf_op jit(solution)/shard_map/ppermute | solution.py:256

commit v3 on v2

--- a/solution.py
+++ b/solution.py
@@ -9,7 +9,7 @@
 
 AXES = ("dom", "grp")
 MIX = 0.3
-CHUNKS = 2
+WIDTHS = (256, 256)
 VMEM = pl.BlockSpec(memory_space=pltpu.VMEM)
 SMEM = pl.BlockSpec(memory_space=pltpu.SMEM)
 ANY = pl.BlockSpec(memory_space=pl.ANY)
@@ -82,7 +82,19 @@
         ).astype(jnp.bfloat16)
 
 
-def mine_kernel(enc_ref, pick_ref, mine_ref, enc, sems):
+def by_dom(core, block, per):
+    return pl.ds((2 * block + core) * per, per)
+
+
+def pieces(own):
+    at, start = [], 0
+    for width in WIDTHS:
+        at.append((2 * start + (0 if own else width), start, width))
+        start += width
+    return at
+
+
+def mine_kernel(per, enc_ref, pick_ref, mine_ref, enc, sems):
     rows, width = enc_ref.shape
     half = width // 2
     z = lax.axis_index("grp")
@@ -93,47 +105,57 @@
     for load in loads:
         load.start()
     for core in range(2):
-        span = pl.ds(core * rows // 2, rows // 2)
         loads[core].wait()
-        mine_ref[span, :] = jnp.dot(
-            pick_ref[span, :], enc[core].astype(jnp.bfloat16), preferred_element_type=jnp.float32
+        part = jnp.dot(
+            pick_ref[pl.ds(core * rows // 2, rows // 2), :],
+            enc[core].astype(jnp.bfloat16),
+            preferred_element_type=jnp.float32,
         ).astype(jnp.bfloat16)
-
-
-def pack_kernel(mine_ref, place_ref, row_0, row_1, out_ref):
-    rows, half = mine_ref.shape
-    part = half // CHUNKS
+        for block in range(rows // 2 // per):
+            mine_ref[by_dom(core, block, per), :] = part[block * per : (block + 1) * per, :]
+
+
+def pack_kernel(per, place_ref, row_0, row_1, mine_ref, packed_ref):
+    half = row_0.shape[1]
+    size = row_0.shape[0] - 16
     line = lax.broadcasted_iota(jnp.int32, (16, 128), 0)
     lane = lax.broadcasted_iota(jnp.int32, (16, 128), 1)
+    for to, start, wide in pieces(True):
+        packed_ref[:, to : to + wide] = mine_ref[:, start : start + wide]
     for core, row in enumerate((row_0, row_1)):
-        span = pl.ds(core * rows // 2, rows // 2)
-        for c in range(CHUNKS):
-            cols = pl.ds(c * part, part)
-            out_ref[span, 2 * c * part : (2 * c + 1) * part] = mine_ref[span, cols]
-            out_ref[span, (2 * c + 1) * part : (2 * c + 2) * part] = row[: rows // 2, cols]
-        total = jnp.zeros((rows // 2, 128), jnp.float32)
-        for n, lines in enumerate((place_ref[:, span], row[rows // 2 :, : rows // 2])):
+        total = jnp.zeros((size, 128), jnp.float32)
+        for n, lines in enumerate((place_ref[:, core * size : (core + 1) * size], row[size:, :size])):
             spread = ((lane == line + 2 * n) & (line < 2)).astype(jnp.bfloat16)
             total += lax.dot_general(
                 lines, spread, (((0,), (0,)), ((), ())), preferred_element_type=jnp.float32
             )
-        out_ref[span, 2 * half :] = total.astype(jnp.bfloat16)
-
-
-def place_kernel(arrived_ref, *outs):
+        total = total.astype(jnp.bfloat16)
+        for block in range(size // per):
+            at = by_dom(core, block, per)
+            span = slice(block * per, (block + 1) * per)
+            for to, start, wide in pieces(False):
+                packed_ref[at, to : to + wide] = row[span, start : start + wide]
+            packed_ref[at, 2 * half :] = total[span, :]
+
+
+def place_kernel(arrived_ref, token, *outs):
     rows = arrived_ref.shape[0]
-    part = outs[0].shape[1]
+    total = sum(out.shape[1] for out in outs)
     line = lax.broadcasted_iota(jnp.int32, (16, 128), 0)
     lane = lax.broadcasted_iota(jnp.int32, (16, 128), 1)
     spread = ((lane == line) & (line < 4)).astype(jnp.bfloat16)
-    outs[0][rows:, :] = lax.dot_general(
-        spread, arrived_ref[:, len(outs) * part :], (((1,), (1,)), ((), ())), preferred_element_type=jnp.float32
+    outs[0][rows:, :rows] = lax.dot_general(
+        spread, arrived_ref[:, total:], (((1,), (1,)), ((), ())), preferred_element_type=jnp.float32
     ).astype(jnp.bfloat16)
-    for c, out in enumerate(outs):
-        out[:rows, :] = arrived_ref[:, c * part : (c + 1) * part]
-
-
-def dense_kernel(list_ref, count_ref, weight_ref, dense_ref, scale_ref, held, sems):
+    if outs[0].shape[1] > rows:
+        outs[0][rows:, rows:] = jnp.zeros((16, outs[0].shape[1] - rows), jnp.bfloat16)
+    start = 0
+    for out in outs:
+        out[:rows, :] = arrived_ref[:, start : start + out.shape[1]]
+        start += out.shape[1]
+
+
+def dense_kernel(list_ref, count_ref, weight_ref, dense_ref, scale_ref, token_ref, held, sems):
     blocks, _, size, _ = weight_ref.shape
     dom, z = lax.axis_index("dom"), lax.axis_index("grp")
     loads = [pltpu.make_async_copy(weight_ref.at[b], held.at[b], sems.at[b]) for b in range(blocks)]
@@ -156,6 +178,7 @@
         total = lax.fori_loop(0, count_ref[b], put, jnp.zeros((size, size), jnp.float32))
         degree = jnp.sum(total, axis=1, keepdims=True)
         scale_ref[span, :] = jnp.broadcast_to((1.0 - MIX) * lax.rsqrt(degree), (size, 128))
+    token_ref[...] = jnp.zeros(token_ref.shape, token_ref.dtype)
 
 
 def steps_of(dom, z, q):
@@ -165,12 +188,12 @@
     return jnp.where(step == 0, 0, jnp.where(step == rx, 1, jnp.where(step == fx, 2, 3)))
 
 
-def pick_kernel(order, rows_ref, pick_ref):
+def pick_kernel(rows_ref, token, pick_ref):
     nodes, size = pick_ref.shape[1:]
     dom, z = lax.axis_index("dom"), lax.axis_index("grp")
-    coded = rows_ref[pl.ds(size, 16), :].astype(jnp.float32).astype(jnp.int32)
-    for k, n in enumerate(order):
-        p = coded[2 * n : 2 * n + 1, :] * 64 + coded[2 * n + 1 : 2 * n + 2, :]
+    coded = rows_ref[pl.ds(size, 16), :size].astype(jnp.float32).astype(jnp.int32)
+    for k in range(2):
+        p = coded[2 * k : 2 * k + 1, :] * 64 + coded[2 * k + 1 : 2 * k + 2, :]
         spot = steps_of(dom, z, p // size) * size + p % size
         for n in range(nodes // size):
             node = lax.broadcasted_iota(jnp.int32, (size, size), 0) + n * size
@@ -211,25 +234,28 @@
         )
 
 
-def last_kernel(dense_a, dense_b, scale_a, scale_b, total_ref, hidden_ref, base_ref, keep_ref, send_ref):
+def last_kernel(start, dense_a, dense_b, scale_a, scale_b, total_ref, hidden_ref, base_ref, *refs):
+    keep_ref, send_ref = refs[-2:]
+    for done, out in zip(refs[:-2], (keep_ref, send_ref)):
+        out[:, :start] = done[...]
     size = dense_a.shape[0]
-    depth = hidden_ref.shape[0]
+    depth, width = hidden_ref.shape
     for n, (dense, scale, out) in enumerate(((dense_a, scale_a, keep_ref), (dense_b, scale_b, send_ref))):
         at = pl.ds(n * size, size)
         total = total_ref[at, :] + jnp.dot(dense[:, depth:], hidden_ref[...], preferred_element_type=jnp.float32)
-        out[...] = (MIX * base_ref[at, :].astype(jnp.float32) + total * scale[:, 0:1]).astype(jnp.bfloat16)
-
-
-def join_kernel(keep_0, keep_1, got_0, got_1, out_ref, sems):
-    part = keep_0.shape[1]
+        out[:, start : start + width] = (
+            MIX * base_ref[at, :].astype(jnp.float32) + total * scale[:, 0:1]
+        ).astype(jnp.bfloat16)
+
+
+def join_kernel(keep_ref, got_ref, out_ref, sems):
+    half = keep_ref.shape[1]
     dom, z = lax.axis_index("dom"), lax.axis_index("grp")
     upper = half_of(dom % 2 == 1, z)
     copies = []
-    for n, piece in enumerate((keep_0, keep_1, got_0, got_1)):
-        start = (upper if n < 2 else 1 - upper) * 2 * part + (n % 2) * part
-        copies.append(
-            pltpu.make_async_copy(piece, out_ref.at[:, pl.ds(pl.multiple_of(start, part), part)], sems.at[n])
-        )
+    for n, (piece, side) in enumerate(((keep_ref, upper), (got_ref, 1 - upper))):
+        to = out_ref.at[:, pl.ds(pl.multiple_of(side * half, half), half)]
+        copies.append(pltpu.make_async_copy(piece, to, sems.at[n]))
     for copy in copies:
         copy.start()
     for copy in copies:
@@ -246,11 +272,9 @@
     half = width // 2
     blocks, slots, size, _ = edge_weights.shape
     nodes = rows * depth
-    part = half // CHUNKS
     devices = [(d, q) for d in range(doms) for q in range(depth)]
     row_pairs = [(d * depth + q, d * depth + (q ^ row_step(d % 2))) for d, q in devices]
     col_pairs = [(d * depth + q, d * depth + (q ^ row_step(1 - d % 2))) for d, q in devices]
-    core_major = [[d for core in range(2) for d in range(core, doms, 2)]]
 
     def to_row(a):
         return lax.ppermute(a, AXES, row_pairs)
@@ -266,7 +290,11 @@
     def dense_of(lists, count, weights, limit):
         return kernel_call(
             dense_kernel,
-            (jax.ShapeDtypeStruct((blocks * size, nodes), bf16), jax.ShapeDtypeStruct((blocks * size, 128), f32)),
+            (
+                jax.ShapeDtypeStruct((blocks * size, nodes), bf16),
+                jax.ShapeDtypeStruct((blocks * size, 128), f32),
+                jax.ShapeDtypeStruct((8, 128), f32),
+            ),
             [SMEM, SMEM, ANY],
             0,
             8 << 20,
@@ -286,8 +314,9 @@
         limit=58,
     )(owner_of.reshape(1, rows), encoded)
     row_0, row_1 = to_row_of(0, other_0), to_row_of(1, other_1)
+    per = rows // doms
     mine = kernel_call(
-        mine_kernel,
+        functools.partial(mine_kernel, per),
         jax.ShapeDtypeStruct((rows, half), bf16),
         [ANY, VMEM],
         2 * rows * rows * half,
@@ -295,45 +324,45 @@
         scratch=[held, pltpu.SemaphoreType.DMA((2,))],
         limit=50,
     )(encoded, pick)
-    sent_weights, row_0, row_1, far_blocks, far_count = lax.optimization_barrier(
-        (edge_weights, row_0, row_1, far_blocks, far_count)
+    sent_weights, mine, row_0, row_1, far_blocks, far_count = lax.optimization_barrier(
+        (edge_weights, mine, row_0, row_1, far_blocks, far_count)
     )
     far_weights = to_row(sent_weights)
     packed = kernel_call(
-        pack_kernel,
+        functools.partial(pack_kernel, per),
         jax.ShapeDtypeStruct((rows, width + 128), bf16),
         [VMEM] * 4,
         1 << 20,
         2 << 20,
-    )(mine, place, row_0, row_1)
-
-    packed = lax.all_to_all(packed, "dom", 0, 0, axis_index_groups=core_major, tiled=True)
+    )(place, row_0, row_1, mine)
+
+    packed = lax.all_to_all(packed, "dom", 0, 0, tiled=True)
+    dense_a, scale_a, token_a = dense_of(nbr_blocks, nbr_count, edge_weights, 50)
     near_rows = kernel_call(
         place_kernel,
-        tuple(jax.ShapeDtypeStruct((rows + (16 if c == 0 else 0), 2 * part), bf16) for c in range(CHUNKS)),
-        [VMEM],
+        tuple(jax.ShapeDtypeStruct((rows + (16 if c == 0 else 0), 2 * w), bf16) for c, w in enumerate(WIDTHS)),
+        [VMEM, ANY],
         1 << 20,
         1 << 20,
-    )(packed)
+    )(packed, token_a)
     far_rows = [to_col(a) for a in near_rows]
 
-    dense_a, scale_a = dense_of(nbr_blocks, nbr_count, edge_weights, 50)
-    dense_b, scale_b = dense_of(far_blocks, far_count, far_weights, 10)
-
-    def picks_of(order, first_rows):
+    dense_b, scale_b, token_b = dense_of(far_blocks, far_count, far_weights, 10)
+
+    def picks_of(first_rows, token):
         return kernel_call(
-            functools.partial(pick_kernel, order),
+            pick_kernel,
             jax.ShapeDtypeStruct((2, nodes, rows), bf16),
-            [VMEM],
+            [VMEM, ANY],
             1 << 20,
             4 << 20,
-        )(first_rows)
-
-    near_picks, far_picks = picks_of((0, 1), near_rows[0]), picks_of((0, 1), far_rows[0])
+        )(first_rows, token)
+
+    near_picks, far_picks = picks_of(near_rows[0], token_a), picks_of(far_rows[0], token_b)
 
     mine_n = 2 * rows
-    kept, sent = [], []
-    for c in range(CHUNKS):
+    result = ()
+    for c, part in enumerate(WIDTHS):
         placed = kernel_call(
             part_kernel,
             jax.ShapeDtypeStruct((nodes, part), bf16),
@@ -357,23 +386,22 @@
             2 * mine_n * mine_n * part,
             4 << 20,
         )(dense_a, dense_b, hidden)
-        keep, send = kernel_call(
-            last_kernel,
-            (jax.ShapeDtypeStruct((rows, part), bf16), jax.ShapeDtypeStruct((rows, part), bf16)),
-            [VMEM] * 7,
+        result = kernel_call(
+            functools.partial(last_kernel, sum(WIDTHS[:c])),
+            (jax.ShapeDtypeStruct((rows, sum(WIDTHS[: c + 1])), bf16),) * 2,
+            [VMEM] * (7 + len(result)),
             2 * mine_n * mine_n * part,
             4 << 20,
-        )(dense_a, dense_b, scale_a, scale_b, running, far_hidden, base)
-        kept.append(keep)
-        sent.append(to_row(send))
+        )(dense_a, dense_b, scale_a, scale_b, running, far_hidden, base, *result)
+    keep, send = result
     return pl.pallas_call(
         join_kernel,
         out_shape=jax.ShapeDtypeStruct((rows, width), bf16),
-        in_specs=[VMEM] * 4,
+        in_specs=[VMEM] * 2,
         out_specs=ANY,
-        scratch_shapes=[pltpu.SemaphoreType.DMA((4,))],
+        scratch_shapes=[pltpu.SemaphoreType.DMA((2,))],
         compiler_params=pltpu.CompilerParams(vmem_limit_bytes=8 << 20),
-    )(*kept, *sent)
+    )(keep, to_row(send))
 
 
 def solution(mesh):

time: 88.9 us -> 84.8 us (0.954)
  blocking collectives: 26.2 us -> 0 us
  waiting for transfers between devices: 25 us -> 36.7 us
  starting transfers between devices: 14.2 us -> 22.9 us
  Pallas kernels: 21.6 us -> 23.6 us
    all_to_all x1 -> x0, blocking collectives: 26.2 us -> none  [shards(): lax.all_to_all(packed, 'dom', 0, 0, axis_index_groups=core_major, tiled=T...]
    all_to_all x0 -> x1, waiting for transfers between devices: none -> 16.3 us  [shards(): packed = lax.all_to_all(packed, 'dom', 0, 0, tiled=True)]
    all_to_all x0 -> x1, starting transfers between devices: none -> 7.36 us  [shards(): packed = lax.all_to_all(packed, 'dom', 0, 0, tiled=True)]
    ppermute x4, waiting for transfers between devices: 13.6 us -> 8.29 us  [to_col(): return lax.ppermute(a, AXES, col_pairs)]
    ppermute x4, starting transfers between devices: 6.82 us -> 8.21 us  [to_col(): return lax.ppermute(a, AXES, col_pairs)]
    pallas_call x6, Pallas kernels: 4.4 us -> 5.42 us  [the longest x2 1.62 us: picks_of(): kernel_call(pick_kernel, jax.ShapeDtypeStruct((2, nodes, rows), bf16), [V...]
    pallas_call x2, Pallas kernels: 4.49 us -> 5.47 us  [dense_of(): kernel_call(dense_kernel, (jax.ShapeDtypeStruct((blocks * size, nodes), b...]
    ppermute x5 -> x4, waiting for transfers between devices: 8.89 us -> 9.63 us  [to_row(): return lax.ppermute(a, AXES, row_pairs)]
  transfers between devices with their start and end apart: 11 -> 11, of which waited for: 6 -> 8; matrix products, arithmetic and copies ran while one was open for 0% -> 0% of each run, Pallas kernels for 20% -> 22%
where the time goes in v3:
time: 84.8 us; the launch traced here: 84.5 us
  waiting for transfers between devices  36.7 us (43%)
  Pallas kernels  23.6 us (28%)
  starting transfers between devices  22.9 us (27%)
  local copies, waits for them, and re-layouts  1.07 us (1%)
    all_to_all x1, waiting for transfers between devices, shards(): packed = lax.all_to_all(packed, 'dom', 0, 0, tiled=True)  16.3 us
    ppermute x4, waiting for transfers between devices, to_row(): return lax.ppermute(a, AXES, row_pairs)  9.63 us
    ppermute x4, waiting for transfers between devices, to_col(): return lax.ppermute(a, AXES, col_pairs)  8.29 us
    ppermute x4, starting transfers between devices, to_col(): return lax.ppermute(a, AXES, col_pairs)  8.21 us
    all_to_all x1, starting transfers between devices, shards(): packed = lax.all_to_all(packed, 'dom', 0, 0, tiled=True)  7.36 us
    pallas_call x2, Pallas kernels, dense_of(): kernel_call(dense_kernel, (jax.ShapeDtypeStruct((blocks * size, nodes), b...  5.47 us
    pallas_call x2, Pallas kernels, shards(): kernel_call(first_kernel, (jax.ShapeDtypeStruct((mine_n, part), bf16), ja...  4.68 us
    ppermute x2, starting transfers between devices, to_row_of(): lax.ppermute(a, AXES, [(d * depth + q, d * depth + (q ^ row_step(core)))...  4.61 us
  transfers between devices with their start and end apart: 11, of which 8 were waited for; matrix products, arithmetic and copies ran while one was open for 0% of the time, Pallas kernels for 22%

profile of v3, /device:TPU:0, one launch (start us, length us, event | category | flops | bytes accessed | tf_op | source)
XLA Modules:
  0.0 84.5 jit_solution(13483669408742373871)
XLA Ops:
  0.0 0.0 copy-start
  0.0 0.0 copy-start.3
  0.0 0.0 copy-start.4
  0.0 2.9 %shard_map.56 = (bf16[272,512]{1,0:T(8,128)(2,1)}, bf16[272,512]{1,0:T(8,128)(2,1)}, bf16[512,512]{1,0:T(8,128)(2,1)}, bf16[16,512]{1,0:T(8,128)(2,1)}) custom-call(s32[1,512]{1,0:T(1,128)} %bitcast.4, f32[512,1024]{1,0:T(8,128)} %enc_ref.3), custom_call_target="tpu_custom_call" | custom-call | flops 268435456 | bytes 4194304 | tf_op jit(solution)/shard_map/pallas_call | solution.py:307
  3.0 2.1 %collective-permute-start = (bf16[272,512]{1,0:T(8,128)(2,1)}, bf16[272,512]{1,0:T(8,128)(2,1)S(1)}, u32[]{:S(2)}, u32[]{:S(2)}) collective-permute-start(bf16[272,512]{1,0:T(8,128)(2,1)} %get-tuple-element.33), channel_id=1, source_target_pairs={{0,1},{1,0},{2,3},{3,2},{4,5},{5,4},{6,7},{7,6},{8,9},{9,8},{10,11... | collective-permute-start | bytes 835592 | tf_op jit(solution)/shard_map/ppermute | solution.py:286
  5.0 2.5 %collective-permute-start.1 = (bf16[272,512]{1,0:T(8,128)(2,1)}, bf16[272,512]{1,0:T(8,128)(2,1)S(1)}, u32[]{:S(2)}, u32[]{:S(2)}) collective-permute-start(bf16[272,512]{1,0:T(8,128)(2,1)} %get-tuple-element.34), channel_id=1, source_target_pairs={{0,3},{1,2},{2,1},{3,0},{4,7},{5,6},{6,5},{7,4},{8,11},{9,10},{10,... | collective-permute-start | bytes 835592 | tf_op jit(solution)/shard_map/ppermute | solution.py:286
  7.6 0.0 copy-done.3
  7.6 1.0 %collective-permute-start.2 = (s32[4,16]{1,0:T(4,128)S(1)}, s32[4,16]{1,0:T(4,128)S(1)}, u32[]{:S(2)}, u32[]{:S(2)}) collective-permute-start(s32[4,16]{1,0:T(4,128)S(1)} %copy-done.3), channel_id=1, source_target_pairs={{0,1},{1,0},{2,3},{3,2},{4,7},{5,6},{6,5},{7,4},{8,9},{9,8},{10,11... | collective-permute-start | bytes 776 | tf_op jit(solution)/shard_map/ppermute | solution.py:280
  8.6 0.0 copy-done.4
  8.6 1.0 %collective-permute-start.3 = (s32[4]{0:T(128)S(1)}, s32[4]{0:T(128)S(1)}, u32[]{:S(2)}, u32[]{:S(2)}) collective-permute-start(s32[4]{0:T(128)S(1)} %copy-done.4), channel_id=1, source_target_pairs={{0,1},{1,0},{2,3},{3,2},{4,7},{5,6},{6,5},{7,4},{8,9},{9,8},{10,11... | collective-permute-start | bytes 56 | tf_op jit(solution)/shard_map/ppermute | solution.py:280
  9.6 0.0 copy-done
  9.6 0.0 copy-start.1
  9.6 1.0 %copy-done.1 = bf16[512,512]{1,0:T(8,128)(2,1)S(1)} copy-done((bf16[512,512]{1,0:T(8,128)(2,1)S(1)}, bf16[512,512]{1,0:T(8,128)(2,1)}, u32[]{:S(2)}) %copy-start.1) | copy-done | bytes 524312
  10.6 0.0 copy-start.2
  10.6 1.0 %shard_map.57.mine_ref = bf16[512,512]{1,0:T(8,128)(2,1)S(1)} custom-call(f32[512,1024]{1,0:T(8,128)S(1)} %copy-done, bf16[512,512]{1,0:T(8,128)(2,1)S(1)} %copy-done.1), custom_call_target="tpu_custom_call" | custom-call | flops 268435456 | bytes 4194304 | tf_op jit(solution)/shard_map/pallas_call | solution.py:318
  11.7 0.5 collective-permute-done.3.count_ref
  12.1 0.0 copy-start.5
  12.1 0.0 collective-permute-done.2.list_ref
  12.1 0.0 collective-permute-done.row_0
  12.1 2.5 %collective-permute-done.1.row_1 = bf16[272,512]{1,0:T(8,128)(2,1)S(1)} collective-permute-done((bf16[272,512]{1,0:T(8,128)(2,1)}, bf16[272,512]{1,0:T(8,128)(2,1)S(1)}, u32[]{:S(2)}, u32[]{:S(2)}) %collective-permute-start.1) | collective-permute-done | bytes 278560 | tf_op jit(solution)/shard_map/ppermute | solution.py:286
  14.6 0.6 collective-permute-start.4
  15.2 0.0 copy-done.2
  15.2 1.3 %shard_map.59 = bf16[512,1152]{1,0:T(8,128)(2,1)} custom-call(bf16[16,512]{1,0:T(8,128)(2,1)S(1)} %copy-done.2, bf16[272,512]{1,0:T(8,128)(2,1)S(1)} %collective-permute-done.row_0, bf16[272,512]{1,0:T(8,128)(2,1)S(1)} %collective-permute-done.1.row_1, bf16[512,512]{1,0:T(8,128)(2,1)S(1)} %shard_map.57.mine_ref), custom_call_target="tpu_custom_call" | custom-call | flops 1048576 | bytes 2097152 | tf_op jit(solution)/shard_map/pallas_call | solution.py:331
  16.5 0.0 copy-done.5
  16.5 7.4 %all-to-all-start = ((bf16[32,16,1152]{2,1,0:T(8,128)(2,1)}), bf16[32,16,1152]{2,1,0:T(8,128)(2,1)S(1)}, u32[]{:S(2)}, u32[]{:S(2)}) async-start(bf16[32,16,1152]{2,1,0:T(8,128)(2,1)} %bitcast.1), calls=%async_computation | async-start | bytes 2359296 | tf_op jit(solution)/shard_map/all_to_all | solution.py:339
  23.9 2.7 %shard_map.55 = (bf16[512,2048]{1,0:T(8,128)(2,1)S(1)}, f32[512,128]{1,0:T(8,128)S(1)}, f32[8,128]{1,0:T(8,128)S(1)}) custom-call(s32[4,16]{1,0:T(4,128)S(1)} %copy-done.3, s32[4]{0:T(128)S(1)} %copy-done.4, bf16[4,16,128,128]{3,2,1,0:T(8,128)(2,1)} %weight_ref.1), custom_call_target="tpu_custom_call" | custom-call | bytes 8388608 | tf_op jit(solution)/shard_map/pallas_call | solution.py:291
  26.6 16.3 %all-to-all-done = bf16[32,16,1152]{2,1,0:T(8,128)(2,1)S(1)} async-done(((bf16[32,16,1152]{2,1,0:T(8,128)(2,1)}), bf16[32,16,1152]{2,1,0:T(8,128)(2,1)S(1)}, u32[]{:S(2)}, u32[]{:S(2)}) %all-to-all-start) | async-done | bytes 1179680 | tf_op jit(solution)/shard_map/all_to_all | solution.py:339
  42.9 0.2 shard_map.60
  43.0 2.3 %collective-permute-start.5 = (bf16[528,512]{1,0:T(8,128)(2,1)S(1)}, bf16[528,512]{1,0:T(8,128)(2,1)S(1)}, u32[]{:S(2)}, u32[]{:S(2)}) collective-permute-start(bf16[528,512]{1,0:T(8,128)(2,1)S(1)} %get-tuple-element.46.rows_ref.near_ref), channel_id=1, source_target_pairs={{0,3},{1,2},{2,1},{3,0},{4,5},{5,4},{6,7},{7,6},{8,11},{9,10},{10,... | collective-permute-start | bytes 1622024 | tf_op jit(solution)/shard_map/ppermute | solution.py:283
  45.4 0.9 %collective-permute-start.6 = (bf16[512,512]{1,0:T(8,128)(2,1)S(1)}, bf16[512,512]{1,0:T(8,128)(2,1)S(1)}, u32[]{:S(2)}, u32[]{:S(2)}) collective-permute-start(bf16[512,512]{1,0:T(8,128)(2,1)S(1)} %get-tuple-element.48.near_ref), channel_id=1, source_target_pairs={{0,3},{1,2},{2,1},{3,0},{4,5},{5,4},{6,7},{7,6},{8,11},{9,10},{10,... | collective-permute-start | bytes 1572872 | tf_op jit(solution)/shard_map/ppermute | solution.py:283
  46.3 0.8 shard_map.62.pick_ref
  47.1 1.3 %shard_map.66.part_ref = bf16[2048,256]{1,0:T(8,128)(2,1)S(1)} custom-call(bf16[2,2048,512]{2,1,0:T(8,128)(2,1)S(1)} %shard_map.62.pick_ref, bf16[528,512]{1,0:T(8,128)(2,1)S(1)} %get-tuple-element.46.rows_ref.near_ref), custom_call_target="tpu_custom_call" | custom-call | flops 1073741824 | bytes 4194304 | tf_op jit(solution)/shard_map/pallas_call | solution.py:366
  48.4 0.0 copy-start.6
  48.4 1.2 %shard_map.63.part_ref = bf16[2048,256]{1,0:T(8,128)(2,1)S(1)} custom-call(bf16[2,2048,512]{2,1,0:T(8,128)(2,1)S(1)} %shard_map.62.pick_ref, bf16[512,512]{1,0:T(8,128)(2,1)S(1)} %get-tuple-element.48.near_ref), custom_call_target="tpu_custom_call" | custom-call | flops 1073741824 | bytes 4194304 | tf_op jit(solution)/shard_map/pallas_call | solution.py:366
  49.6 0.0 collective-permute-done.4.weight_ref
  49.6 0.0 copy-done.6
  49.7 2.8 %shard_map.58 = (bf16[512,2048]{1,0:T(8,128)(2,1)S(1)}, f32[512,128]{1,0:T(8,128)S(1)}, f32[8,128]{1,0:T(8,128)S(1)}) custom-call(s32[4,16]{1,0:T(4,128)S(1)} %collective-permute-done.2.list_ref, s32[4]{0:T(128)S(1)} %copy-done.6, bf16[4,16,128,128]{3,2,1,0:T(8,128)(2,1)} %collective-permute-done.4.weight_ref), custom_call_target="tpu_custom_call" | custom-call | bytes 8388608 | tf_op jit(solution)/shard_map/pallas_call | solution.py:291
  52.4 1.2 %collective-permute-done.5.rows_ref.far_ref = bf16[528,512]{1,0:T(8,128)(2,1)S(1)} collective-permute-done((bf16[528,512]{1,0:T(8,128)(2,1)S(1)}, bf16[528,512]{1,0:T(8,128)(2,1)S(1)}, u32[]{:S(2)}, u32[]{:S(2)}) %collective-permute-start.5) | collective-permute-done | bytes 540704 | tf_op jit(solution)/shard_map/ppermute | solution.py:283
  53.6 0.8 shard_map.61.pick_ref
  54.4 2.3 %shard_map.67 = (bf16[1024,256]{1,0:T(8,128)(2,1)S(1)}, bf16[1024,256]{1,0:T(8,128)(2,1)S(1)}) custom-call(bf16[512,2048]{1,0:T(8,128)(2,1)S(1)} %get-tuple-element.31.dense_a, bf16[512,2048]{1,0:T(8,128)(2,1)S(1)} %get-tuple-element.38.dense_b, f32[512,128]{1,0:T(8,128)S(1)} %get-tuple-element.39.scale_a, f32[512,128]{1,0:T(8,128)S(1)} %get-tuple-element.40.scale_b, ...), custom_call_target="tpu_custom_call" | custom-call | flops 2147483648 | bytes 4194304 | tf_op jit(solution)/shard_map/pallas_call | solution.py:373
  56.8 2.4 %collective-permute-start.8 = (bf16[1024,256]{1,0:T(8,128)(2,1)S(1)}, bf16[1024,256]{1,0:T(8,128)(2,1)S(1)}, u32[]{:S(2)}, u32[]{:S(2)}) collective-permute-start(bf16[1024,256]{1,0:T(8,128)(2,1)S(1)} %get-tuple-element.51.hidden_ref), channel_id=1, source_target_pairs={{0,3},{1,2},{2,1},{3,0},{4,5},{5,4},{6,7},{7,6},{8,11},{9,10},{10,... | collective-permute-start | bytes 1572872 | tf_op jit(solution)/shard_map/ppermute | solution.py:283
  59.2 0.1 collective-permute-done.6.far_ref
  59.2 2.3 %shard_map.64 = (bf16[1024,256]{1,0:T(8,128)(2,1)S(1)}, bf16[1024,256]{1,0:T(8,128)(2,1)S(1)}) custom-call(bf16[512,2048]{1,0:T(8,128)(2,1)S(1)} %get-tuple-element.31.dense_a, bf16[512,2048]{1,0:T(8,128)(2,1)S(1)} %get-tuple-element.38.dense_b, f32[512,128]{1,0:T(8,128)S(1)} %get-tuple-element.39.scale_a, f32[512,128]{1,0:T(8,128)S(1)} %get-tuple-element.40.scale_b, ...), custom_call_target="tpu_custom_call" | custom-call | flops 2147483648 | bytes 4194304 | tf_op jit(solution)/shard_map/pallas_call | solution.py:373
  61.6 2.6 %collective-permute-start.7 = (bf16[1024,256]{1,0:T(8,128)(2,1)S(1)}, bf16[1024,256]{1,0:T(8,128)(2,1)S(1)}, u32[]{:S(2)}, u32[]{:S(2)}) collective-permute-start(bf16[1024,256]{1,0:T(8,128)(2,1)S(1)} %get-tuple-element.49.hidden_ref), channel_id=1, source_target_pairs={{0,3},{1,2},{2,1},{3,0},{4,5},{5,4},{6,7},{7,6},{8,11},{9,10},{10,... | collective-permute-start | bytes 1572872 | tf_op jit(solution)/shard_map/ppermute | solution.py:283
  64.2 0.7 shard_map.68.total_ref
  64.9 0.7 shard_map.65.total_ref
  65.6 1.7 %collective-permute-done.8.hidden_ref = bf16[1024,256]{1,0:T(8,128)(2,1)S(1)} collective-permute-done((bf16[1024,256]{1,0:T(8,128)(2,1)S(1)}, bf16[1024,256]{1,0:T(8,128)(2,1)S(1)}, u32[]{:S(2)}, u32[]{:S(2)}) %collective-permute-start.8) | collective-permute-done | bytes 524320 | tf_op jit(solution)/shard_map/ppermute | solution.py:283
  67.2 0.7 shard_map.69
  68.0 5.4 %collective-permute-done.7.hidden_ref = bf16[1024,256]{1,0:T(8,128)(2,1)S(1)} collective-permute-done((bf16[1024,256]{1,0:T(8,128)(2,1)S(1)}, bf16[1024,256]{1,0:T(8,128)(2,1)S(1)}, u32[]{:S(2)}, u32[]{:S(2)}) %collective-permute-start.7) | collective-permute-done | bytes 524320 | tf_op jit(solution)/shard_map/ppermute | solution.py:283
  73.4 0.7 shard_map.70
  74.1 0.1 collective-permute-start.9
  74.2 9.2 %collective-permute-done.9.got_ref = bf16[512,512]{1,0:T(8,128)(2,1)S(1)} collective-permute-done((bf16[512,512]{1,0:T(8,128)(2,1)S(1)}, bf16[512,512]{1,0:T(8,128)(2,1)S(1)}, u32[]{:S(2)}, u32[]{:S(2)}) %collective-permute-start.9) | collective-permute-done | bytes 524320 | tf_op jit(solution)/shard_map/ppermute | solution.py:280
  83.4 1.0 %shard_map.71 = bf16[512,1024]{1,0:T(8,128)(2,1)} custom-call(bf16[512,512]{1,0:T(8,128)(2,1)S(1)} %get-tuple-element.55.keep_ref, bf16[512,512]{1,0:T(8,128)(2,1)S(1)} %collective-permute-done.9.got_ref), custom_call_target="tpu_custom_call" | custom-call | tf_op jit(solution)/shard_map/pallas_call | solution.py:397
Async XLA Ops:
  0.0 9.6 %copy-start = (f32[512,1024]{1,0:T(8,128)S(1)}, f32[512,1024]{1,0:T(8,128)}, u32[]{:S(2)}) copy-start(f32[512,1024]{1,0:T(8,128)} %enc_ref.3) | copy-start | bytes 6291460
  0.0 7.6 %copy-start.3 = (s32[4,16]{1,0:T(4,128)S(1)}, s32[4,16]{1,0:T(4,128)}, u32[]{:S(2)}) copy-start(s32[4,16]{1,0:T(4,128)} %list_ref.1) | copy-start | bytes 772
  0.0 8.6 %copy-start.4 = (s32[4]{0:T(128)S(1)}, s32[4]{0:T(128)}, u32[]{:S(2)}) copy-start(s32[4]{0:T(128)} %count_ref.1) | copy-start | bytes 52
  3.0 9.2 %collective-permute-start = (bf16[272,512]{1,0:T(8,128)(2,1)}, bf16[272,512]{1,0:T(8,128)(2,1)S(1)}, u32[]{:S(2)}, u32[]{:S(2)}) collective-permute-start(bf16[272,512]{1,0:T(8,128)(2,1)} %get-tuple-element.33), channel_id=1, source_target_pairs={{0,1},{1,0},{2,3},{3,2},{4,5},{5,4},{6,7},{7,6},{8,9},{9,8},{10,11... | collective-permute-start | bytes 835592 | tf_op jit(solution)/shard_map/ppermute | solution.py:286
  5.0 9.6 %collective-permute-start.1 = (bf16[272,512]{1,0:T(8,128)(2,1)}, bf16[272,512]{1,0:T(8,128)(2,1)S(1)}, u32[]{:S(2)}, u32[]{:S(2)}) collective-permute-start(bf16[272,512]{1,0:T(8,128)(2,1)} %get-tuple-element.34), channel_id=1, source_target_pairs={{0,3},{1,2},{2,1},{3,0},{4,7},{5,6},{6,5},{7,4},{8,11},{9,10},{10,... | collective-permute-start | bytes 835592 | tf_op jit(solution)/shard_map/ppermute | solution.py:286
  7.6 4.6 %collective-permute-start.2 = (s32[4,16]{1,0:T(4,128)S(1)}, s32[4,16]{1,0:T(4,128)S(1)}, u32[]{:S(2)}, u32[]{:S(2)}) collective-permute-start(s32[4,16]{1,0:T(4,128)S(1)} %copy-done.3), channel_id=1, source_target_pairs={{0,1},{1,0},{2,3},{3,2},{4,7},{5,6},{6,5},{7,4},{8,9},{9,8},{10,11... | collective-permute-start | bytes 776 | tf_op jit(solution)/shard_map/ppermute | solution.py:280
  8.6 3.5 %collective-permute-start.3 = (s32[4]{0:T(128)S(1)}, s32[4]{0:T(128)S(1)}, u32[]{:S(2)}, u32[]{:S(2)}) collective-permute-start(s32[4]{0:T(128)S(1)} %copy-done.4), channel_id=1, source_target_pairs={{0,1},{1,0},{2,3},{3,2},{4,7},{5,6},{6,5},{7,4},{8,9},{9,8},{10,11... | collective-permute-start | bytes 56 | tf_op jit(solution)/shard_map/ppermute | solution.py:280
  9.6 1.0 %copy-start.1 = (bf16[512,512]{1,0:T(8,128)(2,1)S(1)}, bf16[512,512]{1,0:T(8,128)(2,1)}, u32[]{:S(2)}) copy-start(bf16[512,512]{1,0:T(8,128)(2,1)} %get-tuple-element.32.pick_ref) | copy-start | bytes 1572868
  10.6 4.6 %copy-start.2 = (bf16[16,512]{1,0:T(8,128)(2,1)S(1)}, bf16[16,512]{1,0:T(8,128)(2,1)}, u32[]{:S(2)}) copy-start(bf16[16,512]{1,0:T(8,128)(2,1)} %get-tuple-element.41.place_ref) | copy-start | bytes 49156
  12.1 4.4 %copy-start.5 = (s32[4]{0:T(128)}, s32[4]{0:T(128)S(1)}, u32[]{:S(2)}) copy-start(s32[4]{0:T(128)S(1)} %collective-permute-done.3.count_ref) | copy-start | bytes 52
  14.6 35.0 %collective-permute-start.4 = (bf16[4,16,128,128]{3,2,1,0:T(8,128)(2,1)}, bf16[4,16,128,128]{3,2,1,0:T(8,128)(2,1)}, u32[]{:S(2)}, u32[]{:S(2)}) collective-permute-start(bf16[4,16,128,128]{3,2,1,0:T(8,128)(2,1)} %weight_ref.1), channel_id=1, source_target_pairs={{0,1},{1,0},{2,3},{3,2},{4,7},{5,6},{6,5},{7,4},{8,9},{9,8},{10,11... | collective-permute-start | bytes 6291464 | tf_op jit(solution)/shard_map/ppermute | solution.py:280
  16.5 26.4 %all-to-all-start = ((bf16[32,16,1152]{2,1,0:T(8,128)(2,1)}), bf16[32,16,1152]{2,1,0:T(8,128)(2,1)S(1)}, u32[]{:S(2)}, u32[]{:S(2)}) async-start(bf16[32,16,1152]{2,1,0:T(8,128)(2,1)} %bitcast.1), calls=%async_computation | async-start | bytes 2359296 | tf_op jit(solution)/shard_map/all_to_all | solution.py:339
  43.0 10.6 %collective-permute-start.5 = (bf16[528,512]{1,0:T(8,128)(2,1)S(1)}, bf16[528,512]{1,0:T(8,128)(2,1)S(1)}, u32[]{:S(2)}, u32[]{:S(2)}) collective-permute-start(bf16[528,512]{1,0:T(8,128)(2,1)S(1)} %get-tuple-element.46.rows_ref.near_ref), channel_id=1, source_target_pairs={{0,3},{1,2},{2,1},{3,0},{4,5},{5,4},{6,7},{7,6},{8,11},{9,10},{10,... | collective-permute-start | bytes 1622024 | tf_op jit(solution)/shard_map/ppermute | solution.py:283
  45.4 13.9 %collective-permute-start.6 = (bf16[512,512]{1,0:T(8,128)(2,1)S(1)}, bf16[512,512]{1,0:T(8,128)(2,1)S(1)}, u32[]{:S(2)}, u32[]{:S(2)}) collective-permute-start(bf16[512,512]{1,0:T(8,128)(2,1)S(1)} %get-tuple-element.48.near_ref), channel_id=1, source_target_pairs={{0,3},{1,2},{2,1},{3,0},{4,5},{5,4},{6,7},{7,6},{8,11},{9,10},{10,... | collective-permute-start | bytes 1572872 | tf_op jit(solution)/shard_map/ppermute | solution.py:283
  48.4 1.3 %copy-start.6 = (s32[4]{0:T(128)S(1)}, s32[4]{0:T(128)}, u32[]{:S(2)}) copy-start(s32[4]{0:T(128)} %copy-done.5) | copy-start | bytes 52
  56.8 10.5 %collective-permute-start.8 = (bf16[1024,256]{1,0:T(8,128)(2,1)S(1)}, bf16[1024,256]{1,0:T(8,128)(2,1)S(1)}, u32[]{:S(2)}, u32[]{:S(2)}) collective-permute-start(bf16[1024,256]{1,0:T(8,128)(2,1)S(1)} %get-tuple-element.51.hidden_ref), channel_id=1, source_target_pairs={{0,3},{1,2},{2,1},{3,0},{4,5},{5,4},{6,7},{7,6},{8,11},{9,10},{10,... | collective-permute-start | bytes 1572872 | tf_op jit(solution)/shard_map/ppermute | solution.py:283
  61.6 11.8 %collective-permute-start.7 = (bf16[1024,256]{1,0:T(8,128)(2,1)S(1)}, bf16[1024,256]{1,0:T(8,128)(2,1)S(1)}, u32[]{:S(2)}, u32[]{:S(2)}) collective-permute-start(bf16[1024,256]{1,0:T(8,128)(2,1)S(1)} %get-tuple-element.49.hidden_ref), channel_id=1, source_target_pairs={{0,3},{1,2},{2,1},{3,0},{4,5},{5,4},{6,7},{7,6},{8,11},{9,10},{10,... | collective-permute-start | bytes 1572872 | tf_op jit(solution)/shard_map/ppermute | solution.py:283
  74.1 9.3 %collective-permute-start.9 = (bf16[512,512]{1,0:T(8,128)(2,1)S(1)}, bf16[512,512]{1,0:T(8,128)(2,1)S(1)}, u32[]{:S(2)}, u32[]{:S(2)}) collective-permute-start(bf16[512,512]{1,0:T(8,128)(2,1)S(1)} %get-tuple-element.56), channel_id=1, source_target_pairs={{0,1},{1,0},{2,3},{3,2},{4,7},{5,6},{6,5},{7,4},{8,9},{9,8},{10,11... | collective-permute-start | bytes 1572872 | tf_op jit(solution)/shard_map/ppermute | solution.py:280

commit v4 on v3

--- a/solution.py
+++ b/solution.py
@@ -234,32 +234,43 @@
         )
 
 
-def last_kernel(start, dense_a, dense_b, scale_a, scale_b, total_ref, hidden_ref, base_ref, *refs):
-    keep_ref, send_ref = refs[-2:]
-    for done, out in zip(refs[:-2], (keep_ref, send_ref)):
-        out[:, :start] = done[...]
+def last_kernel(dense_a, dense_b, scale_a, scale_b, total_ref, hidden_ref, base_ref, keep_ref, send_ref):
     size = dense_a.shape[0]
-    depth, width = hidden_ref.shape
+    depth = hidden_ref.shape[0]
     for n, (dense, scale, out) in enumerate(((dense_a, scale_a, keep_ref), (dense_b, scale_b, send_ref))):
         at = pl.ds(n * size, size)
         total = total_ref[at, :] + jnp.dot(dense[:, depth:], hidden_ref[...], preferred_element_type=jnp.float32)
-        out[:, start : start + width] = (
-            MIX * base_ref[at, :].astype(jnp.float32) + total * scale[:, 0:1]
-        ).astype(jnp.bfloat16)
-
-
-def join_kernel(keep_ref, got_ref, out_ref, sems):
-    half = keep_ref.shape[1]
-    dom, z = lax.axis_index("dom"), lax.axis_index("grp")
-    upper = half_of(dom % 2 == 1, z)
+        out[...] = (MIX * base_ref[at, :].astype(jnp.float32) + total * scale[:, 0:1]).astype(jnp.bfloat16)
+
+
+def move_halves(pieces, side, out_ref, sems):
+    part = pieces[0].shape[1]
     copies = []
-    for n, (piece, side) in enumerate(((keep_ref, upper), (got_ref, 1 - upper))):
-        to = out_ref.at[:, pl.ds(pl.multiple_of(side * half, half), half)]
-        copies.append(pltpu.make_async_copy(piece, to, sems.at[n]))
+    for n, piece in enumerate(pieces):
+        start = pl.multiple_of((side * len(pieces) + n) * part, part)
+        copies.append(pltpu.make_async_copy(piece, out_ref.at[:, pl.ds(start, part)], sems.at[n]))
     for copy in copies:
         copy.start()
     for copy in copies:
         copy.wait()
+
+
+def keep_kernel(keep_0, keep_1, out_ref, sems):
+    dom, z = lax.axis_index("dom"), lax.axis_index("grp")
+    move_halves((keep_0, keep_1), half_of(dom % 2 == 1, z), out_ref, sems)
+
+
+def join_kernel(early_0, late_0, got_1, _, out_ref, sems):
+    dom, z = lax.axis_index("dom"), lax.axis_index("grp")
+    side = 1 - half_of(dom % 2 == 1, z)
+
+    @pl.when(dom % 2 == 0)
+    def _():
+        move_halves((early_0, got_1), side, out_ref, sems)
+
+    @pl.when(dom % 2 == 1)
+    def _():
+        move_halves((late_0, got_1), side, out_ref, sems)
 
 
 def row_step(core):
@@ -361,7 +372,7 @@
     near_picks, far_picks = picks_of(near_rows[0], token_a), picks_of(far_rows[0], token_b)
 
     mine_n = 2 * rows
-    result = ()
+    kept, sent = [], []
     for c, part in enumerate(WIDTHS):
         placed = kernel_call(
             part_kernel,
@@ -386,22 +397,41 @@
             2 * mine_n * mine_n * part,
             4 << 20,
         )(dense_a, dense_b, hidden)
-        result = kernel_call(
-            functools.partial(last_kernel, sum(WIDTHS[:c])),
-            (jax.ShapeDtypeStruct((rows, sum(WIDTHS[: c + 1])), bf16),) * 2,
-            [VMEM] * (7 + len(result)),
+        keep, send = kernel_call(
+            last_kernel,
+            (jax.ShapeDtypeStruct((rows, part), bf16),) * 2,
+            [VMEM] * 7,
             2 * mine_n * mine_n * part,
             4 << 20,
-        )(dense_a, dense_b, scale_a, scale_b, running, far_hidden, base, *result)
-    keep, send = result
-    return pl.pallas_call(
-        join_kernel,
-        out_shape=jax.ShapeDtypeStruct((rows, width), bf16),
+        )(dense_a, dense_b, scale_a, scale_b, running, far_hidden, base)
+        kept.append(keep)
+        sent.append(send)
+
+    def to_row_on(core, a):
+        return lax.ppermute(a, AXES, [(p, q) for p, q in row_pairs if p // depth % 2 == core])
+
+    early_0 = to_row_on(0, sent[0])
+    got_1 = to_row(sent[1])
+    held_back, _ = lax.optimization_barrier((sent[0], sent[1]))
+    late_0 = to_row_on(1, held_back)
+    whole = jax.ShapeDtypeStruct((rows, width), bf16)
+    half_done = pl.pallas_call(
+        keep_kernel,
+        out_shape=whole,
         in_specs=[VMEM] * 2,
         out_specs=ANY,
         scratch_shapes=[pltpu.SemaphoreType.DMA((2,))],
         compiler_params=pltpu.CompilerParams(vmem_limit_bytes=8 << 20),
-    )(keep, to_row(send))
+    )(*kept)
+    return pl.pallas_call(
+        join_kernel,
+        out_shape=whole,
+        in_specs=[VMEM] * 3 + [ANY],
+        out_specs=ANY,
+        input_output_aliases={3: 0},
+        scratch_shapes=[pltpu.SemaphoreType.DMA((2,))],
+        compiler_params=pltpu.CompilerParams(vmem_limit_bytes=8 << 20),
+    )(early_0, late_0, got_1, half_done)
 
 
 def solution(mesh):

time: 84.8 us -> 82 us (0.967)
  waiting for transfers between devices: 36.7 us -> 30.8 us
  starting transfers between devices: 22.9 us -> 25.5 us
    ppermute x4, waiting for transfers between devices: 9.63 us -> 4.95 us  [to_row(): return lax.ppermute(a, AXES, row_pairs)]
    ppermute x0 -> x2, starting transfers between devices: none -> 2.6 us  [to_row_on(): lax.ppermute(a, AXES, [(p, q) for p, q in row_pairs if p // depth % 2 ==...]
    ppermute x4, waiting for transfers between devices: 8.29 us -> 5.94 us  [to_col(): return lax.ppermute(a, AXES, col_pairs)]
    ppermute x0 -> x2, waiting for transfers between devices: none -> 1.03 us  [to_row_on(): lax.ppermute(a, AXES, [(p, q) for p, q in row_pairs if p // depth % 2 ==...]
    pallas_call x3 -> x4, Pallas kernels: 2.45 us -> 3.1 us  [the longest x2 1.47 us: shards(): kernel_call(last_kernel, (jax.ShapeDtypeStruct((rows, part), bf16),) * 2,...]
  transfers between devices with their start and end apart: 11 -> 13, of which waited for: 8 -> 9; matrix products, arithmetic and copies ran while one was open for 0% -> 0% of each run, Pallas kernels for 22% -> 25%
where the time goes in v4:
time: 82 us; the launch traced here: 81.7 us
  waiting for transfers between devices  30.8 us (38%)
  starting transfers between devices  25.5 us (31%)
  Pallas kernels  24.1 us (29%)
  local copies, waits for them, and re-layouts  1.07 us (1%)
    all_to_all x1, waiting for transfers between devices, shards(): packed = lax.all_to_all(packed, 'dom', 0, 0, tiled=True)  16.4 us
    ppermute x4, starting transfers between devices, to_col(): return lax.ppermute(a, AXES, col_pairs)  8.21 us
    all_to_all x1, starting transfers between devices, shards(): packed = lax.all_to_all(packed, 'dom', 0, 0, tiled=True)  7.36 us
    ppermute x4, waiting for transfers between devices, to_col(): return lax.ppermute(a, AXES, col_pairs)  5.94 us
    pallas_call x2, Pallas kernels, dense_of(): kernel_call(dense_kernel, (jax.ShapeDtypeStruct((blocks * size, nodes), b...  5.34 us
    ppermute x4, waiting for transfers between devices, to_row(): return lax.ppermute(a, AXES, row_pairs)  4.95 us
    pallas_call x2, Pallas kernels, shards(): kernel_call(first_kernel, (jax.ShapeDtypeStruct((mine_n, part), bf16), ja...  4.68 us
    ppermute x2, starting transfers between devices, to_row_of(): lax.ppermute(a, AXES, [(d * depth + q, d * depth + (q ^ row_step(core)))...  4.61 us
  transfers between devices with their start and end apart: 13, of which 9 were waited for; matrix products, arithmetic and copies ran while one was open for 0% of the time, Pallas kernels for 25%

profile of v4, /device:TPU:0, one launch (start us, length us, event | category | flops | bytes accessed | tf_op | source)
XLA Modules:
  0.0 81.7 jit_solution(16488929558667205415)
XLA Ops:
  0.0 0.0 copy-start
  0.0 0.0 copy-start.3
  0.0 0.0 copy-start.4
  0.0 2.9 %shard_map.56 = (bf16[272,512]{1,0:T(8,128)(2,1)}, bf16[272,512]{1,0:T(8,128)(2,1)}, bf16[512,512]{1,0:T(8,128)(2,1)}, bf16[16,512]{1,0:T(8,128)(2,1)}) custom-call(s32[1,512]{1,0:T(1,128)} %bitcast.4, f32[512,1024]{1,0:T(8,128)} %enc_ref.3), custom_call_target="tpu_custom_call" | custom-call | flops 268435456 | bytes 4194304 | tf_op jit(solution)/shard_map/pallas_call | solution.py:318
  3.0 2.1 %collective-permute-start = (bf16[272,512]{1,0:T(8,128)(2,1)}, bf16[272,512]{1,0:T(8,128)(2,1)S(1)}, u32[]{:S(2)}, u32[]{:S(2)}) collective-permute-start(bf16[272,512]{1,0:T(8,128)(2,1)} %get-tuple-element.34), channel_id=1, source_target_pairs={{0,1},{1,0},{2,3},{3,2},{4,5},{5,4},{6,7},{7,6},{8,9},{9,8},{10,11... | collective-permute-start | bytes 835592 | tf_op jit(solution)/shard_map/ppermute | solution.py:297
  5.0 2.5 %collective-permute-start.1 = (bf16[272,512]{1,0:T(8,128)(2,1)}, bf16[272,512]{1,0:T(8,128)(2,1)S(1)}, u32[]{:S(2)}, u32[]{:S(2)}) collective-permute-start(bf16[272,512]{1,0:T(8,128)(2,1)} %get-tuple-element.35), channel_id=1, source_target_pairs={{0,3},{1,2},{2,1},{3,0},{4,7},{5,6},{6,5},{7,4},{8,11},{9,10},{10,... | collective-permute-start | bytes 835592 | tf_op jit(solution)/shard_map/ppermute | solution.py:297
  7.6 0.0 copy-done.3
  7.6 1.0 %collective-permute-start.2 = (s32[4,16]{1,0:T(4,128)S(1)}, s32[4,16]{1,0:T(4,128)S(1)}, u32[]{:S(2)}, u32[]{:S(2)}) collective-permute-start(s32[4,16]{1,0:T(4,128)S(1)} %copy-done.3), channel_id=1, source_target_pairs={{0,1},{1,0},{2,3},{3,2},{4,7},{5,6},{6,5},{7,4},{8,9},{9,8},{10,11... | collective-permute-start | bytes 776 | tf_op jit(solution)/shard_map/ppermute | solution.py:291
  8.6 0.0 copy-done.4
  8.6 1.0 %collective-permute-start.3 = (s32[4]{0:T(128)S(1)}, s32[4]{0:T(128)S(1)}, u32[]{:S(2)}, u32[]{:S(2)}) collective-permute-start(s32[4]{0:T(128)S(1)} %copy-done.4), channel_id=1, source_target_pairs={{0,1},{1,0},{2,3},{3,2},{4,7},{5,6},{6,5},{7,4},{8,9},{9,8},{10,11... | collective-permute-start | bytes 56 | tf_op jit(solution)/shard_map/ppermute | solution.py:291
  9.6 0.0 copy-done
  9.6 0.0 copy-start.1
  9.6 1.0 %copy-done.1 = bf16[512,512]{1,0:T(8,128)(2,1)S(1)} copy-done((bf16[512,512]{1,0:T(8,128)(2,1)S(1)}, bf16[512,512]{1,0:T(8,128)(2,1)}, u32[]{:S(2)}) %copy-start.1) | copy-done | bytes 524312
  10.6 0.0 copy-start.2
  10.6 1.0 %shard_map.57.mine_ref = bf16[512,512]{1,0:T(8,128)(2,1)S(1)} custom-call(f32[512,1024]{1,0:T(8,128)S(1)} %copy-done, bf16[512,512]{1,0:T(8,128)(2,1)S(1)} %copy-done.1), custom_call_target="tpu_custom_call" | custom-call | flops 268435456 | bytes 4194304 | tf_op jit(solution)/shard_map/pallas_call | solution.py:329
  11.7 0.5 collective-permute-done.3.count_ref
  12.1 0.0 copy-start.5
  12.1 0.0 collective-permute-done.2.list_ref
  12.1 0.0 collective-permute-done.row_0
  12.1 2.5 %collective-permute-done.1.row_1 = bf16[272,512]{1,0:T(8,128)(2,1)S(1)} collective-permute-done((bf16[272,512]{1,0:T(8,128)(2,1)}, bf16[272,512]{1,0:T(8,128)(2,1)S(1)}, u32[]{:S(2)}, u32[]{:S(2)}) %collective-permute-start.1) | collective-permute-done | bytes 278560 | tf_op jit(solution)/shard_map/ppermute | solution.py:297
  14.6 0.6 collective-permute-start.4
  15.2 0.0 copy-done.2
  15.2 1.3 %shard_map.59 = bf16[512,1152]{1,0:T(8,128)(2,1)} custom-call(bf16[16,512]{1,0:T(8,128)(2,1)S(1)} %copy-done.2, bf16[272,512]{1,0:T(8,128)(2,1)S(1)} %collective-permute-done.row_0, bf16[272,512]{1,0:T(8,128)(2,1)S(1)} %collective-permute-done.1.row_1, bf16[512,512]{1,0:T(8,128)(2,1)S(1)} %shard_map.57.mine_ref), custom_call_target="tpu_custom_call" | custom-call | flops 1048576 | bytes 2097152 | tf_op jit(solution)/shard_map/pallas_call | solution.py:342
  16.5 0.0 copy-done.5
  16.5 7.4 %all-to-all-start = ((bf16[32,16,1152]{2,1,0:T(8,128)(2,1)}), bf16[32,16,1152]{2,1,0:T(8,128)(2,1)S(1)}, u32[]{:S(2)}, u32[]{:S(2)}) async-start(bf16[32,16,1152]{2,1,0:T(8,128)(2,1)} %bitcast.1), calls=%async_computation | async-start | bytes 2359296 | tf_op jit(solution)/shard_map/all_to_all | solution.py:350
  23.9 2.6 %shard_map.55 = (bf16[512,2048]{1,0:T(8,128)(2,1)S(1)}, f32[512,128]{1,0:T(8,128)S(1)}, f32[8,128]{1,0:T(8,128)S(1)}) custom-call(s32[4,16]{1,0:T(4,128)S(1)} %copy-done.3, s32[4]{0:T(128)S(1)} %copy-done.4, bf16[4,16,128,128]{3,2,1,0:T(8,128)(2,1)} %weight_ref.1), custom_call_target="tpu_custom_call" | custom-call | bytes 8388608 | tf_op jit(solution)/shard_map/pallas_call | solution.py:302
  26.5 16.4 %all-to-all-done = bf16[32,16,1152]{2,1,0:T(8,128)(2,1)S(1)} async-done(((bf16[32,16,1152]{2,1,0:T(8,128)(2,1)}), bf16[32,16,1152]{2,1,0:T(8,128)(2,1)S(1)}, u32[]{:S(2)}, u32[]{:S(2)}) %all-to-all-start) | async-done | bytes 1179680 | tf_op jit(solution)/shard_map/all_to_all | solution.py:350
  42.9 0.2 shard_map.60
  43.0 2.3 %collective-permute-start.5 = (bf16[528,512]{1,0:T(8,128)(2,1)S(1)}, bf16[528,512]{1,0:T(8,128)(2,1)S(1)}, u32[]{:S(2)}, u32[]{:S(2)}) collective-permute-start(bf16[528,512]{1,0:T(8,128)(2,1)S(1)} %get-tuple-element.47.rows_ref.near_ref), channel_id=1, source_target_pairs={{0,3},{1,2},{2,1},{3,0},{4,5},{5,4},{6,7},{7,6},{8,11},{9,10},{10,... | collective-permute-start | bytes 1622024 | tf_op jit(solution)/shard_map/ppermute | solution.py:294
  45.4 0.9 %collective-permute-start.8 = (bf16[512,512]{1,0:T(8,128)(2,1)S(1)}, bf16[512,512]{1,0:T(8,128)(2,1)S(1)}, u32[]{:S(2)}, u32[]{:S(2)}) collective-permute-start(bf16[512,512]{1,0:T(8,128)(2,1)S(1)} %get-tuple-element.52.near_ref), channel_id=1, source_target_pairs={{0,3},{1,2},{2,1},{3,0},{4,5},{5,4},{6,7},{7,6},{8,11},{9,10},{10,... | collective-permute-start | bytes 1572872 | tf_op jit(solution)/shard_map/ppermute | solution.py:294
  46.3 0.8 shard_map.62.pick_ref
  47.1 1.3 %shard_map.63.part_ref = bf16[2048,256]{1,0:T(8,128)(2,1)S(1)} custom-call(bf16[2,2048,512]{2,1,0:T(8,128)(2,1)S(1)} %shard_map.62.pick_ref, bf16[528,512]{1,0:T(8,128)(2,1)S(1)} %get-tuple-element.47.rows_ref.near_ref), custom_call_target="tpu_custom_call" | custom-call | flops 1073741824 | bytes 4194304 | tf_op jit(solution)/shard_map/pallas_call | solution.py:377
  48.4 0.0 copy-start.6
  48.4 1.2 %shard_map.67.part_ref = bf16[2048,256]{1,0:T(8,128)(2,1)S(1)} custom-call(bf16[2,2048,512]{2,1,0:T(8,128)(2,1)S(1)} %shard_map.62.pick_ref, bf16[512,512]{1,0:T(8,128)(2,1)S(1)} %get-tuple-element.52.near_ref), custom_call_target="tpu_custom_call" | custom-call | flops 1073741824 | bytes 4194304 | tf_op jit(solution)/shard_map/pallas_call | solution.py:377
  49.6 0.0 collective-permute-done.4.weight_ref
  49.6 0.0 copy-done.6
  49.6 2.7 %shard_map.58 = (bf16[512,2048]{1,0:T(8,128)(2,1)S(1)}, f32[512,128]{1,0:T(8,128)S(1)}, f32[8,128]{1,0:T(8,128)S(1)}) custom-call(s32[4,16]{1,0:T(4,128)S(1)} %collective-permute-done.2.list_ref, s32[4]{0:T(128)S(1)} %copy-done.6, bf16[4,16,128,128]{3,2,1,0:T(8,128)(2,1)} %collective-permute-done.4.weight_ref), custom_call_target="tpu_custom_call" | custom-call | bytes 8388608 | tf_op jit(solution)/shard_map/pallas_call | solution.py:302
  52.4 1.2 %collective-permute-done.5.rows_ref.far_ref = bf16[528,512]{1,0:T(8,128)(2,1)S(1)} collective-permute-done((bf16[528,512]{1,0:T(8,128)(2,1)S(1)}, bf16[528,512]{1,0:T(8,128)(2,1)S(1)}, u32[]{:S(2)}, u32[]{:S(2)}) %collective-permute-start.5) | collective-permute-done | bytes 540704 | tf_op jit(solution)/shard_map/ppermute | solution.py:294
  53.6 0.8 shard_map.61.pick_ref
  54.4 2.3 %shard_map.64 = (bf16[1024,256]{1,0:T(8,128)(2,1)S(1)}, bf16[1024,256]{1,0:T(8,128)(2,1)S(1)}) custom-call(bf16[512,2048]{1,0:T(8,128)(2,1)S(1)} %get-tuple-element.32.dense_a, bf16[512,2048]{1,0:T(8,128)(2,1)S(1)} %get-tuple-element.39.dense_b, f32[512,128]{1,0:T(8,128)S(1)} %get-tuple-element.40.scale_a, f32[512,128]{1,0:T(8,128)S(1)} %get-tuple-element.41.scale_b, ...), custom_call_target="tpu_custom_call" | custom-call | flops 2147483648 | bytes 4194304 | tf_op jit(solution)/shard_map/pallas_call | solution.py:384
  56.8 2.4 %collective-permute-start.6 = (bf16[1024,256]{1,0:T(8,128)(2,1)S(1)}, bf16[1024,256]{1,0:T(8,128)(2,1)S(1)}, u32[]{:S(2)}, u32[]{:S(2)}) collective-permute-start(bf16[1024,256]{1,0:T(8,128)(2,1)S(1)} %get-tuple-element.49.hidden_ref), channel_id=1, source_target_pairs={{0,3},{1,2},{2,1},{3,0},{4,5},{5,4},{6,7},{7,6},{8,11},{9,10},{10,... | collective-permute-start | bytes 1572872 | tf_op jit(solution)/shard_map/ppermute | solution.py:294
  59.2 0.1 collective-permute-done.8.far_ref
  59.2 2.3 %shard_map.68 = (bf16[1024,256]{1,0:T(8,128)(2,1)S(1)}, bf16[1024,256]{1,0:T(8,128)(2,1)S(1)}) custom-call(bf16[512,2048]{1,0:T(8,128)(2,1)S(1)} %get-tuple-element.32.dense_a, bf16[512,2048]{1,0:T(8,128)(2,1)S(1)} %get-tuple-element.39.dense_b, f32[512,128]{1,0:T(8,128)S(1)} %get-tuple-element.40.scale_a, f32[512,128]{1,0:T(8,128)S(1)} %get-tuple-element.41.scale_b, ...), custom_call_target="tpu_custom_call" | custom-call | flops 2147483648 | bytes 4194304 | tf_op jit(solution)/shard_map/pallas_call | solution.py:384
  61.6 2.6 %collective-permute-start.9 = (bf16[1024,256]{1,0:T(8,128)(2,1)S(1)}, bf16[1024,256]{1,0:T(8,128)(2,1)S(1)}, u32[]{:S(2)}, u32[]{:S(2)}) collective-permute-start(bf16[1024,256]{1,0:T(8,128)(2,1)S(1)} %get-tuple-element.53.hidden_ref), channel_id=1, source_target_pairs={{0,3},{1,2},{2,1},{3,0},{4,5},{5,4},{6,7},{7,6},{8,11},{9,10},{10,... | collective-permute-start | bytes 1572872 | tf_op jit(solution)/shard_map/ppermute | solution.py:294
  64.2 0.7 shard_map.65.total_ref
  64.9 0.7 shard_map.69.total_ref
  65.6 1.7 %collective-permute-done.6.hidden_ref = bf16[1024,256]{1,0:T(8,128)(2,1)S(1)} collective-permute-done((bf16[1024,256]{1,0:T(8,128)(2,1)S(1)}, bf16[1024,256]{1,0:T(8,128)(2,1)S(1)}, u32[]{:S(2)}, u32[]{:S(2)}) %collective-permute-start.6) | collective-permute-done | bytes 524320 | tf_op jit(solution)/shard_map/ppermute | solution.py:294
  67.2 0.7 shard_map.66
  68.0 1.9 %collective-permute-start.7 = (bf16[512,256]{1,0:T(8,128)(2,1)S(1)}, bf16[512,256]{1,0:T(8,128)(2,1)S(1)}, u32[]{:S(2)}, u32[]{:S(2)}) collective-permute-start(bf16[512,256]{1,0:T(8,128)(2,1)S(1)} %get-tuple-element.56), channel_id=1, source_target_pairs={{0,1},{1,0},{2,3},{3,2},{8,9},{9,8},{10,11},{11,10},{16,17},{17,16... | collective-permute-start | bytes 786440 | tf_op jit(solution)/shard_map/ppermute | solution.py:411
  69.9 2.9 %collective-permute-done.9.hidden_ref = bf16[1024,256]{1,0:T(8,128)(2,1)S(1)} collective-permute-done((bf16[1024,256]{1,0:T(8,128)(2,1)S(1)}, bf16[1024,256]{1,0:T(8,128)(2,1)S(1)}, u32[]{:S(2)}, u32[]{:S(2)}) %collective-permute-start.9) | collective-permute-done | bytes 524320 | tf_op jit(solution)/shard_map/ppermute | solution.py:294
  72.9 0.7 shard_map.70
  73.6 0.7 collective-permute-start.10
  74.3 0.1 collective-permute-start.11
  74.4 0.8 %shard_map.71._ = bf16[512,1024]{1,0:T(8,128)(2,1)} custom-call(bf16[512,256]{1,0:T(8,128)(2,1)S(1)} %get-tuple-element.57.keep_0, bf16[512,256]{1,0:T(8,128)(2,1)S(1)} %get-tuple-element.58.keep_1), custom_call_target="tpu_custom_call" | custom-call | tf_op jit(solution)/shard_map/pallas_call | solution.py:418
  75.2 1.0 %collective-permute-done.7.early_0 = bf16[512,256]{1,0:T(8,128)(2,1)S(1)} collective-permute-done((bf16[512,256]{1,0:T(8,128)(2,1)S(1)}, bf16[512,256]{1,0:T(8,128)(2,1)S(1)}, u32[]{:S(2)}, u32[]{:S(2)}) %collective-permute-start.7) | collective-permute-done | bytes 262176 | tf_op jit(solution)/shard_map/ppermute | solution.py:411
  76.2 0.0 collective-permute-done.10.late_0
  76.2 4.5 %collective-permute-done.11.got_1 = bf16[512,256]{1,0:T(8,128)(2,1)S(1)} collective-permute-done((bf16[512,256]{1,0:T(8,128)(2,1)S(1)}, bf16[512,256]{1,0:T(8,128)(2,1)S(1)}, u32[]{:S(2)}, u32[]{:S(2)}) %collective-permute-start.11) | collective-permute-done | bytes 262176 | tf_op jit(solution)/shard_map/ppermute | solution.py:291
  80.7 0.8 shard_map.72
Async XLA Ops:
  0.0 9.6 %copy-start = (f32[512,1024]{1,0:T(8,128)S(1)}, f32[512,1024]{1,0:T(8,128)}, u32[]{:S(2)}) copy-start(f32[512,1024]{1,0:T(8,128)} %enc_ref.3) | copy-start | bytes 6291460
  0.0 7.6 %copy-start.3 = (s32[4,16]{1,0:T(4,128)S(1)}, s32[4,16]{1,0:T(4,128)}, u32[]{:S(2)}) copy-start(s32[4,16]{1,0:T(4,128)} %list_ref.1) | copy-start | bytes 772
  0.0 8.6 %copy-start.4 = (s32[4]{0:T(128)S(1)}, s32[4]{0:T(128)}, u32[]{:S(2)}) copy-start(s32[4]{0:T(128)} %count_ref.1) | copy-start | bytes 52
  3.0 9.2 %collective-permute-start = (bf16[272,512]{1,0:T(8,128)(2,1)}, bf16[272,512]{1,0:T(8,128)(2,1)S(1)}, u32[]{:S(2)}, u32[]{:S(2)}) collective-permute-start(bf16[272,512]{1,0:T(8,128)(2,1)} %get-tuple-element.34), channel_id=1, source_target_pairs={{0,1},{1,0},{2,3},{3,2},{4,5},{5,4},{6,7},{7,6},{8,9},{9,8},{10,11... | collective-permute-start | bytes 835592 | tf_op jit(solution)/shard_map/ppermute | solution.py:297
  5.0 9.6 %collective-permute-start.1 = (bf16[272,512]{1,0:T(8,128)(2,1)}, bf16[272,512]{1,0:T(8,128)(2,1)S(1)}, u32[]{:S(2)}, u32[]{:S(2)}) collective-permute-start(bf16[272,512]{1,0:T(8,128)(2,1)} %get-tuple-element.35), channel_id=1, source_target_pairs={{0,3},{1,2},{2,1},{3,0},{4,7},{5,6},{6,5},{7,4},{8,11},{9,10},{10,... | collective-permute-start | bytes 835592 | tf_op jit(solution)/shard_map/ppermute | solution.py:297
  7.6 4.6 %collective-permute-start.2 = (s32[4,16]{1,0:T(4,128)S(1)}, s32[4,16]{1,0:T(4,128)S(1)}, u32[]{:S(2)}, u32[]{:S(2)}) collective-permute-start(s32[4,16]{1,0:T(4,128)S(1)} %copy-done.3), channel_id=1, source_target_pairs={{0,1},{1,0},{2,3},{3,2},{4,7},{5,6},{6,5},{7,4},{8,9},{9,8},{10,11... | collective-permute-start | bytes 776 | tf_op jit(solution)/shard_map/ppermute | solution.py:291
  8.6 3.5 %collective-permute-start.3 = (s32[4]{0:T(128)S(1)}, s32[4]{0:T(128)S(1)}, u32[]{:S(2)}, u32[]{:S(2)}) collective-permute-start(s32[4]{0:T(128)S(1)} %copy-done.4), channel_id=1, source_target_pairs={{0,1},{1,0},{2,3},{3,2},{4,7},{5,6},{6,5},{7,4},{8,9},{9,8},{10,11... | collective-permute-start | bytes 56 | tf_op jit(solution)/shard_map/ppermute | solution.py:291
  9.6 1.0 %copy-start.1 = (bf16[512,512]{1,0:T(8,128)(2,1)S(1)}, bf16[512,512]{1,0:T(8,128)(2,1)}, u32[]{:S(2)}) copy-start(bf16[512,512]{1,0:T(8,128)(2,1)} %get-tuple-element.33.pick_ref) | copy-start | bytes 1572868
  10.6 4.6 %copy-start.2 = (bf16[16,512]{1,0:T(8,128)(2,1)S(1)}, bf16[16,512]{1,0:T(8,128)(2,1)}, u32[]{:S(2)}) copy-start(bf16[16,512]{1,0:T(8,128)(2,1)} %get-tuple-element.42.place_ref) | copy-start | bytes 49156
  12.1 4.4 %copy-start.5 = (s32[4]{0:T(128)}, s32[4]{0:T(128)S(1)}, u32[]{:S(2)}) copy-start(s32[4]{0:T(128)S(1)} %collective-permute-done.3.count_ref) | copy-start | bytes 52
  14.6 35.0 %collective-permute-start.4 = (bf16[4,16,128,128]{3,2,1,0:T(8,128)(2,1)}, bf16[4,16,128,128]{3,2,1,0:T(8,128)(2,1)}, u32[]{:S(2)}, u32[]{:S(2)}) collective-permute-start(bf16[4,16,128,128]{3,2,1,0:T(8,128)(2,1)} %weight_ref.1), channel_id=1, source_target_pairs={{0,1},{1,0},{2,3},{3,2},{4,7},{5,6},{6,5},{7,4},{8,9},{9,8},{10,11... | collective-permute-start | bytes 6291464 | tf_op jit(solution)/shard_map/ppermute | solution.py:291
  16.5 26.4 %all-to-all-start = ((bf16[32,16,1152]{2,1,0:T(8,128)(2,1)}), bf16[32,16,1152]{2,1,0:T(8,128)(2,1)S(1)}, u32[]{:S(2)}, u32[]{:S(2)}) async-start(bf16[32,16,1152]{2,1,0:T(8,128)(2,1)} %bitcast.1), calls=%async_computation | async-start | bytes 2359296 | tf_op jit(solution)/shard_map/all_to_all | solution.py:350
  43.0 10.6 %collective-permute-start.5 = (bf16[528,512]{1,0:T(8,128)(2,1)S(1)}, bf16[528,512]{1,0:T(8,128)(2,1)S(1)}, u32[]{:S(2)}, u32[]{:S(2)}) collective-permute-start(bf16[528,512]{1,0:T(8,128)(2,1)S(1)} %get-tuple-element.47.rows_ref.near_ref), channel_id=1, source_target_pairs={{0,3},{1,2},{2,1},{3,0},{4,5},{5,4},{6,7},{7,6},{8,11},{9,10},{10,... | collective-permute-start | bytes 1622024 | tf_op jit(solution)/shard_map/ppermute | solution.py:294
  45.4 13.9 %collective-permute-start.8 = (bf16[512,512]{1,0:T(8,128)(2,1)S(1)}, bf16[512,512]{1,0:T(8,128)(2,1)S(1)}, u32[]{:S(2)}, u32[]{:S(2)}) collective-permute-start(bf16[512,512]{1,0:T(8,128)(2,1)S(1)} %get-tuple-element.52.near_ref), channel_id=1, source_target_pairs={{0,3},{1,2},{2,1},{3,0},{4,5},{5,4},{6,7},{7,6},{8,11},{9,10},{10,... | collective-permute-start | bytes 1572872 | tf_op jit(solution)/shard_map/ppermute | solution.py:294
  48.4 1.3 %copy-start.6 = (s32[4]{0:T(128)S(1)}, s32[4]{0:T(128)}, u32[]{:S(2)}) copy-start(s32[4]{0:T(128)} %copy-done.5) | copy-start | bytes 52
  56.8 10.5 %collective-permute-start.6 = (bf16[1024,256]{1,0:T(8,128)(2,1)S(1)}, bf16[1024,256]{1,0:T(8,128)(2,1)S(1)}, u32[]{:S(2)}, u32[]{:S(2)}) collective-permute-start(bf16[1024,256]{1,0:T(8,128)(2,1)S(1)} %get-tuple-element.49.hidden_ref), channel_id=1, source_target_pairs={{0,3},{1,2},{2,1},{3,0},{4,5},{5,4},{6,7},{7,6},{8,11},{9,10},{10,... | collective-permute-start | bytes 1572872 | tf_op jit(solution)/shard_map/ppermute | solution.py:294
  61.6 11.3 %collective-permute-start.9 = (bf16[1024,256]{1,0:T(8,128)(2,1)S(1)}, bf16[1024,256]{1,0:T(8,128)(2,1)S(1)}, u32[]{:S(2)}, u32[]{:S(2)}) collective-permute-start(bf16[1024,256]{1,0:T(8,128)(2,1)S(1)} %get-tuple-element.53.hidden_ref), channel_id=1, source_target_pairs={{0,3},{1,2},{2,1},{3,0},{4,5},{5,4},{6,7},{7,6},{8,11},{9,10},{10,... | collective-permute-start | bytes 1572872 | tf_op jit(solution)/shard_map/ppermute | solution.py:294
  68.0 8.3 %collective-permute-start.7 = (bf16[512,256]{1,0:T(8,128)(2,1)S(1)}, bf16[512,256]{1,0:T(8,128)(2,1)S(1)}, u32[]{:S(2)}, u32[]{:S(2)}) collective-permute-start(bf16[512,256]{1,0:T(8,128)(2,1)S(1)} %get-tuple-element.56), channel_id=1, source_target_pairs={{0,1},{1,0},{2,3},{3,2},{8,9},{9,8},{10,11},{11,10},{16,17},{17,16... | collective-permute-start | bytes 786440 | tf_op jit(solution)/shard_map/ppermute | solution.py:411
  73.6 2.7 %collective-permute-start.10 = (bf16[512,256]{1,0:T(8,128)(2,1)S(1)}, bf16[512,256]{1,0:T(8,128)(2,1)S(1)}, u32[]{:S(2)}, u32[]{:S(2)}) collective-permute-start(bf16[512,256]{1,0:T(8,128)(2,1)S(1)} %get-tuple-element.56), channel_id=1, source_target_pairs={{4,7},{5,6},{6,5},{7,4},{12,15},{13,14},{14,13},{15,12},{20,23},{2... | collective-permute-start | bytes 786440 | tf_op jit(solution)/shard_map/ppermute | solution.py:411
  74.3 6.5 %collective-permute-start.11 = (bf16[512,256]{1,0:T(8,128)(2,1)S(1)}, bf16[512,256]{1,0:T(8,128)(2,1)S(1)}, u32[]{:S(2)}, u32[]{:S(2)}) collective-permute-start(bf16[512,256]{1,0:T(8,128)(2,1)S(1)} %get-tuple-element.55), channel_id=1, source_target_pairs={{0,1},{1,0},{2,3},{3,2},{4,7},{5,6},{6,5},{7,4},{8,9},{9,8},{10,11... | collective-permute-start | bytes 786440 | tf_op jit(solution)/shard_map/ppermute | solution.py:291

commit v5 on v4

--- a/solution.py
+++ b/solution.py
@@ -234,13 +234,21 @@
         )
 
 
-def last_kernel(dense_a, dense_b, scale_a, scale_b, total_ref, hidden_ref, base_ref, keep_ref, send_ref):
+def finish(dense, scale, total_ref, hidden_ref, base_ref, at, out):
+    depth = hidden_ref.shape[0]
+    total = total_ref[at, :] + jnp.dot(dense[:, depth:], hidden_ref[...], preferred_element_type=jnp.float32)
+    out[...] = (MIX * base_ref[at, :].astype(jnp.float32) + total * scale[:, 0:1]).astype(jnp.bfloat16)
+
+
+def last_kernel(dense_a, dense_b, scale_a, scale_b, total_ref, hidden_ref, base_ref, after, keep_ref, send_ref):
     size = dense_a.shape[0]
-    depth = hidden_ref.shape[0]
-    for n, (dense, scale, out) in enumerate(((dense_a, scale_a, keep_ref), (dense_b, scale_b, send_ref))):
-        at = pl.ds(n * size, size)
-        total = total_ref[at, :] + jnp.dot(dense[:, depth:], hidden_ref[...], preferred_element_type=jnp.float32)
-        out[...] = (MIX * base_ref[at, :].astype(jnp.float32) + total * scale[:, 0:1]).astype(jnp.bfloat16)
+    finish(dense_b, scale_b, total_ref, hidden_ref, base_ref, pl.ds(size, size), send_ref)
+    finish(dense_a, scale_a, total_ref, hidden_ref, base_ref, pl.ds(0, size), keep_ref)
+
+
+def side_kernel(row, dense, scale, total_ref, hidden_ref, base_ref, after, out_ref):
+    size = dense.shape[0]
+    finish(dense, scale, total_ref, hidden_ref, base_ref, pl.ds(row * size, size), out_ref)
 
 
 def move_halves(pieces, side, out_ref, sems):
@@ -253,6 +261,10 @@
         copy.start()
     for copy in copies:
         copy.wait()
+
+
+def hold_kernel(sent_ref, after_0, after_1, back_ref):
+    back_ref[...] = sent_ref[...]
 
 
 def keep_kernel(keep_0, keep_1, out_ref, sems):
@@ -372,7 +384,7 @@
     near_picks, far_picks = picks_of(near_rows[0], token_a), picks_of(far_rows[0], token_b)
 
     mine_n = 2 * rows
-    kept, sent = [], []
+    steps = []
     for c, part in enumerate(WIDTHS):
         placed = kernel_call(
             part_kernel,
@@ -397,24 +409,31 @@
             2 * mine_n * mine_n * part,
             4 << 20,
         )(dense_a, dense_b, hidden)
-        keep, send = kernel_call(
-            last_kernel,
-            (jax.ShapeDtypeStruct((rows, part), bf16),) * 2,
-            [VMEM] * 7,
-            2 * mine_n * mine_n * part,
-            4 << 20,
-        )(dense_a, dense_b, scale_a, scale_b, running, far_hidden, base)
-        kept.append(keep)
-        sent.append(send)
+        steps.append((running, far_hidden, base))
+
+    part = WIDTHS[0]
+    out_shape = jax.ShapeDtypeStruct((rows, part), bf16)
+    work = 2 * rows * mine_n * part
+    keep_0, send_0 = kernel_call(last_kernel, (out_shape,) * 2, [VMEM] * 7 + [ANY], 2 * work, 4 << 20)(
+        dense_a, dense_b, scale_a, scale_b, *steps[0], steps[1][0]
+    )
+    sides = []
+    for row, dense, scale, after in ((1, dense_b, scale_b, send_0), (0, dense_a, scale_a, None)):
+        sides.append(
+            kernel_call(
+                functools.partial(side_kernel, row), out_shape, [VMEM] * 5 + [ANY], work, 2 << 20
+            )(dense, scale, *steps[1], sides[0] if after is None else after)
+        )
+    kept, sent = [keep_0, sides[1]], [send_0, sides[0]]
 
     def to_row_on(core, a):
         return lax.ppermute(a, AXES, [(p, q) for p, q in row_pairs if p // depth % 2 == core])
 
     early_0 = to_row_on(0, sent[0])
     got_1 = to_row(sent[1])
-    held_back, _ = lax.optimization_barrier((sent[0], sent[1]))
+    whole = jax.ShapeDtypeStruct((rows, width), bf16)
+    held_back = kernel_call(hold_kernel, out_shape, [VMEM, ANY, ANY], 0, 1 << 19)(sent[0], early_0, sent[1])
     late_0 = to_row_on(1, held_back)
-    whole = jax.ShapeDtypeStruct((rows, width), bf16)
     half_done = pl.pallas_call(
         keep_kernel,
         out_shape=whole,

time: 82 us -> 83.3 us (1.016)
  waiting for transfers between devices: 30.8 us -> 33.2 us
  starting transfers between devices: 25.5 us -> 24.3 us
    ppermute x4, waiting for transfers between devices: 5.94 us -> 9.51 us  [to_col(): return lax.ppermute(a, AXES, col_pairs)]
    ppermute x4, starting transfers between devices: 8.21 us -> 7.01 us  [to_col(): return lax.ppermute(a, AXES, col_pairs)]
  transfers between devices with their start and end apart: 13 -> 13, of which waited for: 9 -> 8; matrix products, arithmetic and copies ran while one was open for 0% -> 0% of each run, Pallas kernels for 25% -> 25%
where the time goes in v5:
time: 83.3 us; the launch traced here: 82.9 us
  waiting for transfers between devices  33.2 us (40%)
  starting transfers between devices  24.3 us (29%)
  Pallas kernels  24.1 us (29%)
  local copies, waits for them, and re-layouts  1.07 us (1%)
    all_to_all x1, waiting for transfers between devices, shards(): packed = lax.all_to_all(packed, 'dom', 0, 0, tiled=True)  16.4 us
    ppermute x4, waiting for transfers between devices, to_col(): return lax.ppermute(a, AXES, col_pairs)  9.51 us
    all_to_all x1, starting transfers between devices, shards(): packed = lax.all_to_all(packed, 'dom', 0, 0, tiled=True)  7.36 us
    ppermute x4, starting transfers between devices, to_col(): return lax.ppermute(a, AXES, col_pairs)  7.01 us
    pallas_call x2, Pallas kernels, dense_of(): kernel_call(dense_kernel, (jax.ShapeDtypeStruct((blocks * size, nodes), b...  5.18 us
    pallas_call x2, Pallas kernels, shards(): kernel_call(first_kernel, (jax.ShapeDtypeStruct((mine_n, part), bf16), ja...  4.67 us
    ppermute x2, starting transfers between devices, to_row_of(): lax.ppermute(a, AXES, [(d * depth + q, d * depth + (q ^ row_step(core)))...  4.61 us
    ppermute x4, waiting for transfers between devices, to_row(): return lax.ppermute(a, AXES, row_pairs)  4.18 us
  transfers between devices with their start and end apart: 13, of which 8 were waited for; matrix products, arithmetic and copies ran while one was open for 0% of the time, Pallas kernels for 25%

profile of v5, /device:TPU:0, one launch (start us, length us, event | category | flops | bytes accessed | tf_op | source)
XLA Modules:
  0.0 82.9 jit_solution(17340333532392361183)
XLA Ops:
  0.0 0.0 copy-start
  0.0 0.0 copy-start.3
  0.0 0.0 copy-start.4
  0.0 2.9 %shard_map.56 = (bf16[272,512]{1,0:T(8,128)(2,1)}, bf16[272,512]{1,0:T(8,128)(2,1)}, bf16[512,512]{1,0:T(8,128)(2,1)}, bf16[16,512]{1,0:T(8,128)(2,1)}) custom-call(s32[1,512]{1,0:T(1,128)} %bitcast.4, f32[512,1024]{1,0:T(8,128)} %enc_ref.3), custom_call_target="tpu_custom_call" | custom-call | flops 268435456 | bytes 4194304 | tf_op jit(solution)/shard_map/pallas_call | solution.py:330
  3.0 2.1 %collective-permute-start = (bf16[272,512]{1,0:T(8,128)(2,1)}, bf16[272,512]{1,0:T(8,128)(2,1)S(1)}, u32[]{:S(2)}, u32[]{:S(2)}) collective-permute-start(bf16[272,512]{1,0:T(8,128)(2,1)} %get-tuple-element.31), channel_id=1, source_target_pairs={{0,1},{1,0},{2,3},{3,2},{4,5},{5,4},{6,7},{7,6},{8,9},{9,8},{10,11... | collective-permute-start | bytes 835592 | tf_op jit(solution)/shard_map/ppermute | solution.py:309
  5.0 2.5 %collective-permute-start.1 = (bf16[272,512]{1,0:T(8,128)(2,1)}, bf16[272,512]{1,0:T(8,128)(2,1)S(1)}, u32[]{:S(2)}, u32[]{:S(2)}) collective-permute-start(bf16[272,512]{1,0:T(8,128)(2,1)} %get-tuple-element.32), channel_id=1, source_target_pairs={{0,3},{1,2},{2,1},{3,0},{4,7},{5,6},{6,5},{7,4},{8,11},{9,10},{10,... | collective-permute-start | bytes 835592 | tf_op jit(solution)/shard_map/ppermute | solution.py:309
  7.6 0.0 copy-done.3
  7.6 1.0 %collective-permute-start.2 = (s32[4,16]{1,0:T(4,128)S(1)}, s32[4,16]{1,0:T(4,128)S(1)}, u32[]{:S(2)}, u32[]{:S(2)}) collective-permute-start(s32[4,16]{1,0:T(4,128)S(1)} %copy-done.3), channel_id=1, source_target_pairs={{0,1},{1,0},{2,3},{3,2},{4,7},{5,6},{6,5},{7,4},{8,9},{9,8},{10,11... | collective-permute-start | bytes 776 | tf_op jit(solution)/shard_map/ppermute | solution.py:303
  8.6 0.0 copy-done.4
  8.6 1.0 %collective-permute-start.3 = (s32[4]{0:T(128)S(1)}, s32[4]{0:T(128)S(1)}, u32[]{:S(2)}, u32[]{:S(2)}) collective-permute-start(s32[4]{0:T(128)S(1)} %copy-done.4), channel_id=1, source_target_pairs={{0,1},{1,0},{2,3},{3,2},{4,7},{5,6},{6,5},{7,4},{8,9},{9,8},{10,11... | collective-permute-start | bytes 56 | tf_op jit(solution)/shard_map/ppermute | solution.py:303
  9.6 0.0 copy-done
  9.6 0.0 copy-start.1
  9.6 1.0 %copy-done.1 = bf16[512,512]{1,0:T(8,128)(2,1)S(1)} copy-done((bf16[512,512]{1,0:T(8,128)(2,1)S(1)}, bf16[512,512]{1,0:T(8,128)(2,1)}, u32[]{:S(2)}) %copy-start.1) | copy-done | bytes 524312
  10.6 0.0 copy-start.2
  10.6 1.0 %shard_map.57.mine_ref = bf16[512,512]{1,0:T(8,128)(2,1)S(1)} custom-call(f32[512,1024]{1,0:T(8,128)S(1)} %copy-done, bf16[512,512]{1,0:T(8,128)(2,1)S(1)} %copy-done.1), custom_call_target="tpu_custom_call" | custom-call | flops 268435456 | bytes 4194304 | tf_op jit(solution)/shard_map/pallas_call | solution.py:341
  11.7 0.5 collective-permute-done.3.count_ref
  12.1 0.0 copy-start.5
  12.1 0.0 collective-permute-done.2.list_ref
  12.1 0.0 collective-permute-done.row_0
  12.1 2.5 %collective-permute-done.1.row_1 = bf16[272,512]{1,0:T(8,128)(2,1)S(1)} collective-permute-done((bf16[272,512]{1,0:T(8,128)(2,1)}, bf16[272,512]{1,0:T(8,128)(2,1)S(1)}, u32[]{:S(2)}, u32[]{:S(2)}) %collective-permute-start.1) | collective-permute-done | bytes 278560 | tf_op jit(solution)/shard_map/ppermute | solution.py:309
  14.6 0.6 collective-permute-start.4
  15.2 0.0 copy-done.2
  15.2 1.3 %shard_map.59 = bf16[512,1152]{1,0:T(8,128)(2,1)} custom-call(bf16[16,512]{1,0:T(8,128)(2,1)S(1)} %copy-done.2, bf16[272,512]{1,0:T(8,128)(2,1)S(1)} %collective-permute-done.row_0, bf16[272,512]{1,0:T(8,128)(2,1)S(1)} %collective-permute-done.1.row_1, bf16[512,512]{1,0:T(8,128)(2,1)S(1)} %shard_map.57.mine_ref), custom_call_target="tpu_custom_call" | custom-call | flops 1048576 | bytes 2097152 | tf_op jit(solution)/shard_map/pallas_call | solution.py:354
  16.5 0.0 copy-done.5
  16.5 7.4 %all-to-all-start = ((bf16[32,16,1152]{2,1,0:T(8,128)(2,1)}), bf16[32,16,1152]{2,1,0:T(8,128)(2,1)S(1)}, u32[]{:S(2)}, u32[]{:S(2)}) async-start(bf16[32,16,1152]{2,1,0:T(8,128)(2,1)} %bitcast.1), calls=%async_computation | async-start | bytes 2359296 | tf_op jit(solution)/shard_map/all_to_all | solution.py:362
  23.9 2.7 %shard_map.55 = (bf16[512,2048]{1,0:T(8,128)(2,1)S(1)}, f32[512,128]{1,0:T(8,128)S(1)}, f32[8,128]{1,0:T(8,128)S(1)}) custom-call(s32[4,16]{1,0:T(4,128)S(1)} %copy-done.3, s32[4]{0:T(128)S(1)} %copy-done.4, bf16[4,16,128,128]{3,2,1,0:T(8,128)(2,1)} %weight_ref.1), custom_call_target="tpu_custom_call" | custom-call | bytes 8388608 | tf_op jit(solution)/shard_map/pallas_call | solution.py:314
  26.5 16.4 %all-to-all-done = bf16[32,16,1152]{2,1,0:T(8,128)(2,1)S(1)} async-done(((bf16[32,16,1152]{2,1,0:T(8,128)(2,1)}), bf16[32,16,1152]{2,1,0:T(8,128)(2,1)S(1)}, u32[]{:S(2)}, u32[]{:S(2)}) %all-to-all-start) | async-done | bytes 1179680 | tf_op jit(solution)/shard_map/all_to_all | solution.py:362
  42.9 0.2 shard_map.60
  43.0 2.3 %collective-permute-start.5 = (bf16[528,512]{1,0:T(8,128)(2,1)S(1)}, bf16[528,512]{1,0:T(8,128)(2,1)S(1)}, u32[]{:S(2)}, u32[]{:S(2)}) collective-permute-start(bf16[528,512]{1,0:T(8,128)(2,1)S(1)} %get-tuple-element.44.rows_ref.near_ref), channel_id=1, source_target_pairs={{0,3},{1,2},{2,1},{3,0},{4,5},{5,4},{6,7},{7,6},{8,11},{9,10},{10,... | collective-permute-start | bytes 1622024 | tf_op jit(solution)/shard_map/ppermute | solution.py:306
  45.4 0.9 %collective-permute-start.7 = (bf16[512,512]{1,0:T(8,128)(2,1)S(1)}, bf16[512,512]{1,0:T(8,128)(2,1)S(1)}, u32[]{:S(2)}, u32[]{:S(2)}) collective-permute-start(bf16[512,512]{1,0:T(8,128)(2,1)S(1)} %get-tuple-element.48.near_ref), channel_id=1, source_target_pairs={{0,3},{1,2},{2,1},{3,0},{4,5},{5,4},{6,7},{7,6},{8,11},{9,10},{10,... | collective-permute-start | bytes 1572872 | tf_op jit(solution)/shard_map/ppermute | solution.py:306
  46.3 0.8 shard_map.62.pick_ref
  47.1 0.0 copy-start.6
  47.1 1.3 %shard_map.63.part_ref = bf16[2048,256]{1,0:T(8,128)(2,1)S(1)} custom-call(bf16[2,2048,512]{2,1,0:T(8,128)(2,1)S(1)} %shard_map.62.pick_ref, bf16[528,512]{1,0:T(8,128)(2,1)S(1)} %get-tuple-element.44.rows_ref.near_ref), custom_call_target="tpu_custom_call" | custom-call | flops 1073741824 | bytes 4194304 | tf_op jit(solution)/shard_map/pallas_call | solution.py:389
  48.4 0.0 collective-permute-done.4.weight_ref
  48.4 0.0 copy-done.6
  48.4 2.5 %shard_map.58 = (bf16[512,2048]{1,0:T(8,128)(2,1)S(1)}, f32[512,128]{1,0:T(8,128)S(1)}, f32[8,128]{1,0:T(8,128)S(1)}) custom-call(s32[4,16]{1,0:T(4,128)S(1)} %collective-permute-done.2.list_ref, s32[4]{0:T(128)S(1)} %copy-done.6, bf16[4,16,128,128]{3,2,1,0:T(8,128)(2,1)} %collective-permute-done.4.weight_ref), custom_call_target="tpu_custom_call" | custom-call | bytes 8388608 | tf_op jit(solution)/shard_map/pallas_call | solution.py:314
  50.9 2.7 %collective-permute-done.5.rows_ref.far_ref = bf16[528,512]{1,0:T(8,128)(2,1)S(1)} collective-permute-done((bf16[528,512]{1,0:T(8,128)(2,1)S(1)}, bf16[528,512]{1,0:T(8,128)(2,1)S(1)}, u32[]{:S(2)}, u32[]{:S(2)}) %collective-permute-start.5) | collective-permute-done | bytes 540704 | tf_op jit(solution)/shard_map/ppermute | solution.py:306
  53.6 0.8 shard_map.61.pick_ref
  54.4 2.3 %shard_map.64 = (bf16[1024,256]{1,0:T(8,128)(2,1)S(1)}, bf16[1024,256]{1,0:T(8,128)(2,1)S(1)}) custom-call(bf16[512,2048]{1,0:T(8,128)(2,1)S(1)} %get-tuple-element.29.dense_a.dense, bf16[512,2048]{1,0:T(8,128)(2,1)S(1)} %get-tuple-element.36.dense_b.dense, f32[512,128]{1,0:T(8,128)S(1)} %get-tuple-element.37.scale_a.scale, ...), custom_call_target="tpu_custom_call" | custom-call | flops 2147483648 | bytes 4194304 | tf_op jit(solution)/shard_map/pallas_call | solution.py:396
  56.8 2.4 %collective-permute-start.6 = (bf16[1024,256]{1,0:T(8,128)(2,1)S(1)}, bf16[1024,256]{1,0:T(8,128)(2,1)S(1)}, u32[]{:S(2)}, u32[]{:S(2)}) collective-permute-start(bf16[1024,256]{1,0:T(8,128)(2,1)S(1)} %get-tuple-element.46.hidden_ref), channel_id=1, source_target_pairs={{0,3},{1,2},{2,1},{3,0},{4,5},{5,4},{6,7},{7,6},{8,11},{9,10},{10,... | collective-permute-start | bytes 1572872 | tf_op jit(solution)/shard_map/ppermute | solution.py:306
  59.2 1.2 %shard_map.66.part_ref = bf16[2048,256]{1,0:T(8,128)(2,1)S(1)} custom-call(bf16[2,2048,512]{2,1,0:T(8,128)(2,1)S(1)} %shard_map.62.pick_ref, bf16[512,512]{1,0:T(8,128)(2,1)S(1)} %get-tuple-element.48.near_ref), custom_call_target="tpu_custom_call" | custom-call | flops 1073741824 | bytes 4194304 | tf_op jit(solution)/shard_map/pallas_call | solution.py:389
  60.4 0.0 collective-permute-done.7.far_ref
  60.4 2.3 %shard_map.67 = (bf16[1024,256]{1,0:T(8,128)(2,1)S(1)}, bf16[1024,256]{1,0:T(8,128)(2,1)S(1)}) custom-call(bf16[512,2048]{1,0:T(8,128)(2,1)S(1)} %get-tuple-element.29.dense_a.dense, bf16[512,2048]{1,0:T(8,128)(2,1)S(1)} %get-tuple-element.36.dense_b.dense, f32[512,128]{1,0:T(8,128)S(1)} %get-tuple-element.37.scale_a.scale, ...), custom_call_target="tpu_custom_call" | custom-call | flops 2147483648 | bytes 4194304 | tf_op jit(solution)/shard_map/pallas_call | solution.py:396
  62.8 1.4 %collective-permute-start.9 = (bf16[1024,256]{1,0:T(8,128)(2,1)S(1)}, bf16[1024,256]{1,0:T(8,128)(2,1)S(1)}, u32[]{:S(2)}, u32[]{:S(2)}) collective-permute-start(bf16[1024,256]{1,0:T(8,128)(2,1)S(1)} %get-tuple-element.49.hidden_ref), channel_id=1, source_target_pairs={{0,3},{1,2},{2,1},{3,0},{4,5},{5,4},{6,7},{7,6},{8,11},{9,10},{10,... | collective-permute-start | bytes 1572872 | tf_op jit(solution)/shard_map/ppermute | solution.py:306
  64.1 0.7 shard_map.65.total_ref
  64.8 0.7 shard_map.68.after.total_ref
  65.6 1.7 %collective-permute-done.6.hidden_ref = bf16[1024,256]{1,0:T(8,128)(2,1)S(1)} collective-permute-done((bf16[1024,256]{1,0:T(8,128)(2,1)S(1)}, bf16[1024,256]{1,0:T(8,128)(2,1)S(1)}, u32[]{:S(2)}, u32[]{:S(2)}) %collective-permute-start.6) | collective-permute-done | bytes 524320 | tf_op jit(solution)/shard_map/ppermute | solution.py:306
  67.2 0.7 shard_map.69
  68.0 1.9 %collective-permute-start.8 = (bf16[512,256]{1,0:T(8,128)(2,1)S(1)}, bf16[512,256]{1,0:T(8,128)(2,1)S(1)}, u32[]{:S(2)}, u32[]{:S(2)}) collective-permute-start(bf16[512,256]{1,0:T(8,128)(2,1)S(1)} %get-tuple-element.50.after.sent_ref), channel_id=1, source_target_pairs={{0,1},{1,0},{2,3},{3,2},{8,9},{9,8},{10,11},{11,10},{16,17},{17,16... | collective-permute-start | bytes 786440 | tf_op jit(solution)/shard_map/ppermute | solution.py:430
  69.9 5.1 %collective-permute-done.9.hidden_ref = bf16[1024,256]{1,0:T(8,128)(2,1)S(1)} collective-permute-done((bf16[1024,256]{1,0:T(8,128)(2,1)S(1)}, bf16[1024,256]{1,0:T(8,128)(2,1)S(1)}, u32[]{:S(2)}, u32[]{:S(2)}) %collective-permute-start.9) | collective-permute-done | bytes 524320 | tf_op jit(solution)/shard_map/ppermute | solution.py:306
  75.1 0.4 shard_map.70.after_1.after
  75.5 0.1 collective-permute-start.11
  75.6 0.7 collective-permute-done.8.after_0.early_0
  76.3 0.7 collective-permute-start.10
  77.0 0.4 shard_map.72.keep_1
  77.4 0.8 %shard_map.73._ = bf16[512,1024]{1,0:T(8,128)(2,1)} custom-call(bf16[512,256]{1,0:T(8,128)(2,1)S(1)} %get-tuple-element.52.keep_0, bf16[512,256]{1,0:T(8,128)(2,1)S(1)} %shard_map.72.keep_1), custom_call_target="tpu_custom_call" | custom-call | tf_op jit(solution)/shard_map/pallas_call | solution.py:437
  78.2 3.7 %collective-permute-done.11.got_1 = bf16[512,256]{1,0:T(8,128)(2,1)S(1)} collective-permute-done((bf16[512,256]{1,0:T(8,128)(2,1)S(1)}, bf16[512,256]{1,0:T(8,128)(2,1)S(1)}, u32[]{:S(2)}, u32[]{:S(2)}) %collective-permute-start.11) | collective-permute-done | bytes 262176 | tf_op jit(solution)/shard_map/ppermute | solution.py:303
  82.0 0.0 collective-permute-done.10.late_0
  82.0 0.8 shard_map.74
  (1 shorter events, 0.0 us)
Async XLA Ops:
  0.0 9.6 %copy-start = (f32[512,1024]{1,0:T(8,128)S(1)}, f32[512,1024]{1,0:T(8,128)}, u32[]{:S(2)}) copy-start(f32[512,1024]{1,0:T(8,128)} %enc_ref.3) | copy-start | bytes 6291460
  0.0 7.6 %copy-start.3 = (s32[4,16]{1,0:T(4,128)S(1)}, s32[4,16]{1,0:T(4,128)}, u32[]{:S(2)}) copy-start(s32[4,16]{1,0:T(4,128)} %list_ref.1) | copy-start | bytes 772
  0.0 8.6 %copy-start.4 = (s32[4]{0:T(128)S(1)}, s32[4]{0:T(128)}, u32[]{:S(2)}) copy-start(s32[4]{0:T(128)} %count_ref.1) | copy-start | bytes 52
  3.0 9.2 %collective-permute-start = (bf16[272,512]{1,0:T(8,128)(2,1)}, bf16[272,512]{1,0:T(8,128)(2,1)S(1)}, u32[]{:S(2)}, u32[]{:S(2)}) collective-permute-start(bf16[272,512]{1,0:T(8,128)(2,1)} %get-tuple-element.31), channel_id=1, source_target_pairs={{0,1},{1,0},{2,3},{3,2},{4,5},{5,4},{6,7},{7,6},{8,9},{9,8},{10,11... | collective-permute-start | bytes 835592 | tf_op jit(solution)/shard_map/ppermute | solution.py:309
  5.0 9.6 %collective-permute-start.1 = (bf16[272,512]{1,0:T(8,128)(2,1)}, bf16[272,512]{1,0:T(8,128)(2,1)S(1)}, u32[]{:S(2)}, u32[]{:S(2)}) collective-permute-start(bf16[272,512]{1,0:T(8,128)(2,1)} %get-tuple-element.32), channel_id=1, source_target_pairs={{0,3},{1,2},{2,1},{3,0},{4,7},{5,6},{6,5},{7,4},{8,11},{9,10},{10,... | collective-permute-start | bytes 835592 | tf_op jit(solution)/shard_map/ppermute | solution.py:309
  7.6 4.6 %collective-permute-start.2 = (s32[4,16]{1,0:T(4,128)S(1)}, s32[4,16]{1,0:T(4,128)S(1)}, u32[]{:S(2)}, u32[]{:S(2)}) collective-permute-start(s32[4,16]{1,0:T(4,128)S(1)} %copy-done.3), channel_id=1, source_target_pairs={{0,1},{1,0},{2,3},{3,2},{4,7},{5,6},{6,5},{7,4},{8,9},{9,8},{10,11... | collective-permute-start | bytes 776 | tf_op jit(solution)/shard_map/ppermute | solution.py:303
  8.6 3.5 %collective-permute-start.3 = (s32[4]{0:T(128)S(1)}, s32[4]{0:T(128)S(1)}, u32[]{:S(2)}, u32[]{:S(2)}) collective-permute-start(s32[4]{0:T(128)S(1)} %copy-done.4), channel_id=1, source_target_pairs={{0,1},{1,0},{2,3},{3,2},{4,7},{5,6},{6,5},{7,4},{8,9},{9,8},{10,11... | collective-permute-start | bytes 56 | tf_op jit(solution)/shard_map/ppermute | solution.py:303
  9.6 1.0 %copy-start.1 = (bf16[512,512]{1,0:T(8,128)(2,1)S(1)}, bf16[512,512]{1,0:T(8,128)(2,1)}, u32[]{:S(2)}) copy-start(bf16[512,512]{1,0:T(8,128)(2,1)} %get-tuple-element.30.pick_ref) | copy-start | bytes 1572868
  10.6 4.6 %copy-start.2 = (bf16[16,512]{1,0:T(8,128)(2,1)S(1)}, bf16[16,512]{1,0:T(8,128)(2,1)}, u32[]{:S(2)}) copy-start(bf16[16,512]{1,0:T(8,128)(2,1)} %get-tuple-element.39.place_ref) | copy-start | bytes 49156
  12.1 4.4 %copy-start.5 = (s32[4]{0:T(128)}, s32[4]{0:T(128)S(1)}, u32[]{:S(2)}) copy-start(s32[4]{0:T(128)S(1)} %collective-permute-done.3.count_ref) | copy-start | bytes 52
  14.6 33.8 %collective-permute-start.4 = (bf16[4,16,128,128]{3,2,1,0:T(8,128)(2,1)}, bf16[4,16,128,128]{3,2,1,0:T(8,128)(2,1)}, u32[]{:S(2)}, u32[]{:S(2)}) collective-permute-start(bf16[4,16,128,128]{3,2,1,0:T(8,128)(2,1)} %weight_ref.1), channel_id=1, source_target_pairs={{0,1},{1,0},{2,3},{3,2},{4,7},{5,6},{6,5},{7,4},{8,9},{9,8},{10,11... | collective-permute-start | bytes 6291464 | tf_op jit(solution)/shard_map/ppermute | solution.py:303
  16.5 26.4 %all-to-all-start = ((bf16[32,16,1152]{2,1,0:T(8,128)(2,1)}), bf16[32,16,1152]{2,1,0:T(8,128)(2,1)S(1)}, u32[]{:S(2)}, u32[]{:S(2)}) async-start(bf16[32,16,1152]{2,1,0:T(8,128)(2,1)} %bitcast.1), calls=%async_computation | async-start | bytes 2359296 | tf_op jit(solution)/shard_map/all_to_all | solution.py:362
  43.0 10.6 %collective-permute-start.5 = (bf16[528,512]{1,0:T(8,128)(2,1)S(1)}, bf16[528,512]{1,0:T(8,128)(2,1)S(1)}, u32[]{:S(2)}, u32[]{:S(2)}) collective-permute-start(bf16[528,512]{1,0:T(8,128)(2,1)S(1)} %get-tuple-element.44.rows_ref.near_ref), channel_id=1, source_target_pairs={{0,3},{1,2},{2,1},{3,0},{4,5},{5,4},{6,7},{7,6},{8,11},{9,10},{10,... | collective-permute-start | bytes 1622024 | tf_op jit(solution)/shard_map/ppermute | solution.py:306
  45.4 15.1 %collective-permute-start.7 = (bf16[512,512]{1,0:T(8,128)(2,1)S(1)}, bf16[512,512]{1,0:T(8,128)(2,1)S(1)}, u32[]{:S(2)}, u32[]{:S(2)}) collective-permute-start(bf16[512,512]{1,0:T(8,128)(2,1)S(1)} %get-tuple-element.48.near_ref), channel_id=1, source_target_pairs={{0,3},{1,2},{2,1},{3,0},{4,5},{5,4},{6,7},{7,6},{8,11},{9,10},{10,... | collective-permute-start | bytes 1572872 | tf_op jit(solution)/shard_map/ppermute | solution.py:306
  47.1 1.3 %copy-start.6 = (s32[4]{0:T(128)S(1)}, s32[4]{0:T(128)}, u32[]{:S(2)}) copy-start(s32[4]{0:T(128)} %copy-done.5) | copy-start | bytes 52
  56.8 10.5 %collective-permute-start.6 = (bf16[1024,256]{1,0:T(8,128)(2,1)S(1)}, bf16[1024,256]{1,0:T(8,128)(2,1)S(1)}, u32[]{:S(2)}, u32[]{:S(2)}) collective-permute-start(bf16[1024,256]{1,0:T(8,128)(2,1)S(1)} %get-tuple-element.46.hidden_ref), channel_id=1, source_target_pairs={{0,3},{1,2},{2,1},{3,0},{4,5},{5,4},{6,7},{7,6},{8,11},{9,10},{10,... | collective-permute-start | bytes 1572872 | tf_op jit(solution)/shard_map/ppermute | solution.py:306
  62.8 12.3 %collective-permute-start.9 = (bf16[1024,256]{1,0:T(8,128)(2,1)S(1)}, bf16[1024,256]{1,0:T(8,128)(2,1)S(1)}, u32[]{:S(2)}, u32[]{:S(2)}) collective-permute-start(bf16[1024,256]{1,0:T(8,128)(2,1)S(1)} %get-tuple-element.49.hidden_ref), channel_id=1, source_target_pairs={{0,3},{1,2},{2,1},{3,0},{4,5},{5,4},{6,7},{7,6},{8,11},{9,10},{10,... | collective-permute-start | bytes 1572872 | tf_op jit(solution)/shard_map/ppermute | solution.py:306
  68.0 8.3 %collective-permute-start.8 = (bf16[512,256]{1,0:T(8,128)(2,1)S(1)}, bf16[512,256]{1,0:T(8,128)(2,1)S(1)}, u32[]{:S(2)}, u32[]{:S(2)}) collective-permute-start(bf16[512,256]{1,0:T(8,128)(2,1)S(1)} %get-tuple-element.50.after.sent_ref), channel_id=1, source_target_pairs={{0,1},{1,0},{2,3},{3,2},{8,9},{9,8},{10,11},{11,10},{16,17},{17,16... | collective-permute-start | bytes 786440 | tf_op jit(solution)/shard_map/ppermute | solution.py:430
  75.5 6.5 %collective-permute-start.11 = (bf16[512,256]{1,0:T(8,128)(2,1)S(1)}, bf16[512,256]{1,0:T(8,128)(2,1)S(1)}, u32[]{:S(2)}, u32[]{:S(2)}) collective-permute-start(bf16[512,256]{1,0:T(8,128)(2,1)S(1)} %shard_map.70.after_1.after), channel_id=1, source_target_pairs={{0,1},{1,0},{2,3},{3,2},{4,7},{5,6},{6,5},{7,4},{8,9},{9,8},{10,11... | collective-permute-start | bytes 786440 | tf_op jit(solution)/shard_map/ppermute | solution.py:303
  76.3 5.7 %collective-permute-start.10 = (bf16[512,256]{1,0:T(8,128)(2,1)S(1)}, bf16[512,256]{1,0:T(8,128)(2,1)S(1)}, u32[]{:S(2)}, u32[]{:S(2)}) collective-permute-start(bf16[512,256]{1,0:T(8,128)(2,1)S(1)} %shard_map.71), channel_id=1, source_target_pairs={{4,7},{5,6},{6,5},{7,4},{12,15},{13,14},{14,13},{15,12},{20,23},{2... | collective-permute-start | bytes 786440 | tf_op jit(solution)/shard_map/ppermute | solution.py:430

commit v6 on v5

--- a/solution.py
+++ b/solution.py
@@ -188,7 +188,8 @@
     return jnp.where(step == 0, 0, jnp.where(step == rx, 1, jnp.where(step == fx, 2, 3)))
 
 
-def pick_kernel(rows_ref, token, pick_ref):
+def pick_kernel(rows_ref, *refs):
+    pick_ref = refs[-1]
     nodes, size = pick_ref.shape[1:]
     dom, z = lax.axis_index("dom"), lax.axis_index("grp")
     coded = rows_ref[pl.ds(size, 16), :size].astype(jnp.float32).astype(jnp.int32)
@@ -372,27 +373,31 @@
 
     dense_b, scale_b, token_b = dense_of(far_blocks, far_count, far_weights, 10)
 
-    def picks_of(first_rows, token):
+    def picks_of(first_rows, *after):
         return kernel_call(
             pick_kernel,
             jax.ShapeDtypeStruct((2, nodes, rows), bf16),
-            [VMEM, ANY],
+            [VMEM] + [ANY] * len(after),
             1 << 20,
             4 << 20,
-        )(first_rows, token)
-
-    near_picks, far_picks = picks_of(near_rows[0], token_a), picks_of(far_rows[0], token_b)
-
-    mine_n = 2 * rows
-    steps = []
-    for c, part in enumerate(WIDTHS):
-        placed = kernel_call(
+        )(first_rows, *after)
+
+    near_picks = picks_of(near_rows[0], token_a)
+    placed = [
+        kernel_call(
             part_kernel,
             jax.ShapeDtypeStruct((nodes, part), bf16),
             [VMEM] * 2,
             4 * nodes * rows * part,
             4 << 20,
         )(near_picks, near_rows[c])
+        for c, part in enumerate(WIDTHS)
+    ]
+    far_picks = picks_of(far_rows[0], token_b, *placed)
+
+    mine_n = 2 * rows
+    steps = []
+    for c, part in enumerate(WIDTHS):
         base, hidden = kernel_call(
             first_kernel,
             (jax.ShapeDtypeStruct((mine_n, part), bf16), jax.ShapeDtypeStruct((mine_n, part), bf16)),
@@ -400,7 +405,7 @@
             4 * nodes * rows * part + 2 * mine_n * nodes * part,
             4 << 20,
             scratch=[pltpu.VMEM((nodes, part), bf16)],
-        )(dense_a, dense_b, scale_a, scale_b, far_picks, placed, far_rows[c])
+        )(dense_a, dense_b, scale_a, scale_b, far_picks, placed[c], far_rows[c])
         far_hidden = to_col(hidden)
         running = kernel_call(
             half_kernel,

time: 83.3 us -> 81.9 us (0.983)
  waiting for transfers between devices: 33.2 us -> 30.6 us
  starting transfers between devices: 24.3 us -> 25.5 us
    ppermute x4, waiting for transfers between devices: 9.51 us -> 6.9 us  [to_col(): return lax.ppermute(a, AXES, col_pairs)]
    ppermute x2, waiting for transfers between devices: 0.65 us -> 2.06 us  [to_row_on(): lax.ppermute(a, AXES, [(p, q) for p, q in row_pairs if p // depth % 2 ==...]
    ppermute x4, waiting for transfers between devices: 4.18 us -> 2.81 us  [to_row(): return lax.ppermute(a, AXES, row_pairs)]
    ppermute x4, starting transfers between devices: 7.01 us -> 8.23 us  [to_col(): return lax.ppermute(a, AXES, col_pairs)]
  transfers between devices with their start and end apart: 13 -> 13, of which waited for: 8 -> 9; matrix products, arithmetic and copies ran while one was open for 0% -> 0% of each run, Pallas kernels for 25% -> 25%
where the time goes in v6:
time: 81.9 us; the launch traced here: 81.5 us
  waiting for transfers between devices  30.6 us (37%)
  starting transfers between devices  25.5 us (31%)
  Pallas kernels  24.1 us (29%)
  local copies, waits for them, and re-layouts  1.07 us (1%)
    all_to_all x1, waiting for transfers between devices, shards(): packed = lax.all_to_all(packed, 'dom', 0, 0, tiled=True)  16.4 us
    ppermute x4, starting transfers between devices, to_col(): return lax.ppermute(a, AXES, col_pairs)  8.23 us
    all_to_all x1, starting transfers between devices, shards(): packed = lax.all_to_all(packed, 'dom', 0, 0, tiled=True)  7.35 us
    ppermute x4, waiting for transfers between devices, to_col(): return lax.ppermute(a, AXES, col_pairs)  6.9 us
    pallas_call x2, Pallas kernels, dense_of(): kernel_call(dense_kernel, (jax.ShapeDtypeStruct((blocks * size, nodes), b...  5.16 us
    pallas_call x2, Pallas kernels, shards(): kernel_call(first_kernel, (jax.ShapeDtypeStruct((mine_n, part), bf16), ja...  4.71 us
    ppermute x2, starting transfers between devices, to_row_of(): lax.ppermute(a, AXES, [(d * depth + q, d * depth + (q ^ row_step(core)))...  4.61 us
    pallas_call x1, Pallas kernels, shards(): kernel_call(functools.partial(sort_kernel, doms), (other, other, jax.Shap...  2.94 us
  transfers between devices with their start and end apart: 13, of which 9 were waited for; matrix products, arithmetic and copies ran while one was open for 0% of the time, Pallas kernels for 25%

profile of v6, /device:TPU:0, one launch (start us, length us, event | category | flops | bytes accessed | tf_op | source)
XLA Modules:
  0.0 81.5 jit_solution(6293598154324126651)
XLA Ops:
  0.0 0.0 copy-start
  0.0 0.0 copy-start.4
  0.0 0.0 copy-start.3
  0.0 2.9 %shard_map.56 = (bf16[272,512]{1,0:T(8,128)(2,1)}, bf16[272,512]{1,0:T(8,128)(2,1)}, bf16[512,512]{1,0:T(8,128)(2,1)}, bf16[16,512]{1,0:T(8,128)(2,1)}) custom-call(s32[1,512]{1,0:T(1,128)} %bitcast.4, f32[512,1024]{1,0:T(8,128)} %enc_ref.3), custom_call_target="tpu_custom_call" | custom-call | flops 268435456 | bytes 4194304 | tf_op jit(solution)/shard_map/pallas_call | solution.py:331
  3.0 2.1 %collective-permute-start = (bf16[272,512]{1,0:T(8,128)(2,1)}, bf16[272,512]{1,0:T(8,128)(2,1)S(1)}, u32[]{:S(2)}, u32[]{:S(2)}) collective-permute-start(bf16[272,512]{1,0:T(8,128)(2,1)} %get-tuple-element.31), channel_id=1, source_target_pairs={{0,1},{1,0},{2,3},{3,2},{4,5},{5,4},{6,7},{7,6},{8,9},{9,8},{10,11... | collective-permute-start | bytes 835592 | tf_op jit(solution)/shard_map/ppermute | solution.py:310
  5.0 2.5 %collective-permute-start.1 = (bf16[272,512]{1,0:T(8,128)(2,1)}, bf16[272,512]{1,0:T(8,128)(2,1)S(1)}, u32[]{:S(2)}, u32[]{:S(2)}) collective-permute-start(bf16[272,512]{1,0:T(8,128)(2,1)} %get-tuple-element.32), channel_id=1, source_target_pairs={{0,3},{1,2},{2,1},{3,0},{4,7},{5,6},{6,5},{7,4},{8,11},{9,10},{10,... | collective-permute-start | bytes 835592 | tf_op jit(solution)/shard_map/ppermute | solution.py:310
  7.6 0.0 copy-done.4
  7.6 1.0 %collective-permute-start.3 = (s32[4]{0:T(128)S(1)}, s32[4]{0:T(128)S(1)}, u32[]{:S(2)}, u32[]{:S(2)}) collective-permute-start(s32[4]{0:T(128)S(1)} %copy-done.4), channel_id=1, source_target_pairs={{0,1},{1,0},{2,3},{3,2},{4,7},{5,6},{6,5},{7,4},{8,9},{9,8},{10,11... | collective-permute-start | bytes 56 | tf_op jit(solution)/shard_map/ppermute | solution.py:304
  8.6 0.0 copy-done.3
  8.6 1.0 %collective-permute-start.2 = (s32[4,16]{1,0:T(4,128)S(1)}, s32[4,16]{1,0:T(4,128)S(1)}, u32[]{:S(2)}, u32[]{:S(2)}) collective-permute-start(s32[4,16]{1,0:T(4,128)S(1)} %copy-done.3), channel_id=1, source_target_pairs={{0,1},{1,0},{2,3},{3,2},{4,7},{5,6},{6,5},{7,4},{8,9},{9,8},{10,11... | collective-permute-start | bytes 776 | tf_op jit(solution)/shard_map/ppermute | solution.py:304
  9.6 0.0 copy-done
  9.6 0.0 copy-start.1
  9.6 1.0 %copy-done.1 = bf16[512,512]{1,0:T(8,128)(2,1)S(1)} copy-done((bf16[512,512]{1,0:T(8,128)(2,1)S(1)}, bf16[512,512]{1,0:T(8,128)(2,1)}, u32[]{:S(2)}) %copy-start.1) | copy-done | bytes 524312
  10.6 0.0 copy-start.2
  10.6 1.0 %shard_map.57.mine_ref = bf16[512,512]{1,0:T(8,128)(2,1)S(1)} custom-call(f32[512,1024]{1,0:T(8,128)S(1)} %copy-done, bf16[512,512]{1,0:T(8,128)(2,1)S(1)} %copy-done.1), custom_call_target="tpu_custom_call" | custom-call | flops 268435456 | bytes 4194304 | tf_op jit(solution)/shard_map/pallas_call | solution.py:342
  11.7 0.3 collective-permute-done.3.count_ref
  12.0 0.0 copy-start.5
  12.0 0.2 collective-permute-done.2.list_ref
  12.2 0.0 collective-permute-done.row_0
  12.2 2.4 %collective-permute-done.1.row_1 = bf16[272,512]{1,0:T(8,128)(2,1)S(1)} collective-permute-done((bf16[272,512]{1,0:T(8,128)(2,1)}, bf16[272,512]{1,0:T(8,128)(2,1)S(1)}, u32[]{:S(2)}, u32[]{:S(2)}) %collective-permute-start.1) | collective-permute-done | bytes 278560 | tf_op jit(solution)/shard_map/ppermute | solution.py:310
  14.6 0.6 collective-permute-start.4
  15.2 0.0 copy-done.2
  15.2 1.3 %shard_map.59 = bf16[512,1152]{1,0:T(8,128)(2,1)} custom-call(bf16[16,512]{1,0:T(8,128)(2,1)S(1)} %copy-done.2, bf16[272,512]{1,0:T(8,128)(2,1)S(1)} %collective-permute-done.row_0, bf16[272,512]{1,0:T(8,128)(2,1)S(1)} %collective-permute-done.1.row_1, bf16[512,512]{1,0:T(8,128)(2,1)S(1)} %shard_map.57.mine_ref), custom_call_target="tpu_custom_call" | custom-call | flops 1048576 | bytes 2097152 | tf_op jit(solution)/shard_map/pallas_call | solution.py:355
  16.5 0.0 copy-done.5
  16.5 7.3 %all-to-all-start = ((bf16[32,16,1152]{2,1,0:T(8,128)(2,1)}), bf16[32,16,1152]{2,1,0:T(8,128)(2,1)S(1)}, u32[]{:S(2)}, u32[]{:S(2)}) async-start(bf16[32,16,1152]{2,1,0:T(8,128)(2,1)} %bitcast.1), calls=%async_computation | async-start | bytes 2359296 | tf_op jit(solution)/shard_map/all_to_all | solution.py:363
  23.9 2.7 %shard_map.55 = (bf16[512,2048]{1,0:T(8,128)(2,1)S(1)}, f32[512,128]{1,0:T(8,128)S(1)}, f32[8,128]{1,0:T(8,128)S(1)}) custom-call(s32[4,16]{1,0:T(4,128)S(1)} %copy-done.3, s32[4]{0:T(128)S(1)} %copy-done.4, bf16[4,16,128,128]{3,2,1,0:T(8,128)(2,1)} %weight_ref.1), custom_call_target="tpu_custom_call" | custom-call | bytes 8388608 | tf_op jit(solution)/shard_map/pallas_call | solution.py:315
  26.5 16.4 %all-to-all-done = bf16[32,16,1152]{2,1,0:T(8,128)(2,1)S(1)} async-done(((bf16[32,16,1152]{2,1,0:T(8,128)(2,1)}), bf16[32,16,1152]{2,1,0:T(8,128)(2,1)S(1)}, u32[]{:S(2)}, u32[]{:S(2)}) %all-to-all-start) | async-done | bytes 1179680 | tf_op jit(solution)/shard_map/all_to_all | solution.py:363
  42.9 0.2 shard_map.60
  43.0 2.3 %collective-permute-start.5 = (bf16[528,512]{1,0:T(8,128)(2,1)S(1)}, bf16[528,512]{1,0:T(8,128)(2,1)S(1)}, u32[]{:S(2)}, u32[]{:S(2)}) collective-permute-start(bf16[528,512]{1,0:T(8,128)(2,1)S(1)} %get-tuple-element.44.rows_ref.near_ref), channel_id=1, source_target_pairs={{0,3},{1,2},{2,1},{3,0},{4,5},{5,4},{6,7},{7,6},{8,11},{9,10},{10,... | collective-permute-start | bytes 1622024 | tf_op jit(solution)/shard_map/ppermute | solution.py:307
  45.4 0.9 %collective-permute-start.7 = (bf16[512,512]{1,0:T(8,128)(2,1)S(1)}, bf16[512,512]{1,0:T(8,128)(2,1)S(1)}, u32[]{:S(2)}, u32[]{:S(2)}) collective-permute-start(bf16[512,512]{1,0:T(8,128)(2,1)S(1)} %get-tuple-element.46.near_ref), channel_id=1, source_target_pairs={{0,3},{1,2},{2,1},{3,0},{4,5},{5,4},{6,7},{7,6},{8,11},{9,10},{10,... | collective-permute-start | bytes 1572872 | tf_op jit(solution)/shard_map/ppermute | solution.py:307
  46.3 0.8 shard_map.61.pick_ref
  47.1 1.3 %shard_map.62.refs_1_.part_ref = bf16[2048,256]{1,0:T(8,128)(2,1)S(1)} custom-call(bf16[2,2048,512]{2,1,0:T(8,128)(2,1)S(1)} %shard_map.61.pick_ref, bf16[528,512]{1,0:T(8,128)(2,1)S(1)} %get-tuple-element.44.rows_ref.near_ref), custom_call_target="tpu_custom_call" | custom-call | flops 1073741824 | bytes 4194304 | tf_op jit(solution)/shard_map/pallas_call | solution.py:387
  48.4 0.0 copy-start.6
  48.4 1.2 %shard_map.63.refs_2_.part_ref = bf16[2048,256]{1,0:T(8,128)(2,1)S(1)} custom-call(bf16[2,2048,512]{2,1,0:T(8,128)(2,1)S(1)} %shard_map.61.pick_ref, bf16[512,512]{1,0:T(8,128)(2,1)S(1)} %get-tuple-element.46.near_ref), custom_call_target="tpu_custom_call" | custom-call | flops 1073741824 | bytes 4194304 | tf_op jit(solution)/shard_map/pallas_call | solution.py:387
  49.6 0.0 collective-permute-done.4.weight_ref
  49.6 0.0 copy-done.6
  49.6 2.5 %shard_map.58 = (bf16[512,2048]{1,0:T(8,128)(2,1)S(1)}, f32[512,128]{1,0:T(8,128)S(1)}, f32[8,128]{1,0:T(8,128)S(1)}) custom-call(s32[4,16]{1,0:T(4,128)S(1)} %collective-permute-done.2.list_ref, s32[4]{0:T(128)S(1)} %copy-done.6, bf16[4,16,128,128]{3,2,1,0:T(8,128)(2,1)} %collective-permute-done.4.weight_ref), custom_call_target="tpu_custom_call" | custom-call | bytes 8388608 | tf_op jit(solution)/shard_map/pallas_call | solution.py:315
  52.2 1.5 %collective-permute-done.5.rows_ref.far_ref = bf16[528,512]{1,0:T(8,128)(2,1)S(1)} collective-permute-done((bf16[528,512]{1,0:T(8,128)(2,1)S(1)}, bf16[528,512]{1,0:T(8,128)(2,1)S(1)}, u32[]{:S(2)}, u32[]{:S(2)}) %collective-permute-start.5) | collective-permute-done | bytes 540704 | tf_op jit(solution)/shard_map/ppermute | solution.py:307
  53.6 0.8 shard_map.64.pick_ref
  54.4 2.4 %shard_map.65 = (bf16[1024,256]{1,0:T(8,128)(2,1)S(1)}, bf16[1024,256]{1,0:T(8,128)(2,1)S(1)}) custom-call(bf16[512,2048]{1,0:T(8,128)(2,1)S(1)} %get-tuple-element.29.dense_a.dense, bf16[512,2048]{1,0:T(8,128)(2,1)S(1)} %get-tuple-element.36.dense_b.dense, f32[512,128]{1,0:T(8,128)S(1)} %get-tuple-element.37.scale_a.scale, ...), custom_call_target="tpu_custom_call" | custom-call | flops 2147483648 | bytes 4194304 | tf_op jit(solution)/shard_map/pallas_call | solution.py:401
  56.8 2.4 %collective-permute-start.6 = (bf16[1024,256]{1,0:T(8,128)(2,1)S(1)}, bf16[1024,256]{1,0:T(8,128)(2,1)S(1)}, u32[]{:S(2)}, u32[]{:S(2)}) collective-permute-start(bf16[1024,256]{1,0:T(8,128)(2,1)S(1)} %get-tuple-element.47.hidden_ref), channel_id=1, source_target_pairs={{0,3},{1,2},{2,1},{3,0},{4,5},{5,4},{6,7},{7,6},{8,11},{9,10},{10,... | collective-permute-start | bytes 1572872 | tf_op jit(solution)/shard_map/ppermute | solution.py:307
  59.2 0.0 collective-permute-done.7.far_ref
  59.2 2.4 %shard_map.67 = (bf16[1024,256]{1,0:T(8,128)(2,1)S(1)}, bf16[1024,256]{1,0:T(8,128)(2,1)S(1)}) custom-call(bf16[512,2048]{1,0:T(8,128)(2,1)S(1)} %get-tuple-element.29.dense_a.dense, bf16[512,2048]{1,0:T(8,128)(2,1)S(1)} %get-tuple-element.36.dense_b.dense, f32[512,128]{1,0:T(8,128)S(1)} %get-tuple-element.37.scale_a.scale, ...), custom_call_target="tpu_custom_call" | custom-call | flops 2147483648 | bytes 4194304 | tf_op jit(solution)/shard_map/pallas_call | solution.py:401
  61.6 2.6 %collective-permute-start.9 = (bf16[1024,256]{1,0:T(8,128)(2,1)S(1)}, bf16[1024,256]{1,0:T(8,128)(2,1)S(1)}, u32[]{:S(2)}, u32[]{:S(2)}) collective-permute-start(bf16[1024,256]{1,0:T(8,128)(2,1)S(1)} %get-tuple-element.49.hidden_ref), channel_id=1, source_target_pairs={{0,3},{1,2},{2,1},{3,0},{4,5},{5,4},{6,7},{7,6},{8,11},{9,10},{10,... | collective-permute-start | bytes 1572872 | tf_op jit(solution)/shard_map/ppermute | solution.py:307
  64.2 0.7 shard_map.68.after.total_ref
  64.9 0.7 shard_map.66.total_ref
  65.6 1.7 %collective-permute-done.6.hidden_ref = bf16[1024,256]{1,0:T(8,128)(2,1)S(1)} collective-permute-done((bf16[1024,256]{1,0:T(8,128)(2,1)S(1)}, bf16[1024,256]{1,0:T(8,128)(2,1)S(1)}, u32[]{:S(2)}, u32[]{:S(2)}) %collective-permute-start.6) | collective-permute-done | bytes 524320 | tf_op jit(solution)/shard_map/ppermute | solution.py:307
  67.2 0.7 shard_map.69
  68.0 1.9 %collective-permute-start.8 = (bf16[512,256]{1,0:T(8,128)(2,1)S(1)}, bf16[512,256]{1,0:T(8,128)(2,1)S(1)}, u32[]{:S(2)}, u32[]{:S(2)}) collective-permute-start(bf16[512,256]{1,0:T(8,128)(2,1)S(1)} %get-tuple-element.50.after.sent_ref), channel_id=1, source_target_pairs={{0,1},{1,0},{2,3},{3,2},{8,9},{9,8},{10,11},{11,10},{16,17},{17,16... | collective-permute-start | bytes 786440 | tf_op jit(solution)/shard_map/ppermute | solution.py:435
  69.9 3.7 %collective-permute-done.9.hidden_ref = bf16[1024,256]{1,0:T(8,128)(2,1)S(1)} collective-permute-done((bf16[1024,256]{1,0:T(8,128)(2,1)S(1)}, bf16[1024,256]{1,0:T(8,128)(2,1)S(1)}, u32[]{:S(2)}, u32[]{:S(2)}) %collective-permute-start.9) | collective-permute-done | bytes 524320 | tf_op jit(solution)/shard_map/ppermute | solution.py:307
  73.7 0.4 shard_map.70.after_1.after
  74.1 0.1 collective-permute-start.11
  74.2 2.1 %collective-permute-done.8.after_0.early_0 = bf16[512,256]{1,0:T(8,128)(2,1)S(1)} collective-permute-done((bf16[512,256]{1,0:T(8,128)(2,1)S(1)}, bf16[512,256]{1,0:T(8,128)(2,1)S(1)}, u32[]{:S(2)}, u32[]{:S(2)}) %collective-permute-start.8) | collective-permute-done | bytes 262176 | tf_op jit(solution)/shard_map/ppermute | solution.py:435
  76.3 0.7 collective-permute-start.10
  77.0 0.4 shard_map.72.keep_1
  77.4 0.8 %shard_map.73._ = bf16[512,1024]{1,0:T(8,128)(2,1)} custom-call(bf16[512,256]{1,0:T(8,128)(2,1)S(1)} %get-tuple-element.52.keep_0, bf16[512,256]{1,0:T(8,128)(2,1)S(1)} %shard_map.72.keep_1), custom_call_target="tpu_custom_call" | custom-call | tf_op jit(solution)/shard_map/pallas_call | solution.py:442
  78.2 2.3 %collective-permute-done.11.got_1 = bf16[512,256]{1,0:T(8,128)(2,1)S(1)} collective-permute-done((bf16[512,256]{1,0:T(8,128)(2,1)S(1)}, bf16[512,256]{1,0:T(8,128)(2,1)S(1)}, u32[]{:S(2)}, u32[]{:S(2)}) %collective-permute-start.11) | collective-permute-done | bytes 262176 | tf_op jit(solution)/shard_map/ppermute | solution.py:304
  80.6 0.0 collective-permute-done.10.late_0
  80.6 0.8 shard_map.74
  (1 shorter events, 0.0 us)
Async XLA Ops:
  0.0 9.6 %copy-start = (f32[512,1024]{1,0:T(8,128)S(1)}, f32[512,1024]{1,0:T(8,128)}, u32[]{:S(2)}) copy-start(f32[512,1024]{1,0:T(8,128)} %enc_ref.3) | copy-start | bytes 6291460
  0.0 7.6 %copy-start.4 = (s32[4]{0:T(128)S(1)}, s32[4]{0:T(128)}, u32[]{:S(2)}) copy-start(s32[4]{0:T(128)} %count_ref.1) | copy-start | bytes 52
  0.0 8.6 %copy-start.3 = (s32[4,16]{1,0:T(4,128)S(1)}, s32[4,16]{1,0:T(4,128)}, u32[]{:S(2)}) copy-start(s32[4,16]{1,0:T(4,128)} %list_ref.1) | copy-start | bytes 772
  3.0 9.2 %collective-permute-start = (bf16[272,512]{1,0:T(8,128)(2,1)}, bf16[272,512]{1,0:T(8,128)(2,1)S(1)}, u32[]{:S(2)}, u32[]{:S(2)}) collective-permute-start(bf16[272,512]{1,0:T(8,128)(2,1)} %get-tuple-element.31), channel_id=1, source_target_pairs={{0,1},{1,0},{2,3},{3,2},{4,5},{5,4},{6,7},{7,6},{8,9},{9,8},{10,11... | collective-permute-start | bytes 835592 | tf_op jit(solution)/shard_map/ppermute | solution.py:310
  5.0 9.6 %collective-permute-start.1 = (bf16[272,512]{1,0:T(8,128)(2,1)}, bf16[272,512]{1,0:T(8,128)(2,1)S(1)}, u32[]{:S(2)}, u32[]{:S(2)}) collective-permute-start(bf16[272,512]{1,0:T(8,128)(2,1)} %get-tuple-element.32), channel_id=1, source_target_pairs={{0,3},{1,2},{2,1},{3,0},{4,7},{5,6},{6,5},{7,4},{8,11},{9,10},{10,... | collective-permute-start | bytes 835592 | tf_op jit(solution)/shard_map/ppermute | solution.py:310
  7.6 4.4 %collective-permute-start.3 = (s32[4]{0:T(128)S(1)}, s32[4]{0:T(128)S(1)}, u32[]{:S(2)}, u32[]{:S(2)}) collective-permute-start(s32[4]{0:T(128)S(1)} %copy-done.4), channel_id=1, source_target_pairs={{0,1},{1,0},{2,3},{3,2},{4,7},{5,6},{6,5},{7,4},{8,9},{9,8},{10,11... | collective-permute-start | bytes 56 | tf_op jit(solution)/shard_map/ppermute | solution.py:304
  8.6 3.6 %collective-permute-start.2 = (s32[4,16]{1,0:T(4,128)S(1)}, s32[4,16]{1,0:T(4,128)S(1)}, u32[]{:S(2)}, u32[]{:S(2)}) collective-permute-start(s32[4,16]{1,0:T(4,128)S(1)} %copy-done.3), channel_id=1, source_target_pairs={{0,1},{1,0},{2,3},{3,2},{4,7},{5,6},{6,5},{7,4},{8,9},{9,8},{10,11... | collective-permute-start | bytes 776 | tf_op jit(solution)/shard_map/ppermute | solution.py:304
  9.6 1.0 %copy-start.1 = (bf16[512,512]{1,0:T(8,128)(2,1)S(1)}, bf16[512,512]{1,0:T(8,128)(2,1)}, u32[]{:S(2)}) copy-start(bf16[512,512]{1,0:T(8,128)(2,1)} %get-tuple-element.30.pick_ref) | copy-start | bytes 1572868
  10.6 4.6 %copy-start.2 = (bf16[16,512]{1,0:T(8,128)(2,1)S(1)}, bf16[16,512]{1,0:T(8,128)(2,1)}, u32[]{:S(2)}) copy-start(bf16[16,512]{1,0:T(8,128)(2,1)} %get-tuple-element.39.place_ref) | copy-start | bytes 49156
  12.0 4.5 %copy-start.5 = (s32[4]{0:T(128)}, s32[4]{0:T(128)S(1)}, u32[]{:S(2)}) copy-start(s32[4]{0:T(128)S(1)} %collective-permute-done.3.count_ref) | copy-start | bytes 52
  14.6 35.0 %collective-permute-start.4 = (bf16[4,16,128,128]{3,2,1,0:T(8,128)(2,1)}, bf16[4,16,128,128]{3,2,1,0:T(8,128)(2,1)}, u32[]{:S(2)}, u32[]{:S(2)}) collective-permute-start(bf16[4,16,128,128]{3,2,1,0:T(8,128)(2,1)} %weight_ref.1), channel_id=1, source_target_pairs={{0,1},{1,0},{2,3},{3,2},{4,7},{5,6},{6,5},{7,4},{8,9},{9,8},{10,11... | collective-permute-start | bytes 6291464 | tf_op jit(solution)/shard_map/ppermute | solution.py:304
  16.5 26.4 %all-to-all-start = ((bf16[32,16,1152]{2,1,0:T(8,128)(2,1)}), bf16[32,16,1152]{2,1,0:T(8,128)(2,1)S(1)}, u32[]{:S(2)}, u32[]{:S(2)}) async-start(bf16[32,16,1152]{2,1,0:T(8,128)(2,1)} %bitcast.1), calls=%async_computation | async-start | bytes 2359296 | tf_op jit(solution)/shard_map/all_to_all | solution.py:363
  43.0 10.6 %collective-permute-start.5 = (bf16[528,512]{1,0:T(8,128)(2,1)S(1)}, bf16[528,512]{1,0:T(8,128)(2,1)S(1)}, u32[]{:S(2)}, u32[]{:S(2)}) collective-permute-start(bf16[528,512]{1,0:T(8,128)(2,1)S(1)} %get-tuple-element.44.rows_ref.near_ref), channel_id=1, source_target_pairs={{0,3},{1,2},{2,1},{3,0},{4,5},{5,4},{6,7},{7,6},{8,11},{9,10},{10,... | collective-permute-start | bytes 1622024 | tf_op jit(solution)/shard_map/ppermute | solution.py:307
  45.4 13.9 %collective-permute-start.7 = (bf16[512,512]{1,0:T(8,128)(2,1)S(1)}, bf16[512,512]{1,0:T(8,128)(2,1)S(1)}, u32[]{:S(2)}, u32[]{:S(2)}) collective-permute-start(bf16[512,512]{1,0:T(8,128)(2,1)S(1)} %get-tuple-element.46.near_ref), channel_id=1, source_target_pairs={{0,3},{1,2},{2,1},{3,0},{4,5},{5,4},{6,7},{7,6},{8,11},{9,10},{10,... | collective-permute-start | bytes 1572872 | tf_op jit(solution)/shard_map/ppermute | solution.py:307
  48.4 1.3 %copy-start.6 = (s32[4]{0:T(128)S(1)}, s32[4]{0:T(128)}, u32[]{:S(2)}) copy-start(s32[4]{0:T(128)} %copy-done.5) | copy-start | bytes 52
  56.8 10.5 %collective-permute-start.6 = (bf16[1024,256]{1,0:T(8,128)(2,1)S(1)}, bf16[1024,256]{1,0:T(8,128)(2,1)S(1)}, u32[]{:S(2)}, u32[]{:S(2)}) collective-permute-start(bf16[1024,256]{1,0:T(8,128)(2,1)S(1)} %get-tuple-element.47.hidden_ref), channel_id=1, source_target_pairs={{0,3},{1,2},{2,1},{3,0},{4,5},{5,4},{6,7},{7,6},{8,11},{9,10},{10,... | collective-permute-start | bytes 1572872 | tf_op jit(solution)/shard_map/ppermute | solution.py:307
  61.6 12.1 %collective-permute-start.9 = (bf16[1024,256]{1,0:T(8,128)(2,1)S(1)}, bf16[1024,256]{1,0:T(8,128)(2,1)S(1)}, u32[]{:S(2)}, u32[]{:S(2)}) collective-permute-start(bf16[1024,256]{1,0:T(8,128)(2,1)S(1)} %get-tuple-element.49.hidden_ref), channel_id=1, source_target_pairs={{0,3},{1,2},{2,1},{3,0},{4,5},{5,4},{6,7},{7,6},{8,11},{9,10},{10,... | collective-permute-start | bytes 1572872 | tf_op jit(solution)/shard_map/ppermute | solution.py:307
  68.0 8.3 %collective-permute-start.8 = (bf16[512,256]{1,0:T(8,128)(2,1)S(1)}, bf16[512,256]{1,0:T(8,128)(2,1)S(1)}, u32[]{:S(2)}, u32[]{:S(2)}) collective-permute-start(bf16[512,256]{1,0:T(8,128)(2,1)S(1)} %get-tuple-element.50.after.sent_ref), channel_id=1, source_target_pairs={{0,1},{1,0},{2,3},{3,2},{8,9},{9,8},{10,11},{11,10},{16,17},{17,16... | collective-permute-start | bytes 786440 | tf_op jit(solution)/shard_map/ppermute | solution.py:435
  74.1 6.5 %collective-permute-start.11 = (bf16[512,256]{1,0:T(8,128)(2,1)S(1)}, bf16[512,256]{1,0:T(8,128)(2,1)S(1)}, u32[]{:S(2)}, u32[]{:S(2)}) collective-permute-start(bf16[512,256]{1,0:T(8,128)(2,1)S(1)} %shard_map.70.after_1.after), channel_id=1, source_target_pairs={{0,1},{1,0},{2,3},{3,2},{4,7},{5,6},{6,5},{7,4},{8,9},{9,8},{10,11... | collective-permute-start | bytes 786440 | tf_op jit(solution)/shard_map/ppermute | solution.py:304
  76.3 4.3 %collective-permute-start.10 = (bf16[512,256]{1,0:T(8,128)(2,1)S(1)}, bf16[512,256]{1,0:T(8,128)(2,1)S(1)}, u32[]{:S(2)}, u32[]{:S(2)}) collective-permute-start(bf16[512,256]{1,0:T(8,128)(2,1)S(1)} %shard_map.71), channel_id=1, source_target_pairs={{4,7},{5,6},{6,5},{7,4},{12,15},{13,14},{14,13},{15,12},{20,23},{2... | collective-permute-start | bytes 786440 | tf_op jit(solution)/shard_map/ppermute | solution.py:435

commit v7 on v6

--- a/solution.py
+++ b/solution.py
@@ -311,7 +311,7 @@
 
     far_blocks, far_count = to_row(nbr_blocks), to_row(nbr_count)
 
-    def dense_of(lists, count, weights, limit):
+    def dense_of(lists, count, weights, limit, work=0):
         return kernel_call(
             dense_kernel,
             (
@@ -320,7 +320,7 @@
                 jax.ShapeDtypeStruct((8, 128), f32),
             ),
             [SMEM, SMEM, ANY],
-            0,
+            work,
             8 << 20,
             scratch=[pltpu.VMEM(weights.shape, bf16), pltpu.SemaphoreType.DMA((blocks,))],
             limit=limit,
@@ -348,8 +348,8 @@
         scratch=[held, pltpu.SemaphoreType.DMA((2,))],
         limit=50,
     )(encoded, pick)
-    sent_weights, mine, row_0, row_1, far_blocks, far_count = lax.optimization_barrier(
-        (edge_weights, mine, row_0, row_1, far_blocks, far_count)
+    sent_weights, mine, far_blocks, far_count = lax.optimization_barrier(
+        (edge_weights, mine, far_blocks, far_count)
     )
     far_weights = to_row(sent_weights)
     packed = kernel_call(
@@ -361,7 +361,7 @@
     )(place, row_0, row_1, mine)
 
     packed = lax.all_to_all(packed, "dom", 0, 0, tiled=True)
-    dense_a, scale_a, token_a = dense_of(nbr_blocks, nbr_count, edge_weights, 50)
+    dense_a, scale_a, token_a = dense_of(nbr_blocks, nbr_count, edge_weights, 50, 40_000_000_000)
     near_rows = kernel_call(
         place_kernel,
         tuple(jax.ShapeDtypeStruct((rows + (16 if c == 0 else 0), 2 * w), bf16) for c, w in enumerate(WIDTHS)),

time: 81.9 us -> 81.8 us (level)
  waiting for transfers between devices: 30.6 us -> 28 us
  Pallas kernels: 24.1 us -> 25.1 us
    ppermute x2, waiting for transfers between devices: 2.43 us -> 0.89 us  [to_row_of(): lax.ppermute(a, AXES, [(d * depth + q, d * depth + (q ^ row_step(core)))...]
    all_to_all x1, waiting for transfers between devices: 16.4 us -> 15.3 us  [shards(): packed = lax.all_to_all(packed, 'dom', 0, 0, tiled=True)]
    pallas_call x2, Pallas kernels: 5.16 us -> 6.21 us  [dense_of(): kernel_call(dense_kernel, (jax.ShapeDtypeStruct((blocks * size, nodes), b...]
    ppermute x4, starting transfers between devices: 2.7 us -> 3.65 us  [to_row(): return lax.ppermute(a, AXES, row_pairs)]
    unnamed x14 -> x12, local copies, waits for them, and re-layouts: 1.07 us -> 1.71 us
  transfers between devices with their start and end apart: 13 -> 13, of which waited for: 9 -> 10; matrix products, arithmetic and copies ran while one was open for 0% -> 0% of each run, Pallas kernels for 25% -> 26%
where the time goes in v7:
time: 81.8 us; the launch traced here: 81.4 us
  waiting for transfers between devices  28 us (34%)
  starting transfers between devices  26.3 us (32%)
  Pallas kernels  25.1 us (31%)
  local copies, waits for them, and re-layouts  1.71 us (2%)
    all_to_all x1, waiting for transfers between devices, shards(): packed = lax.all_to_all(packed, 'dom', 0, 0, tiled=True)  15.3 us
    all_to_all x1, starting transfers between devices, shards(): packed = lax.all_to_all(packed, 'dom', 0, 0, tiled=True)  7.85 us
    ppermute x4, starting transfers between devices, to_col(): return lax.ppermute(a, AXES, col_pairs)  7.57 us
    ppermute x4, waiting for transfers between devices, to_col(): return lax.ppermute(a, AXES, col_pairs)  6.97 us
    pallas_call x2, Pallas kernels, dense_of(): kernel_call(dense_kernel, (jax.ShapeDtypeStruct((blocks * size, nodes), b...  6.21 us
    pallas_call x2, Pallas kernels, shards(): kernel_call(first_kernel, (jax.ShapeDtypeStruct((mine_n, part), bf16), ja...  4.71 us
    ppermute x2, starting transfers between devices, to_row_of(): lax.ppermute(a, AXES, [(d * depth + q, d * depth + (q ^ row_step(core)))...  4.61 us
    ppermute x4, starting transfers between devices, to_row(): return lax.ppermute(a, AXES, row_pairs)  3.65 us
  transfers between devices with their start and end apart: 13, of which 10 were waited for; matrix products, arithmetic and copies ran while one was open for 0% of the time, Pallas kernels for 26%

profile of v7, /device:TPU:0, one launch (start us, length us, event | category | flops | bytes accessed | tf_op | source)
XLA Modules:
  0.0 81.4 jit_solution(7488585481390885310)
XLA Ops:
  0.0 0.0 copy-start
  0.0 0.0 copy-start.4
  0.0 0.0 copy-start.3
  0.0 2.9 %shard_map.56 = (bf16[272,512]{1,0:T(8,128)(2,1)}, bf16[272,512]{1,0:T(8,128)(2,1)}, bf16[512,512]{1,0:T(8,128)(2,1)}, bf16[16,512]{1,0:T(8,128)(2,1)}) custom-call(s32[1,512]{1,0:T(1,128)} %bitcast.4, f32[512,1024]{1,0:T(8,128)} %enc_ref.3), custom_call_target="tpu_custom_call" | custom-call | flops 268435456 | bytes 4194304 | tf_op jit(solution)/shard_map/pallas_call | solution.py:331
  3.0 2.1 %collective-permute-start.3 = (bf16[272,512]{1,0:T(8,128)(2,1)}, bf16[272,512]{1,0:T(8,128)(2,1)S(1)}, u32[]{:S(2)}, u32[]{:S(2)}) collective-permute-start(bf16[272,512]{1,0:T(8,128)(2,1)} %get-tuple-element.36), channel_id=1, source_target_pairs={{0,1},{1,0},{2,3},{3,2},{4,5},{5,4},{6,7},{7,6},{8,9},{9,8},{10,11... | collective-permute-start | bytes 835592 | tf_op jit(solution)/shard_map/ppermute | solution.py:310
  5.0 2.5 %collective-permute-start.4 = (bf16[272,512]{1,0:T(8,128)(2,1)}, bf16[272,512]{1,0:T(8,128)(2,1)S(1)}, u32[]{:S(2)}, u32[]{:S(2)}) collective-permute-start(bf16[272,512]{1,0:T(8,128)(2,1)} %get-tuple-element.37), channel_id=1, source_target_pairs={{0,3},{1,2},{2,1},{3,0},{4,7},{5,6},{6,5},{7,4},{8,11},{9,10},{10,... | collective-permute-start | bytes 835592 | tf_op jit(solution)/shard_map/ppermute | solution.py:310
  7.6 0.0 copy-done.4
  7.6 1.0 %collective-permute-start.1 = (s32[4]{0:T(128)S(1)}, s32[4]{0:T(128)S(1)}, u32[]{:S(2)}, u32[]{:S(2)}) collective-permute-start(s32[4]{0:T(128)S(1)} %copy-done.4), channel_id=1, source_target_pairs={{0,1},{1,0},{2,3},{3,2},{4,7},{5,6},{6,5},{7,4},{8,9},{9,8},{10,11... | collective-permute-start | bytes 56 | tf_op jit(solution)/shard_map/ppermute | solution.py:304
  8.6 0.0 copy-done.3
  8.6 1.0 %collective-permute-start = (s32[4,16]{1,0:T(4,128)S(1)}, s32[4,16]{1,0:T(4,128)S(1)}, u32[]{:S(2)}, u32[]{:S(2)}) collective-permute-start(s32[4,16]{1,0:T(4,128)S(1)} %copy-done.3), channel_id=1, source_target_pairs={{0,1},{1,0},{2,3},{3,2},{4,7},{5,6},{6,5},{7,4},{8,9},{9,8},{10,11... | collective-permute-start | bytes 776 | tf_op jit(solution)/shard_map/ppermute | solution.py:304
  9.6 0.0 copy-done
  9.6 0.0 copy-start.1
  9.6 1.0 %copy-done.1 = bf16[512,512]{1,0:T(8,128)(2,1)S(1)} copy-done((bf16[512,512]{1,0:T(8,128)(2,1)S(1)}, bf16[512,512]{1,0:T(8,128)(2,1)}, u32[]{:S(2)}) %copy-start.1) | copy-done | bytes 524312
  10.6 0.0 copy-start.2
  10.6 1.0 %shard_map.57.mine_ref = bf16[512,512]{1,0:T(8,128)(2,1)S(1)} custom-call(f32[512,1024]{1,0:T(8,128)S(1)} %copy-done, bf16[512,512]{1,0:T(8,128)(2,1)S(1)} %copy-done.1), custom_call_target="tpu_custom_call" | custom-call | flops 268435456 | bytes 4194304 | tf_op jit(solution)/shard_map/pallas_call | solution.py:342
  11.7 0.3 collective-permute-done.1.count_ref
  12.0 0.2 collective-permute-done.list_ref
  12.2 1.5 %collective-permute-start.2 = (bf16[4,16,128,128]{3,2,1,0:T(8,128)(2,1)}, bf16[4,16,128,128]{3,2,1,0:T(8,128)(2,1)}, u32[]{:S(2)}, u32[]{:S(2)}) collective-permute-start(bf16[4,16,128,128]{3,2,1,0:T(8,128)(2,1)} %weight_ref.1), channel_id=1, source_target_pairs={{0,1},{1,0},{2,3},{3,2},{4,7},{5,6},{6,5},{7,4},{8,9},{9,8},{10,11... | collective-permute-start | bytes 6291464 | tf_op jit(solution)/shard_map/ppermute | solution.py:304
  13.7 0.0 collective-permute-done.3.row_0
  13.7 0.9 %collective-permute-done.4.row_1 = bf16[272,512]{1,0:T(8,128)(2,1)S(1)} collective-permute-done((bf16[272,512]{1,0:T(8,128)(2,1)}, bf16[272,512]{1,0:T(8,128)(2,1)S(1)}, u32[]{:S(2)}, u32[]{:S(2)}) %collective-permute-start.4) | collective-permute-done | bytes 278560 | tf_op jit(solution)/shard_map/ppermute | solution.py:310
  14.6 0.0 copy-done.2
  14.6 1.3 %shard_map.59 = bf16[512,1152]{1,0:T(8,128)(2,1)} custom-call(bf16[16,512]{1,0:T(8,128)(2,1)S(1)} %copy-done.2, bf16[272,512]{1,0:T(8,128)(2,1)S(1)} %collective-permute-done.3.row_0, bf16[272,512]{1,0:T(8,128)(2,1)S(1)} %collective-permute-done.4.row_1, bf16[512,512]{1,0:T(8,128)(2,1)S(1)} %shard_map.57.mine_ref), custom_call_target="tpu_custom_call" | custom-call | flops 1048576 | bytes 2097152 | tf_op jit(solution)/shard_map/pallas_call | solution.py:355
  15.9 7.8 %all-to-all-start = ((bf16[32,16,1152]{2,1,0:T(8,128)(2,1)}), bf16[32,16,1152]{2,1,0:T(8,128)(2,1)S(1)}, u32[]{:S(2)}, u32[]{:S(2)}) async-start(bf16[32,16,1152]{2,1,0:T(8,128)(2,1)} %bitcast.1), calls=%async_computation | async-start | bytes 2359296 | tf_op jit(solution)/shard_map/all_to_all | solution.py:363
  23.8 0.0 copy-start.5
  23.8 0.6 copy-done.5
  24.4 3.1 %shard_map.55 = (bf16[512,2048]{1,0:T(8,128)(2,1)S(1)}, f32[512,128]{1,0:T(8,128)S(1)}, f32[8,128]{1,0:T(8,128)S(1)}) custom-call(s32[4,16]{1,0:T(4,128)S(1)} %copy-done.3, s32[4]{0:T(128)S(1)} %copy-done.5, bf16[4,16,128,128]{3,2,1,0:T(8,128)(2,1)} %weight_ref.1), custom_call_target="tpu_custom_call" | custom-call | flops 40000000000 | bytes 8388608 | tf_op jit(solution)/shard_map/pallas_call | solution.py:315
  27.5 15.3 %all-to-all-done = bf16[32,16,1152]{2,1,0:T(8,128)(2,1)S(1)} async-done(((bf16[32,16,1152]{2,1,0:T(8,128)(2,1)}), bf16[32,16,1152]{2,1,0:T(8,128)(2,1)S(1)}, u32[]{:S(2)}, u32[]{:S(2)}) %all-to-all-start) | async-done | bytes 1179680 | tf_op jit(solution)/shard_map/all_to_all | solution.py:363
  42.8 0.2 shard_map.60
  42.9 2.0 %collective-permute-start.5 = (bf16[528,512]{1,0:T(8,128)(2,1)S(1)}, bf16[528,512]{1,0:T(8,128)(2,1)S(1)}, u32[]{:S(2)}, u32[]{:S(2)}) collective-permute-start(bf16[528,512]{1,0:T(8,128)(2,1)S(1)} %get-tuple-element.40.rows_ref.near_ref), channel_id=1, source_target_pairs={{0,3},{1,2},{2,1},{3,0},{4,5},{5,4},{6,7},{7,6},{8,11},{9,10},{10,... | collective-permute-start | bytes 1622024 | tf_op jit(solution)/shard_map/ppermute | solution.py:307
  44.9 1.2 %collective-permute-start.7 = (bf16[512,512]{1,0:T(8,128)(2,1)S(1)}, bf16[512,512]{1,0:T(8,128)(2,1)S(1)}, u32[]{:S(2)}, u32[]{:S(2)}) collective-permute-start(bf16[512,512]{1,0:T(8,128)(2,1)S(1)} %get-tuple-element.42.near_ref), channel_id=1, source_target_pairs={{0,3},{1,2},{2,1},{3,0},{4,5},{5,4},{6,7},{7,6},{8,11},{9,10},{10,... | collective-permute-start | bytes 1572872 | tf_op jit(solution)/shard_map/ppermute | solution.py:307
  46.2 0.8 shard_map.61.pick_ref
  47.0 1.3 %shard_map.62.refs_1_.part_ref = bf16[2048,256]{1,0:T(8,128)(2,1)S(1)} custom-call(bf16[2,2048,512]{2,1,0:T(8,128)(2,1)S(1)} %shard_map.61.pick_ref, bf16[528,512]{1,0:T(8,128)(2,1)S(1)} %get-tuple-element.40.rows_ref.near_ref), custom_call_target="tpu_custom_call" | custom-call | flops 1073741824 | bytes 4194304 | tf_op jit(solution)/shard_map/pallas_call | solution.py:387
  48.3 1.2 %shard_map.63.refs_2_.part_ref = bf16[2048,256]{1,0:T(8,128)(2,1)S(1)} custom-call(bf16[2,2048,512]{2,1,0:T(8,128)(2,1)S(1)} %shard_map.61.pick_ref, bf16[512,512]{1,0:T(8,128)(2,1)S(1)} %get-tuple-element.42.near_ref), custom_call_target="tpu_custom_call" | custom-call | flops 1073741824 | bytes 4194304 | tf_op jit(solution)/shard_map/pallas_call | solution.py:387
  49.5 0.0 collective-permute-done.2.weight_ref
  49.5 3.1 %shard_map.58 = (bf16[512,2048]{1,0:T(8,128)(2,1)S(1)}, f32[512,128]{1,0:T(8,128)S(1)}, f32[8,128]{1,0:T(8,128)S(1)}) custom-call(s32[4,16]{1,0:T(4,128)S(1)} %collective-permute-done.list_ref, s32[4]{0:T(128)S(1)} %collective-permute-done.1.count_ref, bf16[4,16,128,128]{3,2,1,0:T(8,128)(2,1)} %collective-permute-done.2.weight_ref), custom_call_target="tpu_custom_call" | custom-call | bytes 8388608 | tf_op jit(solution)/shard_map/pallas_call | solution.py:315
  52.7 0.9 %collective-permute-done.5.rows_ref.far_ref = bf16[528,512]{1,0:T(8,128)(2,1)S(1)} collective-permute-done((bf16[528,512]{1,0:T(8,128)(2,1)S(1)}, bf16[528,512]{1,0:T(8,128)(2,1)S(1)}, u32[]{:S(2)}, u32[]{:S(2)}) %collective-permute-start.5) | collective-permute-done | bytes 540704 | tf_op jit(solution)/shard_map/ppermute | solution.py:307
  53.5 0.8 shard_map.64.pick_ref
  54.3 2.4 %shard_map.65 = (bf16[1024,256]{1,0:T(8,128)(2,1)S(1)}, bf16[1024,256]{1,0:T(8,128)(2,1)S(1)}) custom-call(bf16[512,2048]{1,0:T(8,128)(2,1)S(1)} %get-tuple-element.27.dense_a.dense, bf16[512,2048]{1,0:T(8,128)(2,1)S(1)} %get-tuple-element.32.dense_b.dense, f32[512,128]{1,0:T(8,128)S(1)} %get-tuple-element.33.scale_a.scale, ...), custom_call_target="tpu_custom_call" | custom-call | flops 2147483648 | bytes 4194304 | tf_op jit(solution)/shard_map/pallas_call | solution.py:401
  56.7 2.1 %collective-permute-start.6 = (bf16[1024,256]{1,0:T(8,128)(2,1)S(1)}, bf16[1024,256]{1,0:T(8,128)(2,1)S(1)}, u32[]{:S(2)}, u32[]{:S(2)}) collective-permute-start(bf16[1024,256]{1,0:T(8,128)(2,1)S(1)} %get-tuple-element.43.hidden_ref), channel_id=1, source_target_pairs={{0,3},{1,2},{2,1},{3,0},{4,5},{5,4},{6,7},{7,6},{8,11},{9,10},{10,... | collective-permute-start | bytes 1572872 | tf_op jit(solution)/shard_map/ppermute | solution.py:307
  58.8 0.4 collective-permute-done.7.far_ref
  59.1 2.4 %shard_map.67 = (bf16[1024,256]{1,0:T(8,128)(2,1)S(1)}, bf16[1024,256]{1,0:T(8,128)(2,1)S(1)}) custom-call(bf16[512,2048]{1,0:T(8,128)(2,1)S(1)} %get-tuple-element.27.dense_a.dense, bf16[512,2048]{1,0:T(8,128)(2,1)S(1)} %get-tuple-element.32.dense_b.dense, f32[512,128]{1,0:T(8,128)S(1)} %get-tuple-element.33.scale_a.scale, ...), custom_call_target="tpu_custom_call" | custom-call | flops 2147483648 | bytes 4194304 | tf_op jit(solution)/shard_map/pallas_call | solution.py:401
  61.5 2.3 %collective-permute-start.9 = (bf16[1024,256]{1,0:T(8,128)(2,1)S(1)}, bf16[1024,256]{1,0:T(8,128)(2,1)S(1)}, u32[]{:S(2)}, u32[]{:S(2)}) collective-permute-start(bf16[1024,256]{1,0:T(8,128)(2,1)S(1)} %get-tuple-element.45.hidden_ref), channel_id=1, source_target_pairs={{0,3},{1,2},{2,1},{3,0},{4,5},{5,4},{6,7},{7,6},{8,11},{9,10},{10,... | collective-permute-start | bytes 1572872 | tf_op jit(solution)/shard_map/ppermute | solution.py:307
  63.8 0.7 shard_map.68.after.total_ref
  64.5 0.7 shard_map.66.total_ref
  65.2 2.0 %collective-permute-done.6.hidden_ref = bf16[1024,256]{1,0:T(8,128)(2,1)S(1)} collective-permute-done((bf16[1024,256]{1,0:T(8,128)(2,1)S(1)}, bf16[1024,256]{1,0:T(8,128)(2,1)S(1)}, u32[]{:S(2)}, u32[]{:S(2)}) %collective-permute-start.6) | collective-permute-done | bytes 524320 | tf_op jit(solution)/shard_map/ppermute | solution.py:307
  67.2 0.7 shard_map.69
  67.9 1.9 %collective-permute-start.8 = (bf16[512,256]{1,0:T(8,128)(2,1)S(1)}, bf16[512,256]{1,0:T(8,128)(2,1)S(1)}, u32[]{:S(2)}, u32[]{:S(2)}) collective-permute-start(bf16[512,256]{1,0:T(8,128)(2,1)S(1)} %get-tuple-element.46.after.sent_ref), channel_id=1, source_target_pairs={{0,1},{1,0},{2,3},{3,2},{8,9},{9,8},{10,11},{11,10},{16,17},{17,16... | collective-permute-start | bytes 786440 | tf_op jit(solution)/shard_map/ppermute | solution.py:435
  69.8 3.7 %collective-permute-done.9.hidden_ref = bf16[1024,256]{1,0:T(8,128)(2,1)S(1)} collective-permute-done((bf16[1024,256]{1,0:T(8,128)(2,1)S(1)}, bf16[1024,256]{1,0:T(8,128)(2,1)S(1)}, u32[]{:S(2)}, u32[]{:S(2)}) %collective-permute-start.9) | collective-permute-done | bytes 524320 | tf_op jit(solution)/shard_map/ppermute | solution.py:307
  73.6 0.4 shard_map.70.after_1.after
  74.0 0.1 collective-permute-start.11
  74.1 2.1 %collective-permute-done.8.after_0.early_0 = bf16[512,256]{1,0:T(8,128)(2,1)S(1)} collective-permute-done((bf16[512,256]{1,0:T(8,128)(2,1)S(1)}, bf16[512,256]{1,0:T(8,128)(2,1)S(1)}, u32[]{:S(2)}, u32[]{:S(2)}) %collective-permute-start.8) | collective-permute-done | bytes 262176 | tf_op jit(solution)/shard_map/ppermute | solution.py:435
  76.2 0.7 collective-permute-start.10
  76.9 0.4 shard_map.72.keep_1
  77.3 0.8 %shard_map.73._ = bf16[512,1024]{1,0:T(8,128)(2,1)} custom-call(bf16[512,256]{1,0:T(8,128)(2,1)S(1)} %get-tuple-element.48.keep_0, bf16[512,256]{1,0:T(8,128)(2,1)S(1)} %shard_map.72.keep_1), custom_call_target="tpu_custom_call" | custom-call | tf_op jit(solution)/shard_map/pallas_call | solution.py:442
  78.2 2.3 %collective-permute-done.11.got_1 = bf16[512,256]{1,0:T(8,128)(2,1)S(1)} collective-permute-done((bf16[512,256]{1,0:T(8,128)(2,1)S(1)}, bf16[512,256]{1,0:T(8,128)(2,1)S(1)}, u32[]{:S(2)}, u32[]{:S(2)}) %collective-permute-start.11) | collective-permute-done | bytes 262176 | tf_op jit(solution)/shard_map/ppermute | solution.py:304
  80.5 0.0 collective-permute-done.10.late_0
  80.5 0.8 shard_map.74
  (1 shorter events, 0.0 us)
Async XLA Ops:
  0.0 9.6 %copy-start = (f32[512,1024]{1,0:T(8,128)S(1)}, f32[512,1024]{1,0:T(8,128)}, u32[]{:S(2)}) copy-start(f32[512,1024]{1,0:T(8,128)} %enc_ref.3) | copy-start | bytes 6291460
  0.0 7.6 %copy-start.4 = (s32[4]{0:T(128)S(1)}, s32[4]{0:T(128)}, u32[]{:S(2)}) copy-start(s32[4]{0:T(128)} %count_ref.1) | copy-start | bytes 52
  0.0 8.6 %copy-start.3 = (s32[4,16]{1,0:T(4,128)S(1)}, s32[4,16]{1,0:T(4,128)}, u32[]{:S(2)}) copy-start(s32[4,16]{1,0:T(4,128)} %list_ref.1) | copy-start | bytes 772
  3.0 10.8 %collective-permute-start.3 = (bf16[272,512]{1,0:T(8,128)(2,1)}, bf16[272,512]{1,0:T(8,128)(2,1)S(1)}, u32[]{:S(2)}, u32[]{:S(2)}) collective-permute-start(bf16[272,512]{1,0:T(8,128)(2,1)} %get-tuple-element.36), channel_id=1, source_target_pairs={{0,1},{1,0},{2,3},{3,2},{4,5},{5,4},{6,7},{7,6},{8,9},{9,8},{10,11... | collective-permute-start | bytes 835592 | tf_op jit(solution)/shard_map/ppermute | solution.py:310
  5.0 9.6 %collective-permute-start.4 = (bf16[272,512]{1,0:T(8,128)(2,1)}, bf16[272,512]{1,0:T(8,128)(2,1)S(1)}, u32[]{:S(2)}, u32[]{:S(2)}) collective-permute-start(bf16[272,512]{1,0:T(8,128)(2,1)} %get-tuple-element.37), channel_id=1, source_target_pairs={{0,3},{1,2},{2,1},{3,0},{4,7},{5,6},{6,5},{7,4},{8,11},{9,10},{10,... | collective-permute-start | bytes 835592 | tf_op jit(solution)/shard_map/ppermute | solution.py:310
  7.6 4.4 %collective-permute-start.1 = (s32[4]{0:T(128)S(1)}, s32[4]{0:T(128)S(1)}, u32[]{:S(2)}, u32[]{:S(2)}) collective-permute-start(s32[4]{0:T(128)S(1)} %copy-done.4), channel_id=1, source_target_pairs={{0,1},{1,0},{2,3},{3,2},{4,7},{5,6},{6,5},{7,4},{8,9},{9,8},{10,11... | collective-permute-start | bytes 56 | tf_op jit(solution)/shard_map/ppermute | solution.py:304
  8.6 3.6 %collective-permute-start = (s32[4,16]{1,0:T(4,128)S(1)}, s32[4,16]{1,0:T(4,128)S(1)}, u32[]{:S(2)}, u32[]{:S(2)}) collective-permute-start(s32[4,16]{1,0:T(4,128)S(1)} %copy-done.3), channel_id=1, source_target_pairs={{0,1},{1,0},{2,3},{3,2},{4,7},{5,6},{6,5},{7,4},{8,9},{9,8},{10,11... | collective-permute-start | bytes 776 | tf_op jit(solution)/shard_map/ppermute | solution.py:304
  9.6 1.0 %copy-start.1 = (bf16[512,512]{1,0:T(8,128)(2,1)S(1)}, bf16[512,512]{1,0:T(8,128)(2,1)}, u32[]{:S(2)}) copy-start(bf16[512,512]{1,0:T(8,128)(2,1)} %get-tuple-element.28.pick_ref) | copy-start | bytes 1572868
  10.6 4.0 %copy-start.2 = (bf16[16,512]{1,0:T(8,128)(2,1)S(1)}, bf16[16,512]{1,0:T(8,128)(2,1)}, u32[]{:S(2)}) copy-start(bf16[16,512]{1,0:T(8,128)(2,1)} %get-tuple-element.35.place_ref) | copy-start | bytes 49156
  12.2 37.4 %collective-permute-start.2 = (bf16[4,16,128,128]{3,2,1,0:T(8,128)(2,1)}, bf16[4,16,128,128]{3,2,1,0:T(8,128)(2,1)}, u32[]{:S(2)}, u32[]{:S(2)}) collective-permute-start(bf16[4,16,128,128]{3,2,1,0:T(8,128)(2,1)} %weight_ref.1), channel_id=1, source_target_pairs={{0,1},{1,0},{2,3},{3,2},{4,7},{5,6},{6,5},{7,4},{8,9},{9,8},{10,11... | collective-permute-start | bytes 6291464 | tf_op jit(solution)/shard_map/ppermute | solution.py:304
  15.9 26.9 %all-to-all-start = ((bf16[32,16,1152]{2,1,0:T(8,128)(2,1)}), bf16[32,16,1152]{2,1,0:T(8,128)(2,1)S(1)}, u32[]{:S(2)}, u32[]{:S(2)}) async-start(bf16[32,16,1152]{2,1,0:T(8,128)(2,1)} %bitcast.1), calls=%async_computation | async-start | bytes 2359296 | tf_op jit(solution)/shard_map/all_to_all | solution.py:363
  23.8 0.7 copy-start.5
  42.9 10.6 %collective-permute-start.5 = (bf16[528,512]{1,0:T(8,128)(2,1)S(1)}, bf16[528,512]{1,0:T(8,128)(2,1)S(1)}, u32[]{:S(2)}, u32[]{:S(2)}) collective-permute-start(bf16[528,512]{1,0:T(8,128)(2,1)S(1)} %get-tuple-element.40.rows_ref.near_ref), channel_id=1, source_target_pairs={{0,3},{1,2},{2,1},{3,0},{4,5},{5,4},{6,7},{7,6},{8,11},{9,10},{10,... | collective-permute-start | bytes 1622024 | tf_op jit(solution)/shard_map/ppermute | solution.py:307
  44.9 14.2 %collective-permute-start.7 = (bf16[512,512]{1,0:T(8,128)(2,1)S(1)}, bf16[512,512]{1,0:T(8,128)(2,1)S(1)}, u32[]{:S(2)}, u32[]{:S(2)}) collective-permute-start(bf16[512,512]{1,0:T(8,128)(2,1)S(1)} %get-tuple-element.42.near_ref), channel_id=1, source_target_pairs={{0,3},{1,2},{2,1},{3,0},{4,5},{5,4},{6,7},{7,6},{8,11},{9,10},{10,... | collective-permute-start | bytes 1572872 | tf_op jit(solution)/shard_map/ppermute | solution.py:307
  56.7 10.5 %collective-permute-start.6 = (bf16[1024,256]{1,0:T(8,128)(2,1)S(1)}, bf16[1024,256]{1,0:T(8,128)(2,1)S(1)}, u32[]{:S(2)}, u32[]{:S(2)}) collective-permute-start(bf16[1024,256]{1,0:T(8,128)(2,1)S(1)} %get-tuple-element.43.hidden_ref), channel_id=1, source_target_pairs={{0,3},{1,2},{2,1},{3,0},{4,5},{5,4},{6,7},{7,6},{8,11},{9,10},{10,... | collective-permute-start | bytes 1572872 | tf_op jit(solution)/shard_map/ppermute | solution.py:307
  61.5 12.1 %collective-permute-start.9 = (bf16[1024,256]{1,0:T(8,128)(2,1)S(1)}, bf16[1024,256]{1,0:T(8,128)(2,1)S(1)}, u32[]{:S(2)}, u32[]{:S(2)}) collective-permute-start(bf16[1024,256]{1,0:T(8,128)(2,1)S(1)} %get-tuple-element.45.hidden_ref), channel_id=1, source_target_pairs={{0,3},{1,2},{2,1},{3,0},{4,5},{5,4},{6,7},{7,6},{8,11},{9,10},{10,... | collective-permute-start | bytes 1572872 | tf_op jit(solution)/shard_map/ppermute | solution.py:307
  67.9 8.3 %collective-permute-start.8 = (bf16[512,256]{1,0:T(8,128)(2,1)S(1)}, bf16[512,256]{1,0:T(8,128)(2,1)S(1)}, u32[]{:S(2)}, u32[]{:S(2)}) collective-permute-start(bf16[512,256]{1,0:T(8,128)(2,1)S(1)} %get-tuple-element.46.after.sent_ref), channel_id=1, source_target_pairs={{0,1},{1,0},{2,3},{3,2},{8,9},{9,8},{10,11},{11,10},{16,17},{17,16... | collective-permute-start | bytes 786440 | tf_op jit(solution)/shard_map/ppermute | solution.py:435
  74.0 6.5 %collective-permute-start.11 = (bf16[512,256]{1,0:T(8,128)(2,1)S(1)}, bf16[512,256]{1,0:T(8,128)(2,1)S(1)}, u32[]{:S(2)}, u32[]{:S(2)}) collective-permute-start(bf16[512,256]{1,0:T(8,128)(2,1)S(1)} %shard_map.70.after_1.after), channel_id=1, source_target_pairs={{0,1},{1,0},{2,3},{3,2},{4,7},{5,6},{6,5},{7,4},{8,9},{9,8},{10,11... | collective-permute-start | bytes 786440 | tf_op jit(solution)/shard_map/ppermute | solution.py:304
  76.2 4.3 %collective-permute-start.10 = (bf16[512,256]{1,0:T(8,128)(2,1)S(1)}, bf16[512,256]{1,0:T(8,128)(2,1)S(1)}, u32[]{:S(2)}, u32[]{:S(2)}) collective-permute-start(bf16[512,256]{1,0:T(8,128)(2,1)S(1)} %shard_map.71), channel_id=1, source_target_pairs={{4,7},{5,6},{6,5},{7,4},{12,15},{13,14},{14,13},{15,12},{20,23},{2... | collective-permute-start | bytes 786440 | tf_op jit(solution)/shard_map/ppermute | solution.py:435

commit v8 on v7

--- a/solution.py
+++ b/solution.py
@@ -115,13 +115,20 @@
             mine_ref[by_dom(core, block, per), :] = part[block * per : (block + 1) * per, :]
 
 
-def pack_kernel(per, place_ref, row_0, row_1, mine_ref, packed_ref):
-    half = row_0.shape[1]
-    size = row_0.shape[0] - 16
+def pack_kernel(per, place_ref, row_0, row_1, mine_ref, packed_ref, stage, sems):
+    rows, half = stage.shape[0], row_0.shape[1]
+    size = rows // 2
+    copies = []
+
+    def send(source, target):
+        copies.append(pltpu.make_async_copy(source, target, sems.at[len(copies)]))
+        copies[-1].start()
+
+    for to, start, wide in pieces(True):
+        send(mine_ref.at[:, pl.ds(start, wide)], packed_ref.at[:, pl.ds(to, wide)])
     line = lax.broadcasted_iota(jnp.int32, (16, 128), 0)
     lane = lax.broadcasted_iota(jnp.int32, (16, 128), 1)
-    for to, start, wide in pieces(True):
-        packed_ref[:, to : to + wide] = mine_ref[:, start : start + wide]
+    ids = []
     for core, row in enumerate((row_0, row_1)):
         total = jnp.zeros((size, 128), jnp.float32)
         for n, lines in enumerate((place_ref[:, core * size : (core + 1) * size], row[size:, :size])):
@@ -129,13 +136,21 @@
             total += lax.dot_general(
                 lines, spread, (((0,), (0,)), ((), ())), preferred_element_type=jnp.float32
             )
-        total = total.astype(jnp.bfloat16)
-        for block in range(size // per):
-            at = by_dom(core, block, per)
+        ids.append(total.astype(jnp.bfloat16))
+    chips = size // per
+    for part in range(2):
+        for block in range(part * chips // 2, (part + 1) * chips // 2):
             span = slice(block * per, (block + 1) * per)
-            for to, start, wide in pieces(False):
-                packed_ref[at, to : to + wide] = row[span, start : start + wide]
-            packed_ref[at, 2 * half :] = total[span, :]
+            for core, row in enumerate((row_0, row_1)):
+                at = by_dom(core, block, per)
+                stage[at, :half] = row[span, :]
+                stage[at, half:] = ids[core][span, :]
+        some = pl.ds(part * size, size)
+        for n, (to, start, wide) in enumerate(pieces(False)):
+            wide += 128 if n == len(WIDTHS) - 1 else 0
+            send(stage.at[some, pl.ds(start, wide)], packed_ref.at[some, pl.ds(to, wide)])
+    for copy in copies:
+        copy.wait()
 
 
 def place_kernel(arrived_ref, token, *outs):
@@ -239,12 +254,6 @@
     depth = hidden_ref.shape[0]
     total = total_ref[at, :] + jnp.dot(dense[:, depth:], hidden_ref[...], preferred_element_type=jnp.float32)
     out[...] = (MIX * base_ref[at, :].astype(jnp.float32) + total * scale[:, 0:1]).astype(jnp.bfloat16)
-
-
-def last_kernel(dense_a, dense_b, scale_a, scale_b, total_ref, hidden_ref, base_ref, after, keep_ref, send_ref):
-    size = dense_a.shape[0]
-    finish(dense_b, scale_b, total_ref, hidden_ref, base_ref, pl.ds(size, size), send_ref)
-    finish(dense_a, scale_a, total_ref, hidden_ref, base_ref, pl.ds(0, size), keep_ref)
 
 
 def side_kernel(row, dense, scale, total_ref, hidden_ref, base_ref, after, out_ref):
@@ -352,12 +361,14 @@
         (edge_weights, mine, far_blocks, far_count)
     )
     far_weights = to_row(sent_weights)
-    packed = kernel_call(
+    packed = pl.pallas_call(
         functools.partial(pack_kernel, per),
-        jax.ShapeDtypeStruct((rows, width + 128), bf16),
-        [VMEM] * 4,
-        1 << 20,
-        2 << 20,
+        out_shape=jax.ShapeDtypeStruct((rows, width + 128), bf16),
+        in_specs=[VMEM] * 3 + [ANY],
+        out_specs=ANY,
+        scratch_shapes=[pltpu.VMEM((rows, half + 128), bf16), pltpu.SemaphoreType.DMA((3 * len(WIDTHS),))],
+        compiler_params=pltpu.CompilerParams(vmem_limit_bytes=10 << 20),
+        cost_estimate=pl.CostEstimate(flops=1 << 20, bytes_accessed=2 << 20, transcendentals=0),
     )(place, row_0, row_1, mine)
 
     packed = lax.all_to_all(packed, "dom", 0, 0, tiled=True)
@@ -419,17 +430,17 @@
     part = WIDTHS[0]
     out_shape = jax.ShapeDtypeStruct((rows, part), bf16)
     work = 2 * rows * mine_n * part
-    keep_0, send_0 = kernel_call(last_kernel, (out_shape,) * 2, [VMEM] * 7 + [ANY], 2 * work, 4 << 20)(
-        dense_a, dense_b, scale_a, scale_b, *steps[0], steps[1][0]
-    )
-    sides = []
-    for row, dense, scale, after in ((1, dense_b, scale_b, send_0), (0, dense_a, scale_a, None)):
-        sides.append(
-            kernel_call(
-                functools.partial(side_kernel, row), out_shape, [VMEM] * 5 + [ANY], work, 2 << 20
-            )(dense, scale, *steps[1], sides[0] if after is None else after)
+    def side(row, step, after):
+        dense, scale = ((dense_a, scale_a), (dense_b, scale_b))[row]
+        return kernel_call(functools.partial(side_kernel, row), out_shape, [VMEM] * 5 + [ANY], work, 2 << 20)(
+            dense, scale, *steps[step], after
         )
-    kept, sent = [keep_0, sides[1]], [send_0, sides[0]]
+
+    send_0 = side(1, 0, steps[1][0])
+    keep_0 = side(0, 0, send_0)
+    send_1 = side(1, 1, keep_0)
+    keep_1 = side(0, 1, send_1)
+    kept, sent = [keep_0, keep_1], [send_0, send_1]
 
     def to_row_on(core, a):
         return lax.ppermute(a, AXES, [(p, q) for p, q in row_pairs if p // depth % 2 == core])

time: 81.8 us -> 81.6 us (level)
  Pallas kernels: 25.1 us -> 24 us
  waiting for transfers between devices: 28 us -> 29 us
    pallas_call x2, Pallas kernels: 6.21 us -> 5.09 us  [dense_of(): kernel_call(dense_kernel, (jax.ShapeDtypeStruct((blocks * size, nodes), b...]
    pallas_call x4 -> x5, Pallas kernels: 2.93 us -> 2.92 us  [the longest x4 1.76 us: side(): kernel_call(functools.partial(side_kernel, row), out_shape, [VMEM] * 5 +...]
  transfers between devices with their start and end apart: 13 -> 13, of which waited for: 10 -> 10; matrix products, arithmetic and copies ran while one was open for 0% -> 0% of each run, Pallas kernels for 26% -> 25%
where the time goes in v8:
time: 81.6 us; the launch traced here: 81.3 us
  waiting for transfers between devices  29 us (36%)
  starting transfers between devices  26.3 us (32%)
  Pallas kernels  24 us (29%)
  local copies, waits for them, and re-layouts  1.71 us (2%)
    all_to_all x1, waiting for transfers between devices, shards(): packed = lax.all_to_all(packed, 'dom', 0, 0, tiled=True)  15.8 us
    all_to_all x1, starting transfers between devices, shards(): packed = lax.all_to_all(packed, 'dom', 0, 0, tiled=True)  7.86 us
    ppermute x4, starting transfers between devices, to_col(): return lax.ppermute(a, AXES, col_pairs)  7.57 us
    ppermute x4, waiting for transfers between devices, to_col(): return lax.ppermute(a, AXES, col_pairs)  7.43 us
    pallas_call x2, Pallas kernels, dense_of(): kernel_call(dense_kernel, (jax.ShapeDtypeStruct((blocks * size, nodes), b...  5.09 us
    pallas_call x2, Pallas kernels, shards(): kernel_call(first_kernel, (jax.ShapeDtypeStruct((mine_n, part), bf16), ja...  4.71 us
    ppermute x2, starting transfers between devices, to_row_of(): lax.ppermute(a, AXES, [(d * depth + q, d * depth + (q ^ row_step(core)))...  4.61 us
    ppermute x4, starting transfers between devices, to_row(): return lax.ppermute(a, AXES, row_pairs)  3.65 us
  transfers between devices with their start and end apart: 13, of which 10 were waited for; matrix products, arithmetic and copies ran while one was open for 0% of the time, Pallas kernels for 25%

profile of v8, /device:TPU:0, one launch (start us, length us, event | category | flops | bytes accessed | tf_op | source)
XLA Modules:
  0.0 81.3 jit_solution(6810789129093946398)
XLA Ops:
  0.0 0.0 copy-start
  0.0 0.0 copy-start.4
  0.0 0.0 copy-start.3
  0.0 2.9 %shard_map.55 = (bf16[272,512]{1,0:T(8,128)(2,1)}, bf16[272,512]{1,0:T(8,128)(2,1)}, bf16[512,512]{1,0:T(8,128)(2,1)}, bf16[16,512]{1,0:T(8,128)(2,1)}) custom-call(s32[1,512]{1,0:T(1,128)} %bitcast.4, f32[512,1024]{1,0:T(8,128)} %enc_ref.3), custom_call_target="tpu_custom_call" | custom-call | flops 268435456 | bytes 4194304 | tf_op jit(solution)/shard_map/pallas_call | solution.py:340
  3.0 2.1 %collective-permute-start.3 = (bf16[272,512]{1,0:T(8,128)(2,1)}, bf16[272,512]{1,0:T(8,128)(2,1)S(1)}, u32[]{:S(2)}, u32[]{:S(2)}) collective-permute-start(bf16[272,512]{1,0:T(8,128)(2,1)} %get-tuple-element.34), channel_id=1, source_target_pairs={{0,1},{1,0},{2,3},{3,2},{4,5},{5,4},{6,7},{7,6},{8,9},{9,8},{10,11... | collective-permute-start | bytes 835592 | tf_op jit(solution)/shard_map/ppermute | solution.py:319
  5.0 2.5 %collective-permute-start.4 = (bf16[272,512]{1,0:T(8,128)(2,1)}, bf16[272,512]{1,0:T(8,128)(2,1)S(1)}, u32[]{:S(2)}, u32[]{:S(2)}) collective-permute-start(bf16[272,512]{1,0:T(8,128)(2,1)} %get-tuple-element.35), channel_id=1, source_target_pairs={{0,3},{1,2},{2,1},{3,0},{4,7},{5,6},{6,5},{7,4},{8,11},{9,10},{10,... | collective-permute-start | bytes 835592 | tf_op jit(solution)/shard_map/ppermute | solution.py:319
  7.6 0.0 copy-done.4
  7.6 1.0 %collective-permute-start.1 = (s32[4]{0:T(128)S(1)}, s32[4]{0:T(128)S(1)}, u32[]{:S(2)}, u32[]{:S(2)}) collective-permute-start(s32[4]{0:T(128)S(1)} %copy-done.4), channel_id=1, source_target_pairs={{0,1},{1,0},{2,3},{3,2},{4,7},{5,6},{6,5},{7,4},{8,9},{9,8},{10,11... | collective-permute-start | bytes 56 | tf_op jit(solution)/shard_map/ppermute | solution.py:313
  8.6 0.0 copy-done.3
  8.6 1.0 %collective-permute-start = (s32[4,16]{1,0:T(4,128)S(1)}, s32[4,16]{1,0:T(4,128)S(1)}, u32[]{:S(2)}, u32[]{:S(2)}) collective-permute-start(s32[4,16]{1,0:T(4,128)S(1)} %copy-done.3), channel_id=1, source_target_pairs={{0,1},{1,0},{2,3},{3,2},{4,7},{5,6},{6,5},{7,4},{8,9},{9,8},{10,11... | collective-permute-start | bytes 776 | tf_op jit(solution)/shard_map/ppermute | solution.py:313
  9.6 0.0 copy-done
  9.6 0.0 copy-start.1
  9.6 1.0 %copy-done.1 = bf16[512,512]{1,0:T(8,128)(2,1)S(1)} copy-done((bf16[512,512]{1,0:T(8,128)(2,1)S(1)}, bf16[512,512]{1,0:T(8,128)(2,1)}, u32[]{:S(2)}) %copy-start.1) | copy-done | bytes 524312
  10.6 0.0 copy-start.2
  10.6 1.0 %shard_map.56.mine_ref = bf16[512,512]{1,0:T(8,128)(2,1)S(1)} custom-call(f32[512,1024]{1,0:T(8,128)S(1)} %copy-done, bf16[512,512]{1,0:T(8,128)(2,1)S(1)} %copy-done.1), custom_call_target="tpu_custom_call" | custom-call | flops 268435456 | bytes 4194304 | tf_op jit(solution)/shard_map/pallas_call | solution.py:351
  11.7 0.3 collective-permute-done.1.count_ref
  12.0 0.2 collective-permute-done.list_ref
  12.2 1.5 %collective-permute-start.2 = (bf16[4,16,128,128]{3,2,1,0:T(8,128)(2,1)}, bf16[4,16,128,128]{3,2,1,0:T(8,128)(2,1)}, u32[]{:S(2)}, u32[]{:S(2)}) collective-permute-start(bf16[4,16,128,128]{3,2,1,0:T(8,128)(2,1)} %weight_ref.1), channel_id=1, source_target_pairs={{0,1},{1,0},{2,3},{3,2},{4,7},{5,6},{6,5},{7,4},{8,9},{9,8},{10,11... | collective-permute-start | bytes 6291464 | tf_op jit(solution)/shard_map/ppermute | solution.py:313
  13.7 0.0 collective-permute-done.3.row_0
  13.7 0.9 %collective-permute-done.4.row_1 = bf16[272,512]{1,0:T(8,128)(2,1)S(1)} collective-permute-done((bf16[272,512]{1,0:T(8,128)(2,1)}, bf16[272,512]{1,0:T(8,128)(2,1)S(1)}, u32[]{:S(2)}, u32[]{:S(2)}) %collective-permute-start.4) | collective-permute-done | bytes 278560 | tf_op jit(solution)/shard_map/ppermute | solution.py:319
  14.6 0.0 copy-done.2
  14.6 1.2 %shard_map.59 = bf16[512,1152]{1,0:T(8,128)(2,1)} custom-call(bf16[16,512]{1,0:T(8,128)(2,1)S(1)} %copy-done.2, bf16[272,512]{1,0:T(8,128)(2,1)S(1)} %collective-permute-done.3.row_0, bf16[272,512]{1,0:T(8,128)(2,1)S(1)} %collective-permute-done.4.row_1, bf16[512,512]{1,0:T(8,128)(2,1)S(1)} %shard_map.56.mine_ref), custom_call_target="tpu_custom_call" | custom-call | flops 1048576 | bytes 2097152 | tf_op jit(solution)/shard_map/pallas_call | solution.py:364
  15.8 7.9 %all-to-all-start = ((bf16[32,16,1152]{2,1,0:T(8,128)(2,1)}), bf16[32,16,1152]{2,1,0:T(8,128)(2,1)S(1)}, u32[]{:S(2)}, u32[]{:S(2)}) async-start(bf16[32,16,1152]{2,1,0:T(8,128)(2,1)} %bitcast.1), calls=%async_computation | async-start | bytes 2359296 | tf_op jit(solution)/shard_map/all_to_all | solution.py:374
  23.6 0.0 copy-start.5
  23.7 0.6 copy-done.5
  24.3 2.6 %shard_map.58 = (bf16[512,2048]{1,0:T(8,128)(2,1)S(1)}, f32[512,128]{1,0:T(8,128)S(1)}, f32[8,128]{1,0:T(8,128)S(1)}) custom-call(s32[4,16]{1,0:T(4,128)S(1)} %copy-done.3, s32[4]{0:T(128)S(1)} %copy-done.5, bf16[4,16,128,128]{3,2,1,0:T(8,128)(2,1)} %weight_ref.1), custom_call_target="tpu_custom_call" | custom-call | flops 40000000000 | bytes 8388608 | tf_op jit(solution)/shard_map/pallas_call | solution.py:324
  26.9 15.8 %all-to-all-done = bf16[32,16,1152]{2,1,0:T(8,128)(2,1)S(1)} async-done(((bf16[32,16,1152]{2,1,0:T(8,128)(2,1)}), bf16[32,16,1152]{2,1,0:T(8,128)(2,1)S(1)}, u32[]{:S(2)}, u32[]{:S(2)}) %all-to-all-start) | async-done | bytes 1179680 | tf_op jit(solution)/shard_map/all_to_all | solution.py:374
  42.7 0.2 shard_map.60
  42.8 2.0 %collective-permute-start.5 = (bf16[528,512]{1,0:T(8,128)(2,1)S(1)}, bf16[528,512]{1,0:T(8,128)(2,1)S(1)}, u32[]{:S(2)}, u32[]{:S(2)}) collective-permute-start(bf16[528,512]{1,0:T(8,128)(2,1)S(1)} %get-tuple-element.38.rows_ref.near_ref), channel_id=1, source_target_pairs={{0,3},{1,2},{2,1},{3,0},{4,5},{5,4},{6,7},{7,6},{8,11},{9,10},{10,... | collective-permute-start | bytes 1622024 | tf_op jit(solution)/shard_map/ppermute | solution.py:316
  44.8 1.2 %collective-permute-start.7 = (bf16[512,512]{1,0:T(8,128)(2,1)S(1)}, bf16[512,512]{1,0:T(8,128)(2,1)S(1)}, u32[]{:S(2)}, u32[]{:S(2)}) collective-permute-start(bf16[512,512]{1,0:T(8,128)(2,1)S(1)} %get-tuple-element.40.near_ref), channel_id=1, source_target_pairs={{0,3},{1,2},{2,1},{3,0},{4,5},{5,4},{6,7},{7,6},{8,11},{9,10},{10,... | collective-permute-start | bytes 1572872 | tf_op jit(solution)/shard_map/ppermute | solution.py:316
  46.1 0.8 shard_map.61.pick_ref
  46.9 1.3 %shard_map.62.refs_1_.part_ref = bf16[2048,256]{1,0:T(8,128)(2,1)S(1)} custom-call(bf16[2,2048,512]{2,1,0:T(8,128)(2,1)S(1)} %shard_map.61.pick_ref, bf16[528,512]{1,0:T(8,128)(2,1)S(1)} %get-tuple-element.38.rows_ref.near_ref), custom_call_target="tpu_custom_call" | custom-call | flops 1073741824 | bytes 4194304 | tf_op jit(solution)/shard_map/pallas_call | solution.py:398
  48.1 1.2 %shard_map.63.refs_2_.part_ref = bf16[2048,256]{1,0:T(8,128)(2,1)S(1)} custom-call(bf16[2,2048,512]{2,1,0:T(8,128)(2,1)S(1)} %shard_map.61.pick_ref, bf16[512,512]{1,0:T(8,128)(2,1)S(1)} %get-tuple-element.40.near_ref), custom_call_target="tpu_custom_call" | custom-call | flops 1073741824 | bytes 4194304 | tf_op jit(solution)/shard_map/pallas_call | solution.py:398
  49.4 0.0 collective-permute-done.2.weight_ref
  49.4 2.5 %shard_map.57 = (bf16[512,2048]{1,0:T(8,128)(2,1)S(1)}, f32[512,128]{1,0:T(8,128)S(1)}, f32[8,128]{1,0:T(8,128)S(1)}) custom-call(s32[4,16]{1,0:T(4,128)S(1)} %collective-permute-done.list_ref, s32[4]{0:T(128)S(1)} %collective-permute-done.1.count_ref, bf16[4,16,128,128]{3,2,1,0:T(8,128)(2,1)} %collective-permute-done.2.weight_ref), custom_call_target="tpu_custom_call" | custom-call | bytes 8388608 | tf_op jit(solution)/shard_map/pallas_call | solution.py:324
  51.9 1.5 %collective-permute-done.5.rows_ref.far_ref = bf16[528,512]{1,0:T(8,128)(2,1)S(1)} collective-permute-done((bf16[528,512]{1,0:T(8,128)(2,1)S(1)}, bf16[528,512]{1,0:T(8,128)(2,1)S(1)}, u32[]{:S(2)}, u32[]{:S(2)}) %collective-permute-start.5) | collective-permute-done | bytes 540704 | tf_op jit(solution)/shard_map/ppermute | solution.py:316
  53.4 0.8 shard_map.64.pick_ref
  54.2 2.4 %shard_map.65 = (bf16[1024,256]{1,0:T(8,128)(2,1)S(1)}, bf16[1024,256]{1,0:T(8,128)(2,1)S(1)}) custom-call(bf16[512,2048]{1,0:T(8,128)(2,1)S(1)} %get-tuple-element.31.dense_a.dense, bf16[512,2048]{1,0:T(8,128)(2,1)S(1)} %get-tuple-element.29.dense_b.dense, f32[512,128]{1,0:T(8,128)S(1)} %get-tuple-element.32.scale_a.scale, ...), custom_call_target="tpu_custom_call" | custom-call | flops 2147483648 | bytes 4194304 | tf_op jit(solution)/shard_map/pallas_call | solution.py:412
  56.6 2.1 %collective-permute-start.6 = (bf16[1024,256]{1,0:T(8,128)(2,1)S(1)}, bf16[1024,256]{1,0:T(8,128)(2,1)S(1)}, u32[]{:S(2)}, u32[]{:S(2)}) collective-permute-start(bf16[1024,256]{1,0:T(8,128)(2,1)S(1)} %get-tuple-element.41.hidden_ref), channel_id=1, source_target_pairs={{0,3},{1,2},{2,1},{3,0},{4,5},{5,4},{6,7},{7,6},{8,11},{9,10},{10,... | collective-permute-start | bytes 1572872 | tf_op jit(solution)/shard_map/ppermute | solution.py:316
  58.6 0.4 collective-permute-done.7.far_ref
  59.0 2.4 %shard_map.67 = (bf16[1024,256]{1,0:T(8,128)(2,1)S(1)}, bf16[1024,256]{1,0:T(8,128)(2,1)S(1)}) custom-call(bf16[512,2048]{1,0:T(8,128)(2,1)S(1)} %get-tuple-element.31.dense_a.dense, bf16[512,2048]{1,0:T(8,128)(2,1)S(1)} %get-tuple-element.29.dense_b.dense, f32[512,128]{1,0:T(8,128)S(1)} %get-tuple-element.32.scale_a.scale, ...), custom_call_target="tpu_custom_call" | custom-call | flops 2147483648 | bytes 4194304 | tf_op jit(solution)/shard_map/pallas_call | solution.py:412
  61.4 2.3 %collective-permute-start.9 = (bf16[1024,256]{1,0:T(8,128)(2,1)S(1)}, bf16[1024,256]{1,0:T(8,128)(2,1)S(1)}, u32[]{:S(2)}, u32[]{:S(2)}) collective-permute-start(bf16[1024,256]{1,0:T(8,128)(2,1)S(1)} %get-tuple-element.43.hidden_ref), channel_id=1, source_target_pairs={{0,3},{1,2},{2,1},{3,0},{4,5},{5,4},{6,7},{7,6},{8,11},{9,10},{10,... | collective-permute-start | bytes 1572872 | tf_op jit(solution)/shard_map/ppermute | solution.py:316
  63.6 0.7 shard_map.68.after.total_ref
  64.3 0.7 shard_map.66.total_ref
  65.0 2.0 %collective-permute-done.6.hidden_ref = bf16[1024,256]{1,0:T(8,128)(2,1)S(1)} collective-permute-done((bf16[1024,256]{1,0:T(8,128)(2,1)S(1)}, bf16[1024,256]{1,0:T(8,128)(2,1)S(1)}, u32[]{:S(2)}, u32[]{:S(2)}) %collective-permute-start.6) | collective-permute-done | bytes 524320 | tf_op jit(solution)/shard_map/ppermute | solution.py:316
  67.0 0.4 shard_map.69.after.sent_ref
  67.5 1.9 %collective-permute-start.8 = (bf16[512,256]{1,0:T(8,128)(2,1)S(1)}, bf16[512,256]{1,0:T(8,128)(2,1)S(1)}, u32[]{:S(2)}, u32[]{:S(2)}) collective-permute-start(bf16[512,256]{1,0:T(8,128)(2,1)S(1)} %shard_map.69.after.sent_ref), channel_id=1, source_target_pairs={{0,1},{1,0},{2,3},{3,2},{8,9},{9,8},{10,11},{11,10},{16,17},{17,16... | collective-permute-start | bytes 786440 | tf_op jit(solution)/shard_map/ppermute | solution.py:446
  69.4 0.4 shard_map.70.after.keep_0
  69.9 3.6 %collective-permute-done.9.hidden_ref = bf16[1024,256]{1,0:T(8,128)(2,1)S(1)} collective-permute-done((bf16[1024,256]{1,0:T(8,128)(2,1)S(1)}, bf16[1024,256]{1,0:T(8,128)(2,1)S(1)}, u32[]{:S(2)}, u32[]{:S(2)}) %collective-permute-start.9) | collective-permute-done | bytes 524320 | tf_op jit(solution)/shard_map/ppermute | solution.py:316
  73.4 0.4 shard_map.71.after_1.after
  73.9 0.1 collective-permute-start.11
  74.0 1.8 %collective-permute-done.8.after_0.early_0 = bf16[512,256]{1,0:T(8,128)(2,1)S(1)} collective-permute-done((bf16[512,256]{1,0:T(8,128)(2,1)S(1)}, bf16[512,256]{1,0:T(8,128)(2,1)S(1)}, u32[]{:S(2)}, u32[]{:S(2)}) %collective-permute-start.8) | collective-permute-done | bytes 262176 | tf_op jit(solution)/shard_map/ppermute | solution.py:446
  75.8 0.7 collective-permute-start.10
  76.5 0.4 shard_map.73.keep_1
  76.9 0.8 %shard_map.74._ = bf16[512,1024]{1,0:T(8,128)(2,1)} custom-call(bf16[512,256]{1,0:T(8,128)(2,1)S(1)} %shard_map.70.after.keep_0, bf16[512,256]{1,0:T(8,128)(2,1)S(1)} %shard_map.73.keep_1), custom_call_target="tpu_custom_call" | custom-call | tf_op jit(solution)/shard_map/pallas_call | solution.py:453
  77.7 2.6 %collective-permute-done.11.got_1 = bf16[512,256]{1,0:T(8,128)(2,1)S(1)} collective-permute-done((bf16[512,256]{1,0:T(8,128)(2,1)S(1)}, bf16[512,256]{1,0:T(8,128)(2,1)S(1)}, u32[]{:S(2)}, u32[]{:S(2)}) %collective-permute-start.11) | collective-permute-done | bytes 262176 | tf_op jit(solution)/shard_map/ppermute | solution.py:313
  80.3 0.0 collective-permute-done.10.late_0
  80.3 0.8 shard_map.75
  (1 shorter events, 0.0 us)
Async XLA Ops:
  0.0 9.6 %copy-start = (f32[512,1024]{1,0:T(8,128)S(1)}, f32[512,1024]{1,0:T(8,128)}, u32[]{:S(2)}) copy-start(f32[512,1024]{1,0:T(8,128)} %enc_ref.3) | copy-start | bytes 6291460
  0.0 7.6 %copy-start.4 = (s32[4]{0:T(128)S(1)}, s32[4]{0:T(128)}, u32[]{:S(2)}) copy-start(s32[4]{0:T(128)} %count_ref.1) | copy-start | bytes 52
  0.0 8.6 %copy-start.3 = (s32[4,16]{1,0:T(4,128)S(1)}, s32[4,16]{1,0:T(4,128)}, u32[]{:S(2)}) copy-start(s32[4,16]{1,0:T(4,128)} %list_ref.1) | copy-start | bytes 772
  3.0 10.8 %collective-permute-start.3 = (bf16[272,512]{1,0:T(8,128)(2,1)}, bf16[272,512]{1,0:T(8,128)(2,1)S(1)}, u32[]{:S(2)}, u32[]{:S(2)}) collective-permute-start(bf16[272,512]{1,0:T(8,128)(2,1)} %get-tuple-element.34), channel_id=1, source_target_pairs={{0,1},{1,0},{2,3},{3,2},{4,5},{5,4},{6,7},{7,6},{8,9},{9,8},{10,11... | collective-permute-start | bytes 835592 | tf_op jit(solution)/shard_map/ppermute | solution.py:319
  5.0 9.6 %collective-permute-start.4 = (bf16[272,512]{1,0:T(8,128)(2,1)}, bf16[272,512]{1,0:T(8,128)(2,1)S(1)}, u32[]{:S(2)}, u32[]{:S(2)}) collective-permute-start(bf16[272,512]{1,0:T(8,128)(2,1)} %get-tuple-element.35), channel_id=1, source_target_pairs={{0,3},{1,2},{2,1},{3,0},{4,7},{5,6},{6,5},{7,4},{8,11},{9,10},{10,... | collective-permute-start | bytes 835592 | tf_op jit(solution)/shard_map/ppermute | solution.py:319
  7.6 4.4 %collective-permute-start.1 = (s32[4]{0:T(128)S(1)}, s32[4]{0:T(128)S(1)}, u32[]{:S(2)}, u32[]{:S(2)}) collective-permute-start(s32[4]{0:T(128)S(1)} %copy-done.4), channel_id=1, source_target_pairs={{0,1},{1,0},{2,3},{3,2},{4,7},{5,6},{6,5},{7,4},{8,9},{9,8},{10,11... | collective-permute-start | bytes 56 | tf_op jit(solution)/shard_map/ppermute | solution.py:313
  8.6 3.6 %collective-permute-start = (s32[4,16]{1,0:T(4,128)S(1)}, s32[4,16]{1,0:T(4,128)S(1)}, u32[]{:S(2)}, u32[]{:S(2)}) collective-permute-start(s32[4,16]{1,0:T(4,128)S(1)} %copy-done.3), channel_id=1, source_target_pairs={{0,1},{1,0},{2,3},{3,2},{4,7},{5,6},{6,5},{7,4},{8,9},{9,8},{10,11... | collective-permute-start | bytes 776 | tf_op jit(solution)/shard_map/ppermute | solution.py:313
  9.6 1.0 %copy-start.1 = (bf16[512,512]{1,0:T(8,128)(2,1)S(1)}, bf16[512,512]{1,0:T(8,128)(2,1)}, u32[]{:S(2)}) copy-start(bf16[512,512]{1,0:T(8,128)(2,1)} %get-tuple-element.25.pick_ref) | copy-start | bytes 1572868
  10.6 4.0 %copy-start.2 = (bf16[16,512]{1,0:T(8,128)(2,1)S(1)}, bf16[16,512]{1,0:T(8,128)(2,1)}, u32[]{:S(2)}) copy-start(bf16[16,512]{1,0:T(8,128)(2,1)} %get-tuple-element.33.place_ref) | copy-start | bytes 49156
  12.2 37.2 %collective-permute-start.2 = (bf16[4,16,128,128]{3,2,1,0:T(8,128)(2,1)}, bf16[4,16,128,128]{3,2,1,0:T(8,128)(2,1)}, u32[]{:S(2)}, u32[]{:S(2)}) collective-permute-start(bf16[4,16,128,128]{3,2,1,0:T(8,128)(2,1)} %weight_ref.1), channel_id=1, source_target_pairs={{0,1},{1,0},{2,3},{3,2},{4,7},{5,6},{6,5},{7,4},{8,9},{9,8},{10,11... | collective-permute-start | bytes 6291464 | tf_op jit(solution)/shard_map/ppermute | solution.py:313
  15.8 26.9 %all-to-all-start = ((bf16[32,16,1152]{2,1,0:T(8,128)(2,1)}), bf16[32,16,1152]{2,1,0:T(8,128)(2,1)S(1)}, u32[]{:S(2)}, u32[]{:S(2)}) async-start(bf16[32,16,1152]{2,1,0:T(8,128)(2,1)} %bitcast.1), calls=%async_computation | async-start | bytes 2359296 | tf_op jit(solution)/shard_map/all_to_all | solution.py:374
  23.6 0.7 copy-start.5
  42.8 10.6 %collective-permute-start.5 = (bf16[528,512]{1,0:T(8,128)(2,1)S(1)}, bf16[528,512]{1,0:T(8,128)(2,1)S(1)}, u32[]{:S(2)}, u32[]{:S(2)}) collective-permute-start(bf16[528,512]{1,0:T(8,128)(2,1)S(1)} %get-tuple-element.38.rows_ref.near_ref), channel_id=1, source_target_pairs={{0,3},{1,2},{2,1},{3,0},{4,5},{5,4},{6,7},{7,6},{8,11},{9,10},{10,... | collective-permute-start | bytes 1622024 | tf_op jit(solution)/shard_map/ppermute | solution.py:316
  44.8 14.2 %collective-permute-start.7 = (bf16[512,512]{1,0:T(8,128)(2,1)S(1)}, bf16[512,512]{1,0:T(8,128)(2,1)S(1)}, u32[]{:S(2)}, u32[]{:S(2)}) collective-permute-start(bf16[512,512]{1,0:T(8,128)(2,1)S(1)} %get-tuple-element.40.near_ref), channel_id=1, source_target_pairs={{0,3},{1,2},{2,1},{3,0},{4,5},{5,4},{6,7},{7,6},{8,11},{9,10},{10,... | collective-permute-start | bytes 1572872 | tf_op jit(solution)/shard_map/ppermute | solution.py:316
  56.6 10.5 %collective-permute-start.6 = (bf16[1024,256]{1,0:T(8,128)(2,1)S(1)}, bf16[1024,256]{1,0:T(8,128)(2,1)S(1)}, u32[]{:S(2)}, u32[]{:S(2)}) collective-permute-start(bf16[1024,256]{1,0:T(8,128)(2,1)S(1)} %get-tuple-element.41.hidden_ref), channel_id=1, source_target_pairs={{0,3},{1,2},{2,1},{3,0},{4,5},{5,4},{6,7},{7,6},{8,11},{9,10},{10,... | collective-permute-start | bytes 1572872 | tf_op jit(solution)/shard_map/ppermute | solution.py:316
  61.4 12.1 %collective-permute-start.9 = (bf16[1024,256]{1,0:T(8,128)(2,1)S(1)}, bf16[1024,256]{1,0:T(8,128)(2,1)S(1)}, u32[]{:S(2)}, u32[]{:S(2)}) collective-permute-start(bf16[1024,256]{1,0:T(8,128)(2,1)S(1)} %get-tuple-element.43.hidden_ref), channel_id=1, source_target_pairs={{0,3},{1,2},{2,1},{3,0},{4,5},{5,4},{6,7},{7,6},{8,11},{9,10},{10,... | collective-permute-start | bytes 1572872 | tf_op jit(solution)/shard_map/ppermute | solution.py:316
  67.5 8.3 %collective-permute-start.8 = (bf16[512,256]{1,0:T(8,128)(2,1)S(1)}, bf16[512,256]{1,0:T(8,128)(2,1)S(1)}, u32[]{:S(2)}, u32[]{:S(2)}) collective-permute-start(bf16[512,256]{1,0:T(8,128)(2,1)S(1)} %shard_map.69.after.sent_ref), channel_id=1, source_target_pairs={{0,1},{1,0},{2,3},{3,2},{8,9},{9,8},{10,11},{11,10},{16,17},{17,16... | collective-permute-start | bytes 786440 | tf_op jit(solution)/shard_map/ppermute | solution.py:446
  73.9 6.5 %collective-permute-start.11 = (bf16[512,256]{1,0:T(8,128)(2,1)S(1)}, bf16[512,256]{1,0:T(8,128)(2,1)S(1)}, u32[]{:S(2)}, u32[]{:S(2)}) collective-permute-start(bf16[512,256]{1,0:T(8,128)(2,1)S(1)} %shard_map.71.after_1.after), channel_id=1, source_target_pairs={{0,1},{1,0},{2,3},{3,2},{4,7},{5,6},{6,5},{7,4},{8,9},{9,8},{10,11... | collective-permute-start | bytes 786440 | tf_op jit(solution)/shard_map/ppermute | solution.py:313
  75.8 4.6 %collective-permute-start.10 = (bf16[512,256]{1,0:T(8,128)(2,1)S(1)}, bf16[512,256]{1,0:T(8,128)(2,1)S(1)}, u32[]{:S(2)}, u32[]{:S(2)}) collective-permute-start(bf16[512,256]{1,0:T(8,128)(2,1)S(1)} %shard_map.72), channel_id=1, source_target_pairs={{4,7},{5,6},{6,5},{7,4},{12,15},{13,14},{14,13},{15,12},{20,23},{2... | collective-permute-start | bytes 786440 | tf_op jit(solution)/shard_map/ppermute | solution.py:446

commit v9 on v8

--- a/solution.py
+++ b/solution.py
@@ -33,7 +33,9 @@
     return jnp.where(core_is_odd, z // 2, ((z + 1) // 2) % 2)
 
 
-def sort_kernel(doms, owner_hbm, enc_ref, other_0, other_1, pick_ref, place_ref, enc, owner_ref, sems):
+def sort_kernel(
+    doms, owner_hbm, enc_ref, out_0, out_1, pick_hbm, place_ref, enc, owner_ref, other_0, other_1, pick_ref, sems, out_sems
+):
     rows, width = enc_ref.shape
     half = width // 2
     z = lax.axis_index("grp")
@@ -61,6 +63,8 @@
     block = (tdom % 2) * (doms // 2) + tdom // 2
     slot = block * per + rank.astype(jnp.int32)
     pick_ref[...] = (lax.broadcasted_iota(jnp.int32, (rows, rows), 0) == slot).astype(jnp.bfloat16)
+    copies = [pltpu.make_async_copy(pick_ref, pick_hbm, out_sems.at[2])]
+    copies[0].start()
     line = lax.broadcasted_iota(jnp.int32, (16, rows), 0)
     coded = jnp.where(line == 0, place // 64, jnp.where(line == 1, place % 64, 0))
     places = lax.dot_general(
@@ -80,6 +84,10 @@
             enc[core].astype(jnp.bfloat16),
             preferred_element_type=jnp.float32,
         ).astype(jnp.bfloat16)
+        copies.append(pltpu.make_async_copy(out, (out_0, out_1)[core], out_sems.at[core]))
+        copies[-1].start()
+    for copy in copies:
+        copy.wait()
 
 
 def by_dom(core, block, per):
@@ -337,14 +345,27 @@
 
     held = pltpu.VMEM((2, rows, half), f32)
     other = jax.ShapeDtypeStruct((rows // 2 + 16, half), bf16)
-    other_0, other_1, pick, place = kernel_call(
+    other_0, other_1, pick, place = pl.pallas_call(
         functools.partial(sort_kernel, doms),
-        (other, other, jax.ShapeDtypeStruct((rows, rows), bf16), jax.ShapeDtypeStruct((16, rows), bf16)),
-        [ANY, ANY],
-        2 * rows * rows * half,
-        4 << 20,
-        scratch=[held, pltpu.VMEM((1, rows), i32), pltpu.SemaphoreType.DMA((3,))],
-        limit=58,
+        out_shape=(
+            other,
+            other,
+            jax.ShapeDtypeStruct((rows, rows), bf16),
+            jax.ShapeDtypeStruct((16, rows), bf16),
+        ),
+        in_specs=[ANY, ANY],
+        out_specs=(ANY, ANY, ANY, VMEM),
+        scratch_shapes=[
+            held,
+            pltpu.VMEM((1, rows), i32),
+            pltpu.VMEM(other.shape, bf16),
+            pltpu.VMEM(other.shape, bf16),
+            pltpu.VMEM((rows, rows), bf16),
+            pltpu.SemaphoreType.DMA((3,)),
+            pltpu.SemaphoreType.DMA((3,)),
+        ],
+        compiler_params=pltpu.CompilerParams(vmem_limit_bytes=58 << 20),
+        cost_estimate=pl.CostEstimate(flops=2 * rows * rows * half, bytes_accessed=4 << 20, transcendentals=0),
     )(owner_of.reshape(1, rows), encoded)
     row_0, row_1 = to_row_of(0, other_0), to_row_of(1, other_1)
     per = rows // doms

time: 81.6 us -> 82.1 us (level)
  Pallas kernels: 24 us -> 26.1 us
  waiting for transfers between devices: 29 us -> 27.3 us
    pallas_call x2, Pallas kernels: 5.09 us -> 6.72 us  [dense_of(): kernel_call(dense_kernel, (jax.ShapeDtypeStruct((blocks * size, nodes), b...]
    all_to_all x1, waiting for transfers between devices: 15.8 us -> 14.9 us  [shards(): packed = lax.all_to_all(packed, 'dom', 0, 0, tiled=True)]
  transfers between devices with their start and end apart: 13 -> 13, of which waited for: 10 -> 10; matrix products, arithmetic and copies ran while one was open for 0% -> 0% of each run, Pallas kernels for 25% -> 27%
where the time goes in v9:
time: 82.1 us; the launch traced here: 81.8 us
  waiting for transfers between devices  27.3 us (33%)
  starting transfers between devices  26.3 us (32%)
  Pallas kernels  26.1 us (32%)
  local copies, waits for them, and re-layouts  1.71 us (2%)
    all_to_all x1, waiting for transfers between devices, shards(): packed = lax.all_to_all(packed, 'dom', 0, 0, tiled=True)  14.9 us
    all_to_all x1, starting transfers between devices, shards(): packed = lax.all_to_all(packed, 'dom', 0, 0, tiled=True)  7.86 us
    ppermute x4, starting transfers between devices, to_col(): return lax.ppermute(a, AXES, col_pairs)  7.57 us
    pallas_call x2, Pallas kernels, dense_of(): kernel_call(dense_kernel, (jax.ShapeDtypeStruct((blocks * size, nodes), b...  6.72 us
    ppermute x4, waiting for transfers between devices, to_col(): return lax.ppermute(a, AXES, col_pairs)  6.65 us
    pallas_call x2, Pallas kernels, shards(): kernel_call(first_kernel, (jax.ShapeDtypeStruct((mine_n, part), bf16), ja...  4.71 us
    ppermute x2, starting transfers between devices, to_row_of(): lax.ppermute(a, AXES, [(d * depth + q, d * depth + (q ^ row_step(core)))...  4.61 us
    ppermute x4, starting transfers between devices, to_row(): return lax.ppermute(a, AXES, row_pairs)  3.65 us
  transfers between devices with their start and end apart: 13, of which 10 were waited for; matrix products, arithmetic and copies ran while one was open for 0% of the time, Pallas kernels for 27%

profile of v9, /device:TPU:0, one launch (start us, length us, event | category | flops | bytes accessed | tf_op | source)
XLA Modules:
  0.0 81.8 jit_solution(5425021687740230868)
XLA Ops:
  0.0 0.0 copy-start
  0.0 0.0 copy-start.4
  0.0 0.0 copy-start.3
  0.0 3.4 %shard_map.55 = (bf16[272,512]{1,0:T(8,128)(2,1)}, bf16[272,512]{1,0:T(8,128)(2,1)}, bf16[512,512]{1,0:T(8,128)(2,1)}, bf16[16,512]{1,0:T(8,128)(2,1)}) custom-call(s32[1,512]{1,0:T(1,128)} %bitcast.4, f32[512,1024]{1,0:T(8,128)} %enc_ref.3), custom_call_target="tpu_custom_call" | custom-call | flops 268435456 | bytes 4194304 | tf_op jit(solution)/shard_map/pallas_call | solution.py:348
  3.4 2.1 %collective-permute-start.3 = (bf16[272,512]{1,0:T(8,128)(2,1)}, bf16[272,512]{1,0:T(8,128)(2,1)S(1)}, u32[]{:S(2)}, u32[]{:S(2)}) collective-permute-start(bf16[272,512]{1,0:T(8,128)(2,1)} %get-tuple-element.34), channel_id=1, source_target_pairs={{0,1},{1,0},{2,3},{3,2},{4,5},{5,4},{6,7},{7,6},{8,9},{9,8},{10,11... | collective-permute-start | bytes 835592 | tf_op jit(solution)/shard_map/ppermute | solution.py:327
  5.5 2.5 %collective-permute-start.4 = (bf16[272,512]{1,0:T(8,128)(2,1)}, bf16[272,512]{1,0:T(8,128)(2,1)S(1)}, u32[]{:S(2)}, u32[]{:S(2)}) collective-permute-start(bf16[272,512]{1,0:T(8,128)(2,1)} %get-tuple-element.35), channel_id=1, source_target_pairs={{0,3},{1,2},{2,1},{3,0},{4,7},{5,6},{6,5},{7,4},{8,11},{9,10},{10,... | collective-permute-start | bytes 835592 | tf_op jit(solution)/shard_map/ppermute | solution.py:327
  8.0 0.0 copy-done.4
  8.0 1.0 %collective-permute-start.1 = (s32[4]{0:T(128)S(1)}, s32[4]{0:T(128)S(1)}, u32[]{:S(2)}, u32[]{:S(2)}) collective-permute-start(s32[4]{0:T(128)S(1)} %copy-done.4), channel_id=1, source_target_pairs={{0,1},{1,0},{2,3},{3,2},{4,7},{5,6},{6,5},{7,4},{8,9},{9,8},{10,11... | collective-permute-start | bytes 56 | tf_op jit(solution)/shard_map/ppermute | solution.py:321
  9.0 0.0 copy-done.3
  9.0 1.0 %collective-permute-start = (s32[4,16]{1,0:T(4,128)S(1)}, s32[4,16]{1,0:T(4,128)S(1)}, u32[]{:S(2)}, u32[]{:S(2)}) collective-permute-start(s32[4,16]{1,0:T(4,128)S(1)} %copy-done.3), channel_id=1, source_target_pairs={{0,1},{1,0},{2,3},{3,2},{4,7},{5,6},{6,5},{7,4},{8,9},{9,8},{10,11... | collective-permute-start | bytes 776 | tf_op jit(solution)/shard_map/ppermute | solution.py:321
  10.0 0.0 copy-done
  10.0 0.0 copy-start.1
  10.0 1.0 %copy-done.1 = bf16[512,512]{1,0:T(8,128)(2,1)S(1)} copy-done((bf16[512,512]{1,0:T(8,128)(2,1)S(1)}, bf16[512,512]{1,0:T(8,128)(2,1)}, u32[]{:S(2)}) %copy-start.1) | copy-done | bytes 524312
  11.1 0.0 copy-start.2
  11.1 1.0 %shard_map.56.mine_ref = bf16[512,512]{1,0:T(8,128)(2,1)S(1)} custom-call(f32[512,1024]{1,0:T(8,128)S(1)} %copy-done, bf16[512,512]{1,0:T(8,128)(2,1)S(1)} %copy-done.1), custom_call_target="tpu_custom_call" | custom-call | flops 268435456 | bytes 4194304 | tf_op jit(solution)/shard_map/pallas_call | solution.py:372
  12.1 0.3 collective-permute-done.1.count_ref
  12.4 0.2 collective-permute-done.list_ref
  12.6 1.5 %collective-permute-start.2 = (bf16[4,16,128,128]{3,2,1,0:T(8,128)(2,1)}, bf16[4,16,128,128]{3,2,1,0:T(8,128)(2,1)}, u32[]{:S(2)}, u32[]{:S(2)}) collective-permute-start(bf16[4,16,128,128]{3,2,1,0:T(8,128)(2,1)} %weight_ref.1), channel_id=1, source_target_pairs={{0,1},{1,0},{2,3},{3,2},{4,7},{5,6},{6,5},{7,4},{8,9},{9,8},{10,11... | collective-permute-start | bytes 6291464 | tf_op jit(solution)/shard_map/ppermute | solution.py:321
  14.2 0.0 collective-permute-done.3.row_0
  14.2 0.9 %collective-permute-done.4.row_1 = bf16[272,512]{1,0:T(8,128)(2,1)S(1)} collective-permute-done((bf16[272,512]{1,0:T(8,128)(2,1)}, bf16[272,512]{1,0:T(8,128)(2,1)S(1)}, u32[]{:S(2)}, u32[]{:S(2)}) %collective-permute-start.4) | collective-permute-done | bytes 278560 | tf_op jit(solution)/shard_map/ppermute | solution.py:327
  15.0 0.0 copy-done.2
  15.0 1.2 %shard_map.59 = bf16[512,1152]{1,0:T(8,128)(2,1)} custom-call(bf16[16,512]{1,0:T(8,128)(2,1)S(1)} %copy-done.2, bf16[272,512]{1,0:T(8,128)(2,1)S(1)} %collective-permute-done.3.row_0, bf16[272,512]{1,0:T(8,128)(2,1)S(1)} %collective-permute-done.4.row_1, bf16[512,512]{1,0:T(8,128)(2,1)S(1)} %shard_map.56.mine_ref), custom_call_target="tpu_custom_call" | custom-call | flops 1048576 | bytes 2097152 | tf_op jit(solution)/shard_map/pallas_call | solution.py:385
  16.2 7.9 %all-to-all-start = ((bf16[32,16,1152]{2,1,0:T(8,128)(2,1)}), bf16[32,16,1152]{2,1,0:T(8,128)(2,1)S(1)}, u32[]{:S(2)}, u32[]{:S(2)}) async-start(bf16[32,16,1152]{2,1,0:T(8,128)(2,1)} %bitcast.1), calls=%async_computation | async-start | bytes 2359296 | tf_op jit(solution)/shard_map/all_to_all | solution.py:395
  24.1 0.0 copy-start.5
  24.1 0.6 copy-done.5
  24.7 3.4 %shard_map.58 = (bf16[512,2048]{1,0:T(8,128)(2,1)S(1)}, f32[512,128]{1,0:T(8,128)S(1)}, f32[8,128]{1,0:T(8,128)S(1)}) custom-call(s32[4,16]{1,0:T(4,128)S(1)} %copy-done.3, s32[4]{0:T(128)S(1)} %copy-done.5, bf16[4,16,128,128]{3,2,1,0:T(8,128)(2,1)} %weight_ref.1), custom_call_target="tpu_custom_call" | custom-call | flops 40000000000 | bytes 8388608 | tf_op jit(solution)/shard_map/pallas_call | solution.py:332
  28.2 14.9 %all-to-all-done = bf16[32,16,1152]{2,1,0:T(8,128)(2,1)S(1)} async-done(((bf16[32,16,1152]{2,1,0:T(8,128)(2,1)}), bf16[32,16,1152]{2,1,0:T(8,128)(2,1)S(1)}, u32[]{:S(2)}, u32[]{:S(2)}) %all-to-all-start) | async-done | bytes 1179680 | tf_op jit(solution)/shard_map/all_to_all | solution.py:395
  43.1 0.2 shard_map.60
  43.3 2.0 %collective-permute-start.5 = (bf16[528,512]{1,0:T(8,128)(2,1)S(1)}, bf16[528,512]{1,0:T(8,128)(2,1)S(1)}, u32[]{:S(2)}, u32[]{:S(2)}) collective-permute-start(bf16[528,512]{1,0:T(8,128)(2,1)S(1)} %get-tuple-element.38.rows_ref.near_ref), channel_id=1, source_target_pairs={{0,3},{1,2},{2,1},{3,0},{4,5},{5,4},{6,7},{7,6},{8,11},{9,10},{10,... | collective-permute-start | bytes 1622024 | tf_op jit(solution)/shard_map/ppermute | solution.py:324
  45.3 1.2 %collective-permute-start.7 = (bf16[512,512]{1,0:T(8,128)(2,1)S(1)}, bf16[512,512]{1,0:T(8,128)(2,1)S(1)}, u32[]{:S(2)}, u32[]{:S(2)}) collective-permute-start(bf16[512,512]{1,0:T(8,128)(2,1)S(1)} %get-tuple-element.40.near_ref), channel_id=1, source_target_pairs={{0,3},{1,2},{2,1},{3,0},{4,5},{5,4},{6,7},{7,6},{8,11},{9,10},{10,... | collective-permute-start | bytes 1572872 | tf_op jit(solution)/shard_map/ppermute | solution.py:324
  46.5 0.8 shard_map.61.pick_ref
  47.3 1.3 %shard_map.62.refs_1_.part_ref = bf16[2048,256]{1,0:T(8,128)(2,1)S(1)} custom-call(bf16[2,2048,512]{2,1,0:T(8,128)(2,1)S(1)} %shard_map.61.pick_ref, bf16[528,512]{1,0:T(8,128)(2,1)S(1)} %get-tuple-element.38.rows_ref.near_ref), custom_call_target="tpu_custom_call" | custom-call | flops 1073741824 | bytes 4194304 | tf_op jit(solution)/shard_map/pallas_call | solution.py:419
  48.6 1.2 %shard_map.63.refs_2_.part_ref = bf16[2048,256]{1,0:T(8,128)(2,1)S(1)} custom-call(bf16[2,2048,512]{2,1,0:T(8,128)(2,1)S(1)} %shard_map.61.pick_ref, bf16[512,512]{1,0:T(8,128)(2,1)S(1)} %get-tuple-element.40.near_ref), custom_call_target="tpu_custom_call" | custom-call | flops 1073741824 | bytes 4194304 | tf_op jit(solution)/shard_map/pallas_call | solution.py:419
  49.8 0.0 collective-permute-done.2.weight_ref
  49.9 3.3 %shard_map.57 = (bf16[512,2048]{1,0:T(8,128)(2,1)S(1)}, f32[512,128]{1,0:T(8,128)S(1)}, f32[8,128]{1,0:T(8,128)S(1)}) custom-call(s32[4,16]{1,0:T(4,128)S(1)} %collective-permute-done.list_ref, s32[4]{0:T(128)S(1)} %collective-permute-done.1.count_ref, bf16[4,16,128,128]{3,2,1,0:T(8,128)(2,1)} %collective-permute-done.2.weight_ref), custom_call_target="tpu_custom_call" | custom-call | bytes 8388608 | tf_op jit(solution)/shard_map/pallas_call | solution.py:332
  53.1 0.7 collective-permute-done.5.rows_ref.far_ref
  53.8 0.8 shard_map.64.pick_ref
  54.6 2.4 %shard_map.65 = (bf16[1024,256]{1,0:T(8,128)(2,1)S(1)}, bf16[1024,256]{1,0:T(8,128)(2,1)S(1)}) custom-call(bf16[512,2048]{1,0:T(8,128)(2,1)S(1)} %get-tuple-element.31.dense_a.dense, bf16[512,2048]{1,0:T(8,128)(2,1)S(1)} %get-tuple-element.29.dense_b.dense, f32[512,128]{1,0:T(8,128)S(1)} %get-tuple-element.32.scale_a.scale, ...), custom_call_target="tpu_custom_call" | custom-call | flops 2147483648 | bytes 4194304 | tf_op jit(solution)/shard_map/pallas_call | solution.py:433
  57.0 2.1 %collective-permute-start.6 = (bf16[1024,256]{1,0:T(8,128)(2,1)S(1)}, bf16[1024,256]{1,0:T(8,128)(2,1)S(1)}, u32[]{:S(2)}, u32[]{:S(2)}) collective-permute-start(bf16[1024,256]{1,0:T(8,128)(2,1)S(1)} %get-tuple-element.41.hidden_ref), channel_id=1, source_target_pairs={{0,3},{1,2},{2,1},{3,0},{4,5},{5,4},{6,7},{7,6},{8,11},{9,10},{10,... | collective-permute-start | bytes 1572872 | tf_op jit(solution)/shard_map/ppermute | solution.py:324
  59.1 0.4 collective-permute-done.7.far_ref
  59.5 2.4 %shard_map.67 = (bf16[1024,256]{1,0:T(8,128)(2,1)S(1)}, bf16[1024,256]{1,0:T(8,128)(2,1)S(1)}) custom-call(bf16[512,2048]{1,0:T(8,128)(2,1)S(1)} %get-tuple-element.31.dense_a.dense, bf16[512,2048]{1,0:T(8,128)(2,1)S(1)} %get-tuple-element.29.dense_b.dense, f32[512,128]{1,0:T(8,128)S(1)} %get-tuple-element.32.scale_a.scale, ...), custom_call_target="tpu_custom_call" | custom-call | flops 2147483648 | bytes 4194304 | tf_op jit(solution)/shard_map/pallas_call | solution.py:433
  61.8 2.3 %collective-permute-start.9 = (bf16[1024,256]{1,0:T(8,128)(2,1)S(1)}, bf16[1024,256]{1,0:T(8,128)(2,1)S(1)}, u32[]{:S(2)}, u32[]{:S(2)}) collective-permute-start(bf16[1024,256]{1,0:T(8,128)(2,1)S(1)} %get-tuple-element.43.hidden_ref), channel_id=1, source_target_pairs={{0,3},{1,2},{2,1},{3,0},{4,5},{5,4},{6,7},{7,6},{8,11},{9,10},{10,... | collective-permute-start | bytes 1572872 | tf_op jit(solution)/shard_map/ppermute | solution.py:324
  64.1 0.7 shard_map.68.after.total_ref
  64.8 0.7 shard_map.66.total_ref
  65.5 2.0 %collective-permute-done.6.hidden_ref = bf16[1024,256]{1,0:T(8,128)(2,1)S(1)} collective-permute-done((bf16[1024,256]{1,0:T(8,128)(2,1)S(1)}, bf16[1024,256]{1,0:T(8,128)(2,1)S(1)}, u32[]{:S(2)}, u32[]{:S(2)}) %collective-permute-start.6) | collective-permute-done | bytes 524320 | tf_op jit(solution)/shard_map/ppermute | solution.py:324
  67.5 0.4 shard_map.69.after.sent_ref
  67.9 1.9 %collective-permute-start.8 = (bf16[512,256]{1,0:T(8,128)(2,1)S(1)}, bf16[512,256]{1,0:T(8,128)(2,1)S(1)}, u32[]{:S(2)}, u32[]{:S(2)}) collective-permute-start(bf16[512,256]{1,0:T(8,128)(2,1)S(1)} %shard_map.69.after.sent_ref), channel_id=1, source_target_pairs={{0,1},{1,0},{2,3},{3,2},{8,9},{9,8},{10,11},{11,10},{16,17},{17,16... | collective-permute-start | bytes 786440 | tf_op jit(solution)/shard_map/ppermute | solution.py:467
  69.9 0.4 shard_map.70.after.keep_0
  70.3 3.6 %collective-permute-done.9.hidden_ref = bf16[1024,256]{1,0:T(8,128)(2,1)S(1)} collective-permute-done((bf16[1024,256]{1,0:T(8,128)(2,1)S(1)}, bf16[1024,256]{1,0:T(8,128)(2,1)S(1)}, u32[]{:S(2)}, u32[]{:S(2)}) %collective-permute-start.9) | collective-permute-done | bytes 524320 | tf_op jit(solution)/shard_map/ppermute | solution.py:324
  73.9 0.4 shard_map.71.after_1.after
  74.3 0.1 collective-permute-start.11
  74.4 1.8 %collective-permute-done.8.after_0.early_0 = bf16[512,256]{1,0:T(8,128)(2,1)S(1)} collective-permute-done((bf16[512,256]{1,0:T(8,128)(2,1)S(1)}, bf16[512,256]{1,0:T(8,128)(2,1)S(1)}, u32[]{:S(2)}, u32[]{:S(2)}) %collective-permute-start.8) | collective-permute-done | bytes 262176 | tf_op jit(solution)/shard_map/ppermute | solution.py:467
  76.2 0.7 collective-permute-start.10
  76.9 0.4 shard_map.73.keep_1
  77.3 0.8 %shard_map.74._ = bf16[512,1024]{1,0:T(8,128)(2,1)} custom-call(bf16[512,256]{1,0:T(8,128)(2,1)S(1)} %shard_map.70.after.keep_0, bf16[512,256]{1,0:T(8,128)(2,1)S(1)} %shard_map.73.keep_1), custom_call_target="tpu_custom_call" | custom-call | tf_op jit(solution)/shard_map/pallas_call | solution.py:474
  78.2 2.6 %collective-permute-done.11.got_1 = bf16[512,256]{1,0:T(8,128)(2,1)S(1)} collective-permute-done((bf16[512,256]{1,0:T(8,128)(2,1)S(1)}, bf16[512,256]{1,0:T(8,128)(2,1)S(1)}, u32[]{:S(2)}, u32[]{:S(2)}) %collective-permute-start.11) | collective-permute-done | bytes 262176 | tf_op jit(solution)/shard_map/ppermute | solution.py:321
  80.8 0.0 collective-permute-done.10.late_0
  80.8 0.8 shard_map.75
  (1 shorter events, 0.0 us)
Async XLA Ops:
  0.0 10.0 %copy-start = (f32[512,1024]{1,0:T(8,128)S(1)}, f32[512,1024]{1,0:T(8,128)}, u32[]{:S(2)}) copy-start(f32[512,1024]{1,0:T(8,128)} %enc_ref.3) | copy-start | bytes 6291460
  0.0 8.0 %copy-start.4 = (s32[4]{0:T(128)S(1)}, s32[4]{0:T(128)}, u32[]{:S(2)}) copy-start(s32[4]{0:T(128)} %count_ref.1) | copy-start | bytes 52
  0.0 9.0 %copy-start.3 = (s32[4,16]{1,0:T(4,128)S(1)}, s32[4,16]{1,0:T(4,128)}, u32[]{:S(2)}) copy-start(s32[4,16]{1,0:T(4,128)} %list_ref.1) | copy-start | bytes 772
  3.4 10.8 %collective-permute-start.3 = (bf16[272,512]{1,0:T(8,128)(2,1)}, bf16[272,512]{1,0:T(8,128)(2,1)S(1)}, u32[]{:S(2)}, u32[]{:S(2)}) collective-permute-start(bf16[272,512]{1,0:T(8,128)(2,1)} %get-tuple-element.34), channel_id=1, source_target_pairs={{0,1},{1,0},{2,3},{3,2},{4,5},{5,4},{6,7},{7,6},{8,9},{9,8},{10,11... | collective-permute-start | bytes 835592 | tf_op jit(solution)/shard_map/ppermute | solution.py:327
  5.5 9.6 %collective-permute-start.4 = (bf16[272,512]{1,0:T(8,128)(2,1)}, bf16[272,512]{1,0:T(8,128)(2,1)S(1)}, u32[]{:S(2)}, u32[]{:S(2)}) collective-permute-start(bf16[272,512]{1,0:T(8,128)(2,1)} %get-tuple-element.35), channel_id=1, source_target_pairs={{0,3},{1,2},{2,1},{3,0},{4,7},{5,6},{6,5},{7,4},{8,11},{9,10},{10,... | collective-permute-start | bytes 835592 | tf_op jit(solution)/shard_map/ppermute | solution.py:327
  8.0 4.4 %collective-permute-start.1 = (s32[4]{0:T(128)S(1)}, s32[4]{0:T(128)S(1)}, u32[]{:S(2)}, u32[]{:S(2)}) collective-permute-start(s32[4]{0:T(128)S(1)} %copy-done.4), channel_id=1, source_target_pairs={{0,1},{1,0},{2,3},{3,2},{4,7},{5,6},{6,5},{7,4},{8,9},{9,8},{10,11... | collective-permute-start | bytes 56 | tf_op jit(solution)/shard_map/ppermute | solution.py:321
  9.0 3.6 %collective-permute-start = (s32[4,16]{1,0:T(4,128)S(1)}, s32[4,16]{1,0:T(4,128)S(1)}, u32[]{:S(2)}, u32[]{:S(2)}) collective-permute-start(s32[4,16]{1,0:T(4,128)S(1)} %copy-done.3), channel_id=1, source_target_pairs={{0,1},{1,0},{2,3},{3,2},{4,7},{5,6},{6,5},{7,4},{8,9},{9,8},{10,11... | collective-permute-start | bytes 776 | tf_op jit(solution)/shard_map/ppermute | solution.py:321
  10.0 1.0 %copy-start.1 = (bf16[512,512]{1,0:T(8,128)(2,1)S(1)}, bf16[512,512]{1,0:T(8,128)(2,1)}, u32[]{:S(2)}) copy-start(bf16[512,512]{1,0:T(8,128)(2,1)} %get-tuple-element.25.pick_ref) | copy-start | bytes 1572868
  11.1 4.0 %copy-start.2 = (bf16[16,512]{1,0:T(8,128)(2,1)S(1)}, bf16[16,512]{1,0:T(8,128)(2,1)}, u32[]{:S(2)}) copy-start(bf16[16,512]{1,0:T(8,128)(2,1)} %get-tuple-element.33.place_ref) | copy-start | bytes 49156
  12.6 37.2 %collective-permute-start.2 = (bf16[4,16,128,128]{3,2,1,0:T(8,128)(2,1)}, bf16[4,16,128,128]{3,2,1,0:T(8,128)(2,1)}, u32[]{:S(2)}, u32[]{:S(2)}) collective-permute-start(bf16[4,16,128,128]{3,2,1,0:T(8,128)(2,1)} %weight_ref.1), channel_id=1, source_target_pairs={{0,1},{1,0},{2,3},{3,2},{4,7},{5,6},{6,5},{7,4},{8,9},{9,8},{10,11... | collective-permute-start | bytes 6291464 | tf_op jit(solution)/shard_map/ppermute | solution.py:321
  16.2 26.9 %all-to-all-start = ((bf16[32,16,1152]{2,1,0:T(8,128)(2,1)}), bf16[32,16,1152]{2,1,0:T(8,128)(2,1)S(1)}, u32[]{:S(2)}, u32[]{:S(2)}) async-start(bf16[32,16,1152]{2,1,0:T(8,128)(2,1)} %bitcast.1), calls=%async_computation | async-start | bytes 2359296 | tf_op jit(solution)/shard_map/all_to_all | solution.py:395
  24.1 0.7 copy-start.5
  43.3 10.6 %collective-permute-start.5 = (bf16[528,512]{1,0:T(8,128)(2,1)S(1)}, bf16[528,512]{1,0:T(8,128)(2,1)S(1)}, u32[]{:S(2)}, u32[]{:S(2)}) collective-permute-start(bf16[528,512]{1,0:T(8,128)(2,1)S(1)} %get-tuple-element.38.rows_ref.near_ref), channel_id=1, source_target_pairs={{0,3},{1,2},{2,1},{3,0},{4,5},{5,4},{6,7},{7,6},{8,11},{9,10},{10,... | collective-permute-start | bytes 1622024 | tf_op jit(solution)/shard_map/ppermute | solution.py:324
  45.3 14.2 %collective-permute-start.7 = (bf16[512,512]{1,0:T(8,128)(2,1)S(1)}, bf16[512,512]{1,0:T(8,128)(2,1)S(1)}, u32[]{:S(2)}, u32[]{:S(2)}) collective-permute-start(bf16[512,512]{1,0:T(8,128)(2,1)S(1)} %get-tuple-element.40.near_ref), channel_id=1, source_target_pairs={{0,3},{1,2},{2,1},{3,0},{4,5},{5,4},{6,7},{7,6},{8,11},{9,10},{10,... | collective-permute-start | bytes 1572872 | tf_op jit(solution)/shard_map/ppermute | solution.py:324
  57.0 10.5 %collective-permute-start.6 = (bf16[1024,256]{1,0:T(8,128)(2,1)S(1)}, bf16[1024,256]{1,0:T(8,128)(2,1)S(1)}, u32[]{:S(2)}, u32[]{:S(2)}) collective-permute-start(bf16[1024,256]{1,0:T(8,128)(2,1)S(1)} %get-tuple-element.41.hidden_ref), channel_id=1, source_target_pairs={{0,3},{1,2},{2,1},{3,0},{4,5},{5,4},{6,7},{7,6},{8,11},{9,10},{10,... | collective-permute-start | bytes 1572872 | tf_op jit(solution)/shard_map/ppermute | solution.py:324
  61.8 12.1 %collective-permute-start.9 = (bf16[1024,256]{1,0:T(8,128)(2,1)S(1)}, bf16[1024,256]{1,0:T(8,128)(2,1)S(1)}, u32[]{:S(2)}, u32[]{:S(2)}) collective-permute-start(bf16[1024,256]{1,0:T(8,128)(2,1)S(1)} %get-tuple-element.43.hidden_ref), channel_id=1, source_target_pairs={{0,3},{1,2},{2,1},{3,0},{4,5},{5,4},{6,7},{7,6},{8,11},{9,10},{10,... | collective-permute-start | bytes 1572872 | tf_op jit(solution)/shard_map/ppermute | solution.py:324
  67.9 8.3 %collective-permute-start.8 = (bf16[512,256]{1,0:T(8,128)(2,1)S(1)}, bf16[512,256]{1,0:T(8,128)(2,1)S(1)}, u32[]{:S(2)}, u32[]{:S(2)}) collective-permute-start(bf16[512,256]{1,0:T(8,128)(2,1)S(1)} %shard_map.69.after.sent_ref), channel_id=1, source_target_pairs={{0,1},{1,0},{2,3},{3,2},{8,9},{9,8},{10,11},{11,10},{16,17},{17,16... | collective-permute-start | bytes 786440 | tf_op jit(solution)/shard_map/ppermute | solution.py:467
  74.3 6.5 %collective-permute-start.11 = (bf16[512,256]{1,0:T(8,128)(2,1)S(1)}, bf16[512,256]{1,0:T(8,128)(2,1)S(1)}, u32[]{:S(2)}, u32[]{:S(2)}) collective-permute-start(bf16[512,256]{1,0:T(8,128)(2,1)S(1)} %shard_map.71.after_1.after), channel_id=1, source_target_pairs={{0,1},{1,0},{2,3},{3,2},{4,7},{5,6},{6,5},{7,4},{8,9},{9,8},{10,11... | collective-permute-start | bytes 786440 | tf_op jit(solution)/shard_map/ppermute | solution.py:321
  76.2 4.6 %collective-permute-start.10 = (bf16[512,256]{1,0:T(8,128)(2,1)S(1)}, bf16[512,256]{1,0:T(8,128)(2,1)S(1)}, u32[]{:S(2)}, u32[]{:S(2)}) collective-permute-start(bf16[512,256]{1,0:T(8,128)(2,1)S(1)} %shard_map.72), channel_id=1, source_target_pairs={{4,7},{5,6},{6,5},{7,4},{12,15},{13,14},{14,13},{15,12},{20,23},{2... | collective-permute-start | bytes 786440 | tf_op jit(solution)/shard_map/ppermute | solution.py:467

commit v10 on v8

--- a/solution.py
+++ b/solution.py
@@ -437,8 +437,8 @@
         )
 
     send_0 = side(1, 0, steps[1][0])
-    keep_0 = side(0, 0, send_0)
-    send_1 = side(1, 1, keep_0)
+    send_1 = side(1, 1, send_0)
+    keep_0 = side(0, 0, send_1)
     keep_1 = side(0, 1, send_1)
     kept, sent = [keep_0, keep_1], [send_0, send_1]
 

time: 81.6 us -> 81.6 us (level)
  transfers between devices with their start and end apart: 13 -> 13, of which waited for: 10 -> 10; matrix products, arithmetic and copies ran while one was open for 0% -> 0% of each run, Pallas kernels for 25% -> 26%
where the time goes in v10:
time: 81.6 us; the launch traced here: 81.3 us
  waiting for transfers between devices  28.5 us (35%)
  starting transfers between devices  26.3 us (32%)
  Pallas kernels  24.5 us (30%)
  local copies, waits for them, and re-layouts  1.71 us (2%)
    all_to_all x1, waiting for transfers between devices, shards(): packed = lax.all_to_all(packed, 'dom', 0, 0, tiled=True)  15.4 us
    all_to_all x1, starting transfers between devices, shards(): packed = lax.all_to_all(packed, 'dom', 0, 0, tiled=True)  7.86 us
    ppermute x4, waiting for transfers between devices, to_col(): return lax.ppermute(a, AXES, col_pairs)  7.74 us
    ppermute x4, starting transfers between devices, to_col(): return lax.ppermute(a, AXES, col_pairs)  7.57 us
    pallas_call x2, Pallas kernels, dense_of(): kernel_call(dense_kernel, (jax.ShapeDtypeStruct((blocks * size, nodes), b...  5.56 us
    pallas_call x2, Pallas kernels, shards(): kernel_call(first_kernel, (jax.ShapeDtypeStruct((mine_n, part), bf16), ja...  4.71 us
    ppermute x2, starting transfers between devices, to_row_of(): lax.ppermute(a, AXES, [(d * depth + q, d * depth + (q ^ row_step(core)))...  4.61 us
    ppermute x4, starting transfers between devices, to_row(): return lax.ppermute(a, AXES, row_pairs)  3.65 us
  transfers between devices with their start and end apart: 13, of which 10 were waited for; matrix products, arithmetic and copies ran while one was open for 0% of the time, Pallas kernels for 26%

profile of v10, /device:TPU:0, one launch (start us, length us, event | category | flops | bytes accessed | tf_op | source)
XLA Modules:
  0.0 81.3 jit_solution(4678205271003638177)
XLA Ops:
  0.0 0.0 copy-start
  0.0 0.0 copy-start.4
  0.0 0.0 copy-start.3
  0.0 2.9 %shard_map.55 = (bf16[272,512]{1,0:T(8,128)(2,1)}, bf16[272,512]{1,0:T(8,128)(2,1)}, bf16[512,512]{1,0:T(8,128)(2,1)}, bf16[16,512]{1,0:T(8,128)(2,1)}) custom-call(s32[1,512]{1,0:T(1,128)} %bitcast.4, f32[512,1024]{1,0:T(8,128)} %enc_ref.3), custom_call_target="tpu_custom_call" | custom-call | flops 268435456 | bytes 4194304 | tf_op jit(solution)/shard_map/pallas_call | solution.py:340
  3.0 2.1 %collective-permute-start.3 = (bf16[272,512]{1,0:T(8,128)(2,1)}, bf16[272,512]{1,0:T(8,128)(2,1)S(1)}, u32[]{:S(2)}, u32[]{:S(2)}) collective-permute-start(bf16[272,512]{1,0:T(8,128)(2,1)} %get-tuple-element.34), channel_id=1, source_target_pairs={{0,1},{1,0},{2,3},{3,2},{4,5},{5,4},{6,7},{7,6},{8,9},{9,8},{10,11... | collective-permute-start | bytes 835592 | tf_op jit(solution)/shard_map/ppermute | solution.py:319
  5.0 2.5 %collective-permute-start.4 = (bf16[272,512]{1,0:T(8,128)(2,1)}, bf16[272,512]{1,0:T(8,128)(2,1)S(1)}, u32[]{:S(2)}, u32[]{:S(2)}) collective-permute-start(bf16[272,512]{1,0:T(8,128)(2,1)} %get-tuple-element.35), channel_id=1, source_target_pairs={{0,3},{1,2},{2,1},{3,0},{4,7},{5,6},{6,5},{7,4},{8,11},{9,10},{10,... | collective-permute-start | bytes 835592 | tf_op jit(solution)/shard_map/ppermute | solution.py:319
  7.6 0.0 copy-done.4
  7.6 1.0 %collective-permute-start.1 = (s32[4]{0:T(128)S(1)}, s32[4]{0:T(128)S(1)}, u32[]{:S(2)}, u32[]{:S(2)}) collective-permute-start(s32[4]{0:T(128)S(1)} %copy-done.4), channel_id=1, source_target_pairs={{0,1},{1,0},{2,3},{3,2},{4,7},{5,6},{6,5},{7,4},{8,9},{9,8},{10,11... | collective-permute-start | bytes 56 | tf_op jit(solution)/shard_map/ppermute | solution.py:313
  8.6 0.0 copy-done.3
  8.6 1.0 %collective-permute-start = (s32[4,16]{1,0:T(4,128)S(1)}, s32[4,16]{1,0:T(4,128)S(1)}, u32[]{:S(2)}, u32[]{:S(2)}) collective-permute-start(s32[4,16]{1,0:T(4,128)S(1)} %copy-done.3), channel_id=1, source_target_pairs={{0,1},{1,0},{2,3},{3,2},{4,7},{5,6},{6,5},{7,4},{8,9},{9,8},{10,11... | collective-permute-start | bytes 776 | tf_op jit(solution)/shard_map/ppermute | solution.py:313
  9.6 0.0 copy-done
  9.6 0.0 copy-start.1
  9.6 1.0 %copy-done.1 = bf16[512,512]{1,0:T(8,128)(2,1)S(1)} copy-done((bf16[512,512]{1,0:T(8,128)(2,1)S(1)}, bf16[512,512]{1,0:T(8,128)(2,1)}, u32[]{:S(2)}) %copy-start.1) | copy-done | bytes 524312
  10.6 0.0 copy-start.2
  10.6 1.0 %shard_map.56.mine_ref = bf16[512,512]{1,0:T(8,128)(2,1)S(1)} custom-call(f32[512,1024]{1,0:T(8,128)S(1)} %copy-done, bf16[512,512]{1,0:T(8,128)(2,1)S(1)} %copy-done.1), custom_call_target="tpu_custom_call" | custom-call | flops 268435456 | bytes 4194304 | tf_op jit(solution)/shard_map/pallas_call | solution.py:351
  11.7 0.3 collective-permute-done.1.count_ref
  12.0 0.2 collective-permute-done.list_ref
  12.2 1.5 %collective-permute-start.2 = (bf16[4,16,128,128]{3,2,1,0:T(8,128)(2,1)}, bf16[4,16,128,128]{3,2,1,0:T(8,128)(2,1)}, u32[]{:S(2)}, u32[]{:S(2)}) collective-permute-start(bf16[4,16,128,128]{3,2,1,0:T(8,128)(2,1)} %weight_ref.1), channel_id=1, source_target_pairs={{0,1},{1,0},{2,3},{3,2},{4,7},{5,6},{6,5},{7,4},{8,9},{9,8},{10,11... | collective-permute-start | bytes 6291464 | tf_op jit(solution)/shard_map/ppermute | solution.py:313
  13.7 0.0 collective-permute-done.3.row_0
  13.7 0.9 %collective-permute-done.4.row_1 = bf16[272,512]{1,0:T(8,128)(2,1)S(1)} collective-permute-done((bf16[272,512]{1,0:T(8,128)(2,1)}, bf16[272,512]{1,0:T(8,128)(2,1)S(1)}, u32[]{:S(2)}, u32[]{:S(2)}) %collective-permute-start.4) | collective-permute-done | bytes 278560 | tf_op jit(solution)/shard_map/ppermute | solution.py:319
  14.6 0.0 copy-done.2
  14.6 1.2 %shard_map.59 = bf16[512,1152]{1,0:T(8,128)(2,1)} custom-call(bf16[16,512]{1,0:T(8,128)(2,1)S(1)} %copy-done.2, bf16[272,512]{1,0:T(8,128)(2,1)S(1)} %collective-permute-done.3.row_0, bf16[272,512]{1,0:T(8,128)(2,1)S(1)} %collective-permute-done.4.row_1, bf16[512,512]{1,0:T(8,128)(2,1)S(1)} %shard_map.56.mine_ref), custom_call_target="tpu_custom_call" | custom-call | flops 1048576 | bytes 2097152 | tf_op jit(solution)/shard_map/pallas_call | solution.py:364
  15.8 7.9 %all-to-all-start = ((bf16[32,16,1152]{2,1,0:T(8,128)(2,1)}), bf16[32,16,1152]{2,1,0:T(8,128)(2,1)S(1)}, u32[]{:S(2)}, u32[]{:S(2)}) async-start(bf16[32,16,1152]{2,1,0:T(8,128)(2,1)} %bitcast.1), calls=%async_computation | async-start | bytes 2359296 | tf_op jit(solution)/shard_map/all_to_all | solution.py:374
  23.6 0.0 copy-start.5
  23.7 0.6 copy-done.5
  24.3 2.9 %shard_map.58 = (bf16[512,2048]{1,0:T(8,128)(2,1)S(1)}, f32[512,128]{1,0:T(8,128)S(1)}, f32[8,128]{1,0:T(8,128)S(1)}) custom-call(s32[4,16]{1,0:T(4,128)S(1)} %copy-done.3, s32[4]{0:T(128)S(1)} %copy-done.5, bf16[4,16,128,128]{3,2,1,0:T(8,128)(2,1)} %weight_ref.1), custom_call_target="tpu_custom_call" | custom-call | flops 40000000000 | bytes 8388608 | tf_op jit(solution)/shard_map/pallas_call | solution.py:324
  27.2 15.4 %all-to-all-done = bf16[32,16,1152]{2,1,0:T(8,128)(2,1)S(1)} async-done(((bf16[32,16,1152]{2,1,0:T(8,128)(2,1)}), bf16[32,16,1152]{2,1,0:T(8,128)(2,1)S(1)}, u32[]{:S(2)}, u32[]{:S(2)}) %all-to-all-start) | async-done | bytes 1179680 | tf_op jit(solution)/shard_map/all_to_all | solution.py:374
  42.7 0.2 shard_map.60
  42.8 2.0 %collective-permute-start.5 = (bf16[528,512]{1,0:T(8,128)(2,1)S(1)}, bf16[528,512]{1,0:T(8,128)(2,1)S(1)}, u32[]{:S(2)}, u32[]{:S(2)}) collective-permute-start(bf16[528,512]{1,0:T(8,128)(2,1)S(1)} %get-tuple-element.38.rows_ref.near_ref), channel_id=1, source_target_pairs={{0,3},{1,2},{2,1},{3,0},{4,5},{5,4},{6,7},{7,6},{8,11},{9,10},{10,... | collective-permute-start | bytes 1622024 | tf_op jit(solution)/shard_map/ppermute | solution.py:316
  44.8 1.2 %collective-permute-start.7 = (bf16[512,512]{1,0:T(8,128)(2,1)S(1)}, bf16[512,512]{1,0:T(8,128)(2,1)S(1)}, u32[]{:S(2)}, u32[]{:S(2)}) collective-permute-start(bf16[512,512]{1,0:T(8,128)(2,1)S(1)} %get-tuple-element.40.near_ref), channel_id=1, source_target_pairs={{0,3},{1,2},{2,1},{3,0},{4,5},{5,4},{6,7},{7,6},{8,11},{9,10},{10,... | collective-permute-start | bytes 1572872 | tf_op jit(solution)/shard_map/ppermute | solution.py:316
  46.1 0.8 shard_map.61.pick_ref
  46.9 1.3 %shard_map.62.refs_1_.part_ref = bf16[2048,256]{1,0:T(8,128)(2,1)S(1)} custom-call(bf16[2,2048,512]{2,1,0:T(8,128)(2,1)S(1)} %shard_map.61.pick_ref, bf16[528,512]{1,0:T(8,128)(2,1)S(1)} %get-tuple-element.38.rows_ref.near_ref), custom_call_target="tpu_custom_call" | custom-call | flops 1073741824 | bytes 4194304 | tf_op jit(solution)/shard_map/pallas_call | solution.py:398
  48.1 1.3 %shard_map.63.refs_2_.part_ref = bf16[2048,256]{1,0:T(8,128)(2,1)S(1)} custom-call(bf16[2,2048,512]{2,1,0:T(8,128)(2,1)S(1)} %shard_map.61.pick_ref, bf16[512,512]{1,0:T(8,128)(2,1)S(1)} %get-tuple-element.40.near_ref), custom_call_target="tpu_custom_call" | custom-call | flops 1073741824 | bytes 4194304 | tf_op jit(solution)/shard_map/pallas_call | solution.py:398
  49.4 0.0 collective-permute-done.2.weight_ref
  49.4 2.6 %shard_map.57 = (bf16[512,2048]{1,0:T(8,128)(2,1)S(1)}, f32[512,128]{1,0:T(8,128)S(1)}, f32[8,128]{1,0:T(8,128)S(1)}) custom-call(s32[4,16]{1,0:T(4,128)S(1)} %collective-permute-done.list_ref, s32[4]{0:T(128)S(1)} %collective-permute-done.1.count_ref, bf16[4,16,128,128]{3,2,1,0:T(8,128)(2,1)} %collective-permute-done.2.weight_ref), custom_call_target="tpu_custom_call" | custom-call | bytes 8388608 | tf_op jit(solution)/shard_map/pallas_call | solution.py:324
  52.0 1.3 %collective-permute-done.5.rows_ref.far_ref = bf16[528,512]{1,0:T(8,128)(2,1)S(1)} collective-permute-done((bf16[528,512]{1,0:T(8,128)(2,1)S(1)}, bf16[528,512]{1,0:T(8,128)(2,1)S(1)}, u32[]{:S(2)}, u32[]{:S(2)}) %collective-permute-start.5) | collective-permute-done | bytes 540704 | tf_op jit(solution)/shard_map/ppermute | solution.py:316
  53.4 0.8 shard_map.64.pick_ref
  54.2 2.4 %shard_map.65 = (bf16[1024,256]{1,0:T(8,128)(2,1)S(1)}, bf16[1024,256]{1,0:T(8,128)(2,1)S(1)}) custom-call(bf16[512,2048]{1,0:T(8,128)(2,1)S(1)} %get-tuple-element.31.dense_a.dense, bf16[512,2048]{1,0:T(8,128)(2,1)S(1)} %get-tuple-element.29.dense_b.dense, f32[512,128]{1,0:T(8,128)S(1)} %get-tuple-element.32.scale_a.scale, ...), custom_call_target="tpu_custom_call" | custom-call | flops 2147483648 | bytes 4194304 | tf_op jit(solution)/shard_map/pallas_call | solution.py:412
  56.6 2.1 %collective-permute-start.6 = (bf16[1024,256]{1,0:T(8,128)(2,1)S(1)}, bf16[1024,256]{1,0:T(8,128)(2,1)S(1)}, u32[]{:S(2)}, u32[]{:S(2)}) collective-permute-start(bf16[1024,256]{1,0:T(8,128)(2,1)S(1)} %get-tuple-element.41.hidden_ref), channel_id=1, source_target_pairs={{0,3},{1,2},{2,1},{3,0},{4,5},{5,4},{6,7},{7,6},{8,11},{9,10},{10,... | collective-permute-start | bytes 1572872 | tf_op jit(solution)/shard_map/ppermute | solution.py:316
  58.6 0.4 collective-permute-done.7.far_ref
  59.0 2.4 %shard_map.67 = (bf16[1024,256]{1,0:T(8,128)(2,1)S(1)}, bf16[1024,256]{1,0:T(8,128)(2,1)S(1)}) custom-call(bf16[512,2048]{1,0:T(8,128)(2,1)S(1)} %get-tuple-element.31.dense_a.dense, bf16[512,2048]{1,0:T(8,128)(2,1)S(1)} %get-tuple-element.29.dense_b.dense, f32[512,128]{1,0:T(8,128)S(1)} %get-tuple-element.32.scale_a.scale, ...), custom_call_target="tpu_custom_call" | custom-call | flops 2147483648 | bytes 4194304 | tf_op jit(solution)/shard_map/pallas_call | solution.py:412
  61.4 2.3 %collective-permute-start.9 = (bf16[1024,256]{1,0:T(8,128)(2,1)S(1)}, bf16[1024,256]{1,0:T(8,128)(2,1)S(1)}, u32[]{:S(2)}, u32[]{:S(2)}) collective-permute-start(bf16[1024,256]{1,0:T(8,128)(2,1)S(1)} %get-tuple-element.43.hidden_ref), channel_id=1, source_target_pairs={{0,3},{1,2},{2,1},{3,0},{4,5},{5,4},{6,7},{7,6},{8,11},{9,10},{10,... | collective-permute-start | bytes 1572872 | tf_op jit(solution)/shard_map/ppermute | solution.py:316
  63.6 0.7 shard_map.68.after.total_ref
  64.3 0.7 shard_map.66.total_ref
  65.0 2.0 %collective-permute-done.6.hidden_ref = bf16[1024,256]{1,0:T(8,128)(2,1)S(1)} collective-permute-done((bf16[1024,256]{1,0:T(8,128)(2,1)S(1)}, bf16[1024,256]{1,0:T(8,128)(2,1)S(1)}, u32[]{:S(2)}, u32[]{:S(2)}) %collective-permute-start.6) | collective-permute-done | bytes 524320 | tf_op jit(solution)/shard_map/ppermute | solution.py:316
  67.0 0.4 shard_map.69.after.sent_ref
  67.5 1.9 %collective-permute-start.8 = (bf16[512,256]{1,0:T(8,128)(2,1)S(1)}, bf16[512,256]{1,0:T(8,128)(2,1)S(1)}, u32[]{:S(2)}, u32[]{:S(2)}) collective-permute-start(bf16[512,256]{1,0:T(8,128)(2,1)S(1)} %shard_map.69.after.sent_ref), channel_id=1, source_target_pairs={{0,1},{1,0},{2,3},{3,2},{8,9},{9,8},{10,11},{11,10},{16,17},{17,16... | collective-permute-start | bytes 786440 | tf_op jit(solution)/shard_map/ppermute | solution.py:446
  69.4 4.0 %collective-permute-done.9.hidden_ref = bf16[1024,256]{1,0:T(8,128)(2,1)S(1)} collective-permute-done((bf16[1024,256]{1,0:T(8,128)(2,1)S(1)}, bf16[1024,256]{1,0:T(8,128)(2,1)S(1)}, u32[]{:S(2)}, u32[]{:S(2)}) %collective-permute-start.9) | collective-permute-done | bytes 524320 | tf_op jit(solution)/shard_map/ppermute | solution.py:316
  73.4 0.4 shard_map.70.after_1.after
  73.9 0.1 collective-permute-start.11
  74.0 1.8 %collective-permute-done.8.after_0.early_0 = bf16[512,256]{1,0:T(8,128)(2,1)S(1)} collective-permute-done((bf16[512,256]{1,0:T(8,128)(2,1)S(1)}, bf16[512,256]{1,0:T(8,128)(2,1)S(1)}, u32[]{:S(2)}, u32[]{:S(2)}) %collective-permute-start.8) | collective-permute-done | bytes 262176 | tf_op jit(solution)/shard_map/ppermute | solution.py:446
  75.8 0.7 collective-permute-start.10
  76.5 0.4 shard_map.73.keep_1
  76.9 0.4 shard_map.72.keep_0
  77.3 0.8 %shard_map.74._ = bf16[512,1024]{1,0:T(8,128)(2,1)} custom-call(bf16[512,256]{1,0:T(8,128)(2,1)S(1)} %shard_map.72.keep_0, bf16[512,256]{1,0:T(8,128)(2,1)S(1)} %shard_map.73.keep_1), custom_call_target="tpu_custom_call" | custom-call | tf_op jit(solution)/shard_map/pallas_call | solution.py:453
  78.2 2.2 %collective-permute-done.11.got_1 = bf16[512,256]{1,0:T(8,128)(2,1)S(1)} collective-permute-done((bf16[512,256]{1,0:T(8,128)(2,1)S(1)}, bf16[512,256]{1,0:T(8,128)(2,1)S(1)}, u32[]{:S(2)}, u32[]{:S(2)}) %collective-permute-start.11) | collective-permute-done | bytes 262176 | tf_op jit(solution)/shard_map/ppermute | solution.py:313
  80.3 0.0 collective-permute-done.10.late_0
  80.3 0.8 shard_map.75
  (1 shorter events, 0.0 us)
Async XLA Ops:
  0.0 9.6 %copy-start = (f32[512,1024]{1,0:T(8,128)S(1)}, f32[512,1024]{1,0:T(8,128)}, u32[]{:S(2)}) copy-start(f32[512,1024]{1,0:T(8,128)} %enc_ref.3) | copy-start | bytes 6291460
  0.0 7.6 %copy-start.4 = (s32[4]{0:T(128)S(1)}, s32[4]{0:T(128)}, u32[]{:S(2)}) copy-start(s32[4]{0:T(128)} %count_ref.1) | copy-start | bytes 52
  0.0 8.6 %copy-start.3 = (s32[4,16]{1,0:T(4,128)S(1)}, s32[4,16]{1,0:T(4,128)}, u32[]{:S(2)}) copy-start(s32[4,16]{1,0:T(4,128)} %list_ref.1) | copy-start | bytes 772
  3.0 10.8 %collective-permute-start.3 = (bf16[272,512]{1,0:T(8,128)(2,1)}, bf16[272,512]{1,0:T(8,128)(2,1)S(1)}, u32[]{:S(2)}, u32[]{:S(2)}) collective-permute-start(bf16[272,512]{1,0:T(8,128)(2,1)} %get-tuple-element.34), channel_id=1, source_target_pairs={{0,1},{1,0},{2,3},{3,2},{4,5},{5,4},{6,7},{7,6},{8,9},{9,8},{10,11... | collective-permute-start | bytes 835592 | tf_op jit(solution)/shard_map/ppermute | solution.py:319
  5.0 9.6 %collective-permute-start.4 = (bf16[272,512]{1,0:T(8,128)(2,1)}, bf16[272,512]{1,0:T(8,128)(2,1)S(1)}, u32[]{:S(2)}, u32[]{:S(2)}) collective-permute-start(bf16[272,512]{1,0:T(8,128)(2,1)} %get-tuple-element.35), channel_id=1, source_target_pairs={{0,3},{1,2},{2,1},{3,0},{4,7},{5,6},{6,5},{7,4},{8,11},{9,10},{10,... | collective-permute-start | bytes 835592 | tf_op jit(solution)/shard_map/ppermute | solution.py:319
  7.6 4.4 %collective-permute-start.1 = (s32[4]{0:T(128)S(1)}, s32[4]{0:T(128)S(1)}, u32[]{:S(2)}, u32[]{:S(2)}) collective-permute-start(s32[4]{0:T(128)S(1)} %copy-done.4), channel_id=1, source_target_pairs={{0,1},{1,0},{2,3},{3,2},{4,7},{5,6},{6,5},{7,4},{8,9},{9,8},{10,11... | collective-permute-start | bytes 56 | tf_op jit(solution)/shard_map/ppermute | solution.py:313
  8.6 3.6 %collective-permute-start = (s32[4,16]{1,0:T(4,128)S(1)}, s32[4,16]{1,0:T(4,128)S(1)}, u32[]{:S(2)}, u32[]{:S(2)}) collective-permute-start(s32[4,16]{1,0:T(4,128)S(1)} %copy-done.3), channel_id=1, source_target_pairs={{0,1},{1,0},{2,3},{3,2},{4,7},{5,6},{6,5},{7,4},{8,9},{9,8},{10,11... | collective-permute-start | bytes 776 | tf_op jit(solution)/shard_map/ppermute | solution.py:313
  9.6 1.0 %copy-start.1 = (bf16[512,512]{1,0:T(8,128)(2,1)S(1)}, bf16[512,512]{1,0:T(8,128)(2,1)}, u32[]{:S(2)}) copy-start(bf16[512,512]{1,0:T(8,128)(2,1)} %get-tuple-element.25.pick_ref) | copy-start | bytes 1572868
  10.6 4.0 %copy-start.2 = (bf16[16,512]{1,0:T(8,128)(2,1)S(1)}, bf16[16,512]{1,0:T(8,128)(2,1)}, u32[]{:S(2)}) copy-start(bf16[16,512]{1,0:T(8,128)(2,1)} %get-tuple-element.33.place_ref) | copy-start | bytes 49156
  12.2 37.2 %collective-permute-start.2 = (bf16[4,16,128,128]{3,2,1,0:T(8,128)(2,1)}, bf16[4,16,128,128]{3,2,1,0:T(8,128)(2,1)}, u32[]{:S(2)}, u32[]{:S(2)}) collective-permute-start(bf16[4,16,128,128]{3,2,1,0:T(8,128)(2,1)} %weight_ref.1), channel_id=1, source_target_pairs={{0,1},{1,0},{2,3},{3,2},{4,7},{5,6},{6,5},{7,4},{8,9},{9,8},{10,11... | collective-permute-start | bytes 6291464 | tf_op jit(solution)/shard_map/ppermute | solution.py:313
  15.8 26.9 %all-to-all-start = ((bf16[32,16,1152]{2,1,0:T(8,128)(2,1)}), bf16[32,16,1152]{2,1,0:T(8,128)(2,1)S(1)}, u32[]{:S(2)}, u32[]{:S(2)}) async-start(bf16[32,16,1152]{2,1,0:T(8,128)(2,1)} %bitcast.1), calls=%async_computation | async-start | bytes 2359296 | tf_op jit(solution)/shard_map/all_to_all | solution.py:374
  23.6 0.7 copy-start.5
  42.8 10.6 %collective-permute-start.5 = (bf16[528,512]{1,0:T(8,128)(2,1)S(1)}, bf16[528,512]{1,0:T(8,128)(2,1)S(1)}, u32[]{:S(2)}, u32[]{:S(2)}) collective-permute-start(bf16[528,512]{1,0:T(8,128)(2,1)S(1)} %get-tuple-element.38.rows_ref.near_ref), channel_id=1, source_target_pairs={{0,3},{1,2},{2,1},{3,0},{4,5},{5,4},{6,7},{7,6},{8,11},{9,10},{10,... | collective-permute-start | bytes 1622024 | tf_op jit(solution)/shard_map/ppermute | solution.py:316
  44.8 14.2 %collective-permute-start.7 = (bf16[512,512]{1,0:T(8,128)(2,1)S(1)}, bf16[512,512]{1,0:T(8,128)(2,1)S(1)}, u32[]{:S(2)}, u32[]{:S(2)}) collective-permute-start(bf16[512,512]{1,0:T(8,128)(2,1)S(1)} %get-tuple-element.40.near_ref), channel_id=1, source_target_pairs={{0,3},{1,2},{2,1},{3,0},{4,5},{5,4},{6,7},{7,6},{8,11},{9,10},{10,... | collective-permute-start | bytes 1572872 | tf_op jit(solution)/shard_map/ppermute | solution.py:316
  56.6 10.5 %collective-permute-start.6 = (bf16[1024,256]{1,0:T(8,128)(2,1)S(1)}, bf16[1024,256]{1,0:T(8,128)(2,1)S(1)}, u32[]{:S(2)}, u32[]{:S(2)}) collective-permute-start(bf16[1024,256]{1,0:T(8,128)(2,1)S(1)} %get-tuple-element.41.hidden_ref), channel_id=1, source_target_pairs={{0,3},{1,2},{2,1},{3,0},{4,5},{5,4},{6,7},{7,6},{8,11},{9,10},{10,... | collective-permute-start | bytes 1572872 | tf_op jit(solution)/shard_map/ppermute | solution.py:316
  61.4 12.1 %collective-permute-start.9 = (bf16[1024,256]{1,0:T(8,128)(2,1)S(1)}, bf16[1024,256]{1,0:T(8,128)(2,1)S(1)}, u32[]{:S(2)}, u32[]{:S(2)}) collective-permute-start(bf16[1024,256]{1,0:T(8,128)(2,1)S(1)} %get-tuple-element.43.hidden_ref), channel_id=1, source_target_pairs={{0,3},{1,2},{2,1},{3,0},{4,5},{5,4},{6,7},{7,6},{8,11},{9,10},{10,... | collective-permute-start | bytes 1572872 | tf_op jit(solution)/shard_map/ppermute | solution.py:316
  67.5 8.3 %collective-permute-start.8 = (bf16[512,256]{1,0:T(8,128)(2,1)S(1)}, bf16[512,256]{1,0:T(8,128)(2,1)S(1)}, u32[]{:S(2)}, u32[]{:S(2)}) collective-permute-start(bf16[512,256]{1,0:T(8,128)(2,1)S(1)} %shard_map.69.after.sent_ref), channel_id=1, source_target_pairs={{0,1},{1,0},{2,3},{3,2},{8,9},{9,8},{10,11},{11,10},{16,17},{17,16... | collective-permute-start | bytes 786440 | tf_op jit(solution)/shard_map/ppermute | solution.py:446
  73.9 6.5 %collective-permute-start.11 = (bf16[512,256]{1,0:T(8,128)(2,1)S(1)}, bf16[512,256]{1,0:T(8,128)(2,1)S(1)}, u32[]{:S(2)}, u32[]{:S(2)}) collective-permute-start(bf16[512,256]{1,0:T(8,128)(2,1)S(1)} %shard_map.70.after_1.after), channel_id=1, source_target_pairs={{0,1},{1,0},{2,3},{3,2},{4,7},{5,6},{6,5},{7,4},{8,9},{9,8},{10,11... | collective-permute-start | bytes 786440 | tf_op jit(solution)/shard_map/ppermute | solution.py:313
  75.8 4.6 %collective-permute-start.10 = (bf16[512,256]{1,0:T(8,128)(2,1)S(1)}, bf16[512,256]{1,0:T(8,128)(2,1)S(1)}, u32[]{:S(2)}, u32[]{:S(2)}) collective-permute-start(bf16[512,256]{1,0:T(8,128)(2,1)S(1)} %shard_map.71), channel_id=1, source_target_pairs={{4,7},{5,6},{6,5},{7,4},{12,15},{13,14},{14,13},{15,12},{20,23},{2... | collective-permute-start | bytes 786440 | tf_op jit(solution)/shard_map/ppermute | solution.py:446
